TPU v7x, 32 devices: a whole 2x2x4 slice. The times are simulated.
32 devices in a mesh: grp: 4 (over x, core), mz: 8 (over z, y).
Axes of the slice: x: 2, y: 2, z: 4, core: 2. Of those that a mesh axis runs over, the one named last changes fastest.
Arguments:
- intensities: float32 [512, 8, 32768], P('grp', None, 'mz'), as said below
- sample_start: float32 [512, 256], P('grp'), as said below
- scan_start: float32 [8, 256], replicated, as said below
- mass_start: float32 [32768, 256], P('mz'), as said below
Outputs:
- sample_factor: float32 [512, 256], P('grp')
- scan_factor: float32 [8, 256], replicated
- mass_factor: float32 [32768, 256], P('mz')
Inputs may be any that keep to these rules, and one draw needn't show every extreme that they name: Measured intensities of the cohort. `sample_start`: a starting estimate of the sample factor. `scan_start`: a starting estimate of the scan factor. `mass_start`: a starting estimate of the m/z factor.
All inputs are finite; a program needn't handle non-finite values.
Results may differ from a plain program's by a relative error of at most 0.0001.
Values sent between devices are 32-bit elements; how exact they have to be, the bound alone decides.
No kernel may reach another device: no remote copies, remote signals or barrier semaphores. Data moves between devices by JAX's collectives and lax.ppermute only.
A program may use at most 128 MiB of HBM per device.

v0:
```python
import jax
import jax.numpy as jnp
from jax import lax
from jax.sharding import PartitionSpec as P

STEPS = 2


precise = lax.Precision.HIGHEST


def frobenius(gram):
    return jnp.sqrt(jnp.sum(gram * gram) + 1e-12)


def gram_of(factor):
    return jnp.dot(factor.T, factor, precision=precise, preferred_element_type=jnp.float32)


def descend(factor, hessian, drive):
    product = jnp.dot(factor, hessian, precision=precise, preferred_element_type=jnp.float32)
    return factor - (product - drive) / frobenius(hessian)


def local(intensities, sample_start, scan_start, mass_start):
    factor_a = sample_start
    factor_b = scan_start
    factor_c = mass_start
    samples_here = intensities.shape[0]
    scans_here = intensities.shape[1]
    bins_here = intensities.shape[2]
    rank_width = factor_a.shape[1]
    unfolded = intensities.reshape(samples_here * scans_here, bins_here)
    for iteration in range(STEPS):
        gram_a = lax.psum(gram_of(factor_a), "grp")
        gram_b = gram_of(factor_b)
        gram_c = lax.psum(gram_of(factor_c), "mz")
        contracted = jnp.einsum("ijk,kr->ijr", intensities, factor_c, precision=precise)
        drive_a = lax.psum(jnp.einsum("ijr,jr->ir", contracted, factor_b, precision=precise), "mz")
        drive_b = lax.psum(
            jnp.einsum("ijr,ir->jr", contracted, factor_a, precision=precise), ("grp", "mz")
        )
        khatri_rao = (factor_a[:, None, :] * factor_b[None, :, :]).reshape(
            samples_here * scans_here, rank_width
        )
        hessian_a = gram_b * gram_c
        hessian_b = gram_a * gram_c
        hessian_c = gram_a * gram_b
        partial_c = lax.dot_general(
            unfolded,
            khatri_rao,
            (((0,), (0,)), ((), ())),
            precision=precise,
            preferred_element_type=jnp.float32,
        )
        drive_c = lax.psum(partial_c, "grp")
        new_c = descend(factor_c, hessian_c, drive_c)
        new_a = descend(factor_a, hessian_a, drive_a)
        new_b = descend(factor_b, hessian_b, drive_b)
        factor_a, factor_b, factor_c = (new_a, new_b, new_c)
    return (factor_a, factor_b, factor_c)


def solution(mesh):
    placed = (P("grp", None, "mz"), P("grp", None), P(), P("mz", None))
    return jax.shard_map(
        local,
        mesh=mesh,
        in_specs=placed,
        out_specs=(P("grp", None), P(), P("mz", None)),
        check_vma=False,
    )
```

profile of v0, /device:TPU:1, one launch (start us, length us, event | category | flops | bytes accessed | tf_op | source)
XLA Modules:
  0.0 491.7 jit_solution(3441949510386141994)
XLA Ops:
  7.2 0.0 all-reduce.12.cloned.1.call-start
  7.2 0.0 copy-start
  7.2 11.1 %fusion.53 = f32[256,256]{1,0:T(8,128)} fusion(f32[4096,256]{1,0:T(8,128)} %param.7), kind=kOutput, calls=%fused_computation.59 | convolution fusion | flops 3221225472 | bytes 4456448 | tf_op jit(solution)/shard_map/dot_general | solution.py:17
  18.3 0.0 copy-done
  18.3 0.0 copy-start.6
  18.3 0.0 copy-start.2
  18.3 16.7 %fusion.18 = f32[128,8,256]{2,1,0:T(8,128)S(1)} fusion(f32[128,8,4096]{2,1,0:T(8,128)} %param.4, f32[4096,256]{1,0:T(8,128)S(1)} %copy-done), kind=kOutput, calls=%fused_computation.16 | convolution fusion | flops 12884901888 | bytes 22020096 | tf_op jit(solution)/shard_map/ijk,kr->ijr/dot_general | solution.py:38
  35.0 0.0 copy-done.6
  35.0 0.3 fusion.36
  35.3 0.8 copy.26
  36.1 0.0 all-reduce.12.cloned.1.call-update
  36.1 0.3 all-reduce.16.cloned.1.call-start
  36.4 0.0 copy-done.2
  36.4 0.1 copy.8
  36.5 28.8 %fusion.7 = f32[4096,256]{0,1:T(8,128)} fusion(f32[128,8,4096]{2,1,0:T(8,128)} %param.4, f32[8,256]{1,0:T(8,128)S(1)} %copy-done.6, f32[128,256]{0,1:T(8,128)S(1)} %copy.8), kind=kOutput, calls=%fused_computation.9 | convolution fusion | flops 12885164032 | bytes 21110784 | tf_op jit(solution)/shard_map/dot_general | solution.py:49
  65.3 1.1 fusion.54
  66.4 0.0 all-reduce.16.cloned.1.call-update
  66.4 0.4 all-reduce.10.cloned.1.call-start
  66.9 5.7 %copy.11 = f32[4096,256]{0,1:T(8,128)} copy(f32[4096,256]{1,0:T(8,128)} %param.7) | data formatting | bytes 8388608 | tf_op args[3]
  72.6 0.3 fusion.35
  72.9 35.2 %all-reduce.12.cloned.1.call-done = (f32[128,256]{0,1:T(8,128)}, f32[256,256]{1,0:T(8,128)}) async-done(((f32[128,256]{0,1:T(8,128)}, f32[256,256]{1,0:T(8,128)}), (f32[128,256]{0,1:T(8,128)}, f32[256,256]{1,0:T(8,128)})) %all-reduce.12.cloned.1.call-update) | async-done | bytes 393232 | tf_op jit(solution)/shard_map/psum | solution.py:39
  108.1 93.8 %all-reduce.16.cloned.1.call-done = (f32[256,256]{1,0:T(8,128)}, f32[4096,256]{0,1:T(8,128)}) async-done(((f32[256,256]{1,0:T(8,128)}, f32[4096,256]{0,1:T(8,128)}), (f32[256,256]{1,0:T(8,128)}, f32[4096,256]{0,1:T(8,128)})) %all-reduce.16.cloned.1.call-update) | async-done | bytes 4456464 | tf_op jit(solution)/shard_map/psum | solution.py:35
  201.9 2.1 multiply_reduce_fusion.3
  204.7 11.9 %fusion.14 = f32[4096,256]{0,1:T(8,128)S(1)} fusion(f32[4096,256]{0,1:T(8,128)} %copy.11, f32[4096,256]{0,1:T(8,128)} %get-tuple-element.21, f32[4096,256]{1,0:T(8,128)} %param.7, f32[]{:T(128)S(6)} %sqrt.20, f32[256,256]{1,0:T(8,128)} %get-tuple-element.20, f32[256,256]{1,0:T(8,128)S(1)} %get-tuple-element.22), kind=kOutput, calls=%fused_computation.12 | convolution fusion | flops 3224436736 | bytes 17301508 | tf_op jit(solution)/shard_map/dot_general | solution.py:21
  216.6 0.0 copy-start.1
  216.6 4.3 fusion.55
  220.9 0.0 copy-done.1
  220.9 0.0 copy-start.5
  220.9 0.0 copy-start.8
  220.9 0.0 copy-start.3
  220.9 28.1 %fusion.20 = f32[128,8,256]{0,2,1:T(8,128)S(1)} fusion(f32[128,8,4096]{2,1,0:T(8,128)} %param.4, f32[4096,256]{0,1:T(8,128)S(1)} %fusion.14), kind=kOutput, calls=%fused_computation.18 | convolution fusion | flops 12884901888 | bytes 22020096 | tf_op jit(solution)/shard_map/ijk,kr->ijr/dot_general | solution.py:38
  250.4 0.0 copy-done.5
  250.4 0.0 copy-done.8
  250.4 0.6 fusion.29
  251.0 2.3 fusion.39
  253.3 0.1 copy.38
  253.4 39.2 %all-reduce = (f32[8,256]{1,0:T(8,128)S(1)}, f32[8,256]{1,0:T(8,128)S(1)}) all-reduce(f32[8,256]{1,0:T(8,128)S(1)} %bitcast.90, f32[8,256]{1,0:T(8,128)S(1)} %bitcast.91), channel_id=1, replica_groups=mesh['grp'=4,'mz'=8] {'grp','mz'}, use_global_device_ids=true, to_apply=%region_4.0 | all-reduce | flops 4096 | bytes 32768 | tf_op jit(solution)/shard_map/psum | solution.py:40
  292.6 0.0 copy-done.3
  292.6 0.2 fusion.34
  292.8 0.1 copy.34
  293.0 3.0 fusion.41
  296.0 0.0 all-reduce.10.cloned.1.call-update
  296.0 0.0 all-reduce.14.cloned.1.call-start
  296.1 29.0 %fusion.10 = f32[4096,256]{0,1:T(8,128)} fusion(f32[128,8,4096]{2,1,0:T(8,128)} %param.4, f32[8,256]{1,0:T(8,128)S(1)} %fusion.34, f32[128,256]{0,1:T(8,128)S(1)} %fusion.29), kind=kOutput, calls=%fused_computation.10 | convolution fusion | flops 12885164032 | bytes 21110784 | tf_op jit(solution)/shard_map/dot_general | solution.py:49
  325.1 1.1 fusion.56
  326.2 0.0 all-reduce.14.cloned.1.call-update
  326.2 41.0 %all-reduce.10.cloned.1.call-done = (f32[128,256]{0,1:T(8,128)}, f32[256,256]{1,0:T(8,128)}) async-done(((f32[128,256]{0,1:T(8,128)}, f32[256,256]{1,0:T(8,128)}), (f32[128,256]{0,1:T(8,128)}, f32[256,256]{1,0:T(8,128)})) %all-reduce.10.cloned.1.call-update) | async-done | bytes 393232 | tf_op jit(solution)/shard_map/psum | solution.py:39
  367.2 93.5 %all-reduce.14.cloned.1.call-done = (f32[256,256]{1,0:T(8,128)}, f32[4096,256]{0,1:T(8,128)}) async-done(((f32[256,256]{1,0:T(8,128)}, f32[4096,256]{0,1:T(8,128)}), (f32[256,256]{1,0:T(8,128)}, f32[4096,256]{0,1:T(8,128)})) %all-reduce.14.cloned.1.call-update) | async-done | bytes 4456464 | tf_op jit(solution)/shard_map/psum | solution.py:35
  460.7 2.1 multiply_reduce_fusion
  464.8 1.6 fusion.26
  466.4 0.8 copy.16
  467.2 11.0 %fusion.16 = f32[4096,256]{0,1:T(8,128)} fusion(f32[4096,256]{0,1:T(8,128)} %copy-done.1, f32[4096,256]{0,1:T(8,128)} %get-tuple-element.19, f32[]{:T(128)S(6)} %sqrt.23, f32[256,256]{1,0:T(8,128)} %get-tuple-element.18, f32[256,256]{1,0:T(8,128)S(1)} %get-tuple-element.23), kind=kOutput, calls=%fused_computation.14 | convolution fusion | flops 3224436736 | bytes 13107204 | tf_op jit(solution)/shard_map/dot_general | solution.py:21
  478.2 0.0 copy-start.4
  478.2 0.0 copy-start.7
  478.2 5.7 %copy.17 = f32[4096,256]{1,0:T(8,128)} copy(f32[4096,256]{0,1:T(8,128)} %fusion.16) | data formatting | bytes 8388608
  483.8 0.0 copy-done.4
  483.8 0.0 copy-done.7
  483.8 0.8 fusion.31
Async XLA Ops:
  7.2 101.0 %all-reduce.12.cloned.1.call-start = ((), (), s32[]{:S(2)}) async-start(), calls=%async_computation.1 | async-start | bytes 786432 | tf_op jit(solution)/shard_map/psum | solution.py:39
  7.2 11.1 %copy-start = (f32[4096,256]{1,0:T(8,128)S(1)}, f32[4096,256]{1,0:T(8,128)}, u32[]{:S(2)}) copy-start(f32[4096,256]{1,0:T(8,128)} %param.7) | copy-start | bytes 12582916
  18.3 16.7 %copy-start.6 = (f32[8,256]{1,0:T(8,128)S(1)}, f32[8,256]{1,0:T(8,128)}, u32[]{:S(2)}) copy-start(f32[8,256]{1,0:T(8,128)} %param.6) | copy-start | bytes 24580
  18.3 18.1 %copy-start.2 = (f32[128,256]{1,0:T(8,128)S(1)}, f32[128,256]{1,0:T(8,128)}, u32[]{:S(2)}) copy-start(f32[128,256]{1,0:T(8,128)} %param.5) | copy-start | bytes 393220
  36.1 165.8 %all-reduce.16.cloned.1.call-start = ((), (), s32[]{:S(2)}) async-start(), calls=%async_computation.3 | async-start | bytes 8912896 | tf_op jit(solution)/shard_map/psum | solution.py:35
  66.4 300.7 %all-reduce.10.cloned.1.call-start = ((), (), s32[]{:S(2)}) async-start(), calls=%async_computation | async-start | bytes 786432 | tf_op jit(solution)/shard_map/psum | solution.py:39
  216.6 4.3 copy-start.1
  220.9 29.5 %copy-start.5 = (f32[256,256]{1,0:T(8,128)S(1)}, f32[256,256]{1,0:T(8,128)}, u32[]{:S(2)}) copy-start(f32[256,256]{1,0:T(8,128)} %get-tuple-element.17) | copy-start | bytes 786436
  220.9 29.5 %copy-start.8 = (f32[128,256]{0,1:T(8,128)S(1)}, f32[128,256]{0,1:T(8,128)}, u32[]{:S(2)}) copy-start(f32[128,256]{0,1:T(8,128)} %get-tuple-element.16) | copy-start | bytes 393220
  220.9 71.7 %copy-start.3 = (f32[256,256]{1,0:T(8,128)S(1)}, f32[256,256]{1,0:T(8,128)}, u32[]{:S(2)}) copy-start(f32[256,256]{1,0:T(8,128)} %get-tuple-element.20) | copy-start | bytes 786436
  296.0 164.7 %all-reduce.14.cloned.1.call-start = ((), (), s32[]{:S(2)}) async-start(), calls=%async_computation.2 | async-start | bytes 8912896 | tf_op jit(solution)/shard_map/psum | solution.py:35
  478.2 5.7 %copy-start.4 = (f32[256,256]{1,0:T(8,128)S(1)}, f32[256,256]{1,0:T(8,128)}, u32[]{:S(2)}) copy-start(f32[256,256]{1,0:T(8,128)} %get-tuple-element.15) | copy-start | bytes 786436
  478.2 5.7 %copy-start.7 = (f32[256,256]{1,0:T(8,128)S(1)}, f32[256,256]{1,0:T(8,128)}, u32[]{:S(2)}) copy-start(f32[256,256]{1,0:T(8,128)} %get-tuple-element.18) | copy-start | bytes 786436
Sparse Core Ops, SparseCore 0:
  36.2 71.8 all-reduce.11
  111.3 90.6 all-reduce.15
  296.1 70.9 all-reduce.9
  370.0 90.6 all-reduce.13
where the time goes:
time: 501 us; the launch traced here: 492 us
  waiting for transfers between devices  264 us (53%)
  matrix products  156 us (31%)
  blocking collectives  39.2 us (8%)
  between operations  18.5 us (4%)
  local copies, waits for them, and re-layouts  13.2 us (3%)
    psum x2, waiting for transfers between devices, local(): gram_a = lax.psum(gram_of(factor_a), 'grp')  187 us
    psum x2, waiting for transfers between devices, local(): lax.psum(jnp.einsum('ijr,jr->ir', contracted, factor_b, precision=precise...  76.2 us
    dot_general x2, matrix products, local(): lax.dot_general(unfolded, khatri_rao, (((0,), (0,)), ((), ())), precision...  57.8 us
    dot_general x2, matrix products, local(): jnp.einsum('ijk,kr->ijr', intensities, factor_c, precision=precise)  44.8 us
    psum x1, blocking collectives, local(): lax.psum(jnp.einsum('ijr,ir->jr', contracted, factor_a, precision=precise...  39.2 us
    dot_general x6, matrix products, descend(): jnp.dot(factor, hessian, precision=precise, preferred_element_type=jnp.fl...  26.2 us
    dot_general x6, matrix products, gram_of(): jnp.dot(factor.T, factor, precision=precise, preferred_element_type=jnp.f...  21.7 us
    unnamed x22, local copies, waits for them, and re-layouts  12.2 us
  transfers between devices with their start and end apart: 4, of which 4 were waited for; matrix products, arithmetic and copies ran while one was open for 13% of the time, Pallas kernels for 0%

commit v1 on v0

v1 whole, which is shorter than its diff:
```python
import functools

import jax
import jax.numpy as jnp
from jax import lax
from jax.experimental import pallas as pl
from jax.experimental.pallas import tpu as pltpu
from jax.sharding import PartitionSpec as P

STEPS = 2
UNIT = 256
PAIR = 2 * UNIT
FIRST = (1, 3, 4)
LAST = (4, 2, 1, 1)
F32 = jnp.float32
BF16 = jnp.bfloat16
VMEM_LIMIT = 36 << 20
NOWHERE = pl.BlockSpec(memory_space=pl.ANY)
HELD = pl.BlockSpec(memory_space=pltpu.VMEM)


def split(value):
    high = value.astype(BF16)
    return high, (value - high.astype(F32)).astype(BF16)


def plain(a, b):
    return jnp.dot(a, b, preferred_element_type=F32)


def dot(a, b):
    a_high, a_low = split(a)
    b_high, b_low = split(b)
    return plain(a_high, b_high) + (plain(a_high, b_low) + plain(a_low, b_high))


def gram(factor):
    return dot(factor.T, factor)


def inverse_norm(matrix):
    return 1.0 / jnp.sqrt(jnp.sum(matrix * matrix, keepdims=True) + 1e-12)


def in_vmem(value):
    return pltpu.with_memory_space_constraint(value, pltpu.VMEM)


def params():
    return pltpu.CompilerParams(vmem_limit_bytes=VMEM_LIMIT)


def shaped(*dims):
    return jax.ShapeDtypeStruct(dims, F32)


def whole(shape):
    return pl.BlockSpec(shape, lambda *_: (0,) * len(shape))


def rows_block(rows, rank, start=0):
    return pl.BlockSpec((rows, rank), lambda j, *_: (start + j, 0))


def call(kernel, name, grid, in_specs, out_specs, out_shape, scratch=(), aliases=None):
    return pl.pallas_call(
        kernel,
        grid_spec=pltpu.PrefetchScalarGridSpec(
            num_scalar_prefetch=1,
            grid=grid,
            in_specs=in_specs,
            out_specs=out_specs,
            scratch_shapes=scratch,
        ),
        out_shape=out_shape,
        input_output_aliases=aliases or {},
        cost_estimate=pl.CostEstimate(flops=0, bytes_accessed=0, transcendentals=0),
        compiler_params=params(),
        name=name,
    )


def fill_khatri_rao(krt_ref, a, b):
    rank = a.shape[1]
    product = (a[:, None, :] * b[None, :, :]).reshape(-1, rank).T
    krt_ref[:rank], krt_ref[rank:] = split(product)


def mass_part(krt_ref, x_high, x_low):
    rank = krt_ref.shape[0] // 2
    both = plain(krt_ref[...], x_high)
    return (both[:rank] + (both[rank:] + plain(krt_ref[:rank], x_low))).T


def store_sides(core, out, theirs_ref, mine_ref):
    at_zero = core == 0
    theirs_ref[...] = jnp.where(at_zero, out[UNIT:], out[:UNIT])
    mine_ref[...] = jnp.where(at_zero, out[:UNIT], out[UNIT:])


def contract(x_high, x_low, c):
    rank = c.shape[1]
    c_high, c_low = split(c)
    both = plain(x_high, jnp.concatenate([c_high, c_low], 1))
    return both[:, :rank] + (both[:, rank:] + plain(x_low, c_high))


def store_drives(out_ref, total, a, b):
    rows = a.shape[0]
    folded = total.reshape(rows, b.shape[0], a.shape[1])
    out_ref[:rows] = jnp.sum(folded * b[None], 1)
    out_ref[rows : rows + b.shape[0]] = jnp.sum(folded * a[:, None, :], 0)


def sides(core, mine, theirs):
    at_zero = core == 0
    return jnp.concatenate([jnp.where(at_zero, mine, theirs), jnp.where(at_zero, theirs, mine)], 0)


def add_half_gram(out_ref, core, factor):
    half = factor.shape[1] // 2
    out_ref[-half:] += dot(jnp.where(core == 0, factor[:, :half], factor[:, half:]).T, factor)


def load_kernel(core_ref, a_ref, b_ref, x_ref, c_ref, high_ref, low_ref, krt_ref, out_ref, total_ref):
    step = pl.program_id(0)

    @pl.when(step == 0)
    def _():
        total_ref[...] = jnp.zeros_like(total_ref)
        out_ref[...] = jnp.zeros_like(out_ref)
        fill_khatri_rao(krt_ref, a_ref[...], b_ref[...])

    x_high, x_low = split(x_ref[...])
    high_ref[step] = x_high
    low_ref[step] = x_low
    c = c_ref[...]
    total_ref[...] += contract(x_high, x_low, c)
    add_half_gram(out_ref, core_ref[0], c)

    @pl.when(step == pl.num_programs(0) - 1)
    def _():
        store_drives(out_ref, total_ref[...], a_ref[...], b_ref[...])


def load(core, a, b, x, c):
    rows, bins = x.shape
    rank = c.shape[1]
    units = bins // PAIR
    out = shaped(a.shape[0] + b.shape[0] + rank // 2, rank)
    part = pltpu.VMEM((units, rows, PAIR), BF16)
    return call(
        load_kernel,
        "load",
        (units,),
        [
            whole(a.shape),
            whole(b.shape),
            pl.BlockSpec((rows, PAIR), lambda j, core_ref: (0, j)),
            rows_block(PAIR, rank),
        ],
        [HELD, HELD, HELD, whole(out.shape)],
        (part, part, pltpu.VMEM((2 * rank, rows), BF16), out),
        [pltpu.VMEM((rows, rank), F32)],
    )(core, a, b, pltpu.with_memory_space_constraint(x, pltpu.HBM), c)


def mass_kernel(start, core_ref, krt_ref, high_ref, low_ref, *refs):
    theirs_ref, mine_ref = refs[-2:]
    unit = start + pl.program_id(0)
    out = mass_part(krt_ref, high_ref[unit], low_ref[unit])
    store_sides(core_ref[0], out, theirs_ref, mine_ref)


def mass_products(core, krt, parts, after, start, units):
    rank = krt.shape[0] // 2
    out = shaped(units * UNIT, rank)
    side = rows_block(UNIT, rank)
    return call(
        functools.partial(mass_kernel, start),
        "mass_products",
        (units,),
        [HELD, HELD, HELD] + [NOWHERE] * len(after),
        [side, side],
        (out, out),
    )(core, in_vmem(krt), in_vmem(parts[0]), in_vmem(parts[1]), *after)


def drive_kernel(start, started, last, core_ref, a_ref, b_ref, hessian_ref, high_ref, low_ref, c_ref, mine_ref, theirs_ref, held_ref, gram_ref, *refs):
    new_ref, out_ref, out_gram_ref, total_ref = refs
    step = pl.program_id(0)
    core = core_ref[0]

    @pl.when(step == 0)
    def _():
        total_ref[...] = held_ref[...] if started else jnp.zeros_like(total_ref)
        out_gram_ref[...] = gram_ref[...] if started else jnp.zeros_like(out_gram_ref)

    new = mass_new(hessian_ref, c_ref[...], sides(core, mine_ref[...], theirs_ref[...]))
    new_ref[...] = new
    unit = start + step
    total_ref[...] += contract(high_ref[unit], low_ref[unit], new)
    add_half_gram(out_gram_ref, core, new)

    @pl.when(step == pl.num_programs(0) - 1)
    def _():
        if last:
            store_drives(out_ref, total_ref[...], a_ref[...], b_ref[...])
        else:
            out_ref[...] = total_ref[...]


def drive_products(core, a, b, hessian, parts, c, mine, theirs, held, start, last):
    rank = a.shape[1]
    rows = a.shape[0] * b.shape[0]
    units = mine.shape[0] // UNIT
    side = rows_block(UNIT, rank)
    half = shaped(rank // 2, rank)
    out = shaped(a.shape[0] + b.shape[0], rank) if last else shaped(rows, rank)
    started = held is not None
    new = shaped(units * PAIR, rank)
    total, gram_held = held if started else (mine, mine)
    return call(
        functools.partial(drive_kernel, start, started, last),
        "drive_products",
        (units,),
        [
            whole(a.shape),
            whole(b.shape),
            whole(hessian.shape),
            HELD,
            HELD,
            rows_block(PAIR, rank, start),
            side,
            side,
            whole((rows, rank)) if started else NOWHERE,
            whole(half.shape) if started else NOWHERE,
        ],
        [rows_block(PAIR, rank), whole(out.shape), whole(half.shape)],
        (new, out, half),
        [pltpu.VMEM((rows, rank), F32)],
    )(core, a, b, hessian, in_vmem(parts[0]), in_vmem(parts[1]), c, mine, theirs, total, gram_held)


def mass_new(hessian_ref, c, total):
    rank = c.shape[1]
    return c - dot(c, hessian_ref[:rank]) + total * hessian_ref[rank:, :1][:1]


def last_kernel(core_ref, hessian_ref, c_ref, mine_ref, theirs_ref, held_ref, out_ref):
    total = sides(core_ref[0], mine_ref[...], theirs_ref[...])
    out_ref[...] = mass_new(hessian_ref, c_ref[...], total)


def last_step(core, hessian, c, c_start, mine, theirs, held, start, bins):
    rank = c.shape[1]
    side = rows_block(UNIT, rank)
    first = held is None
    return call(
        last_kernel,
        "last_step",
        (mine.shape[0] // UNIT,),
        [whole(hessian.shape), rows_block(PAIR, rank, c_start), side, side, NOWHERE],
        rows_block(PAIR, rank, start),
        shaped(bins, rank),
        (),
        {} if first else {5: 0},
    )(core, hessian, c, mine, theirs, mine if first else held)


def sample_gram_kernel(core_ref, a_ref, far_ref, out_ref):
    out_ref[...] = gram(a_ref[...]) + gram(far_ref[...])


def sample_gram(core, a, far):
    rank = a.shape[1]
    return call(
        sample_gram_kernel,
        "sample_gram",
        (1,),
        [whole(a.shape), whole(a.shape)],
        whole((rank, rank)),
        shaped(rank, rank),
    )(core, a, far)


def hessian_kernel(core_ref, gram_ref, other_ref, b_ref, out_ref):
    rank = gram_ref.shape[0]
    hessian = (gram_ref[...] + other_ref[...]) * gram(b_ref[...])
    scale = inverse_norm(hessian)
    out_ref[:rank] = hessian * scale
    out_ref[rank:] = jnp.broadcast_to(scale, (8, rank))


def mass_hessian(core, gram_a, gram_a_other, b):
    rank = b.shape[1]
    square = whole((rank, rank))
    return call(
        hessian_kernel,
        "mass_hessian",
        (1,),
        [square, square, whole(b.shape)],
        whole((rank + 8, rank)),
        shaped(rank + 8, rank),
    )(core, gram_a, gram_a_other, b)


def small_step_kernel(
    core_ref,
    a_ref,
    b_ref,
    gram_a_ref,
    gram_a_other_ref,
    gram_c_ref,
    gram_c_other_ref,
    drive_ref,
    drive_far_ref,
    drive_b_ref,
    drive_b_far_ref,
    after_ref,
    new_a_ref,
    new_b_ref,
    *refs,
):
    a, b = a_ref[...], b_ref[...]
    rows = a.shape[0]
    scans = b.shape[0]
    gram_a = gram_a_ref[...] + gram_a_other_ref[...]
    gram_c = sides(core_ref[0], gram_c_ref[scans:], gram_c_other_ref[scans:])
    hessian_a = gram(b) * gram_c
    hessian_b = gram_a * gram_c
    drive_a = drive_ref[:rows] + drive_far_ref[:rows]
    drive_b = drive_b_ref[...] + drive_b_far_ref[...]
    new_a = a - (dot(a, hessian_a) - drive_a) * inverse_norm(hessian_a)
    new_b = b - (dot(b, hessian_b) - drive_b) * inverse_norm(hessian_b)
    new_a_ref[...] = new_a
    new_b_ref[...] = new_b
    if refs:
        fill_khatri_rao(refs[0], new_a, new_b)


def small_step(core, a, b, args, after, last):
    outs = [shaped(*a.shape), shaped(*b.shape)]
    specs = [whole(a.shape), whole(b.shape)]
    if not last:
        outs.append(pltpu.VMEM((2 * a.shape[1], a.shape[0] * b.shape[0]), BF16))
        specs.append(HELD)
    return call(
        small_step_kernel,
        "small_step",
        (1,),
        [whole(v.shape) for v in (a, b, *args)] + [NOWHERE],
        specs,
        outs,
    )(core, a, b, *args, after)


def swap(value, axis, size, distance):
    return lax.ppermute(value, axis, [(i, i ^ distance) for i in range(size)])


def local(mz, intensities, sample_start, scan_start, mass_start):
    a, b, c = sample_start, scan_start, mass_start
    bins, rank = c.shape
    rows, scans = a.shape[0], b.shape[0]
    x = intensities.reshape(-1, bins)
    core = (lax.axis_index("grp") % 2).reshape(1).astype(jnp.int32)

    def over_core(value):
        return swap(value, "grp", 4, 1)

    def over_x(value):
        return swap(value, "grp", 4, 2)

    def sum_mz(value):
        distance = 1
        while True:
            far = swap(value, "mz", mz, distance)
            distance *= 2
            if distance >= mz:
                return value, far
            value = value + far

    def close_drives(packed):
        packed, far = sum_mz(packed)
        tail = packed[rows:] + far[rows:]
        other = over_core(tail)
        drive_b = tail[:scans] + other[:scans]
        return tail, other, packed, far, drive_b, over_x(drive_b)

    high, low, krt, packed = load(core, a, b, x, c)
    parts = high, low
    sums = []
    after = (packed,)
    start = 0
    for number, units in enumerate(FIRST):
        theirs, mine = mass_products(core, krt, parts, after, start, units)
        after = (mine,)
        total = mine + over_core(theirs)
        if number == 0:
            total = jnp.concatenate([total, a], 0)
        far = over_x(total)
        if number == 0:
            gram_a = sample_gram(core, a, far[units * UNIT :])
            gram_a = gram_a, over_core(gram_a)
        sums.append((start, total[: units * UNIT] + far[: units * UNIT]))
        start += units
    small = close_drives(packed)
    hessian = mass_hessian(core, *gram_a, b)
    held = None
    firsts = []
    for start, total in sums[:-1]:
        new, *held = drive_products(
            core, a, b, hessian, parts, c, total, over_core(total), held, start, False
        )
        firsts.append((start, new))
    a, b, krt = small_step(core, a, b, (*gram_a, *small), held[0], False)

    lasts = []
    after = ()
    first = 0
    for number, units in enumerate(LAST):
        theirs, mine = mass_products(core, krt, parts, after, first, units)
        after = (mine,)
        total = mine + over_core(theirs)
        if number == 0:
            total = jnp.concatenate([total, a], 0)
        far = over_x(total)
        if number == 0:
            gram_a = sample_gram(core, a, far[units * UNIT :])
            gram_a = gram_a, over_core(gram_a)
        lasts.append((first, units, total[: units * UNIT] + far[: units * UNIT]))
        first += units
    start, total = sums[-1]
    new, *packed = drive_products(
        core, a, b, hessian, parts, c, total, over_core(total), held, start, True
    )
    firsts.append((start, new))
    small = close_drives(jnp.concatenate(packed, 0))
    hessian = mass_hessian(core, *gram_a, b)
    out = None
    for start, units, total in lasts:
        other = over_core(total)
        done = 0
        while done < units:
            begin, new = [v for v in firsts if v[0] <= start + done][-1]
            here = min(units - done, begin + new.shape[0] // PAIR - start - done)
            part = slice(done * UNIT, (done + here) * UNIT)
            whole_chunk = here == units
            out = last_step(
                core,
                hessian,
                new,
                start + done - begin,
                total if whole_chunk else total[part],
                other if whole_chunk else other[part],
                out,
                start + done,
                bins,
            )
            done += here
    new_a, new_b = small_step(core, a, b, (*gram_a, *small), a, True)
    return new_a, new_b, out


def solution(mesh):
    placed = (P("grp", None, "mz"), P("grp", None), P(), P("mz", None))
    return jax.shard_map(
        functools.partial(local, mesh.shape["mz"]),
        mesh=mesh,
        in_specs=placed,
        out_specs=(P("grp", None), P(), P("mz", None)),
        check_vma=False,
    )
```

time: 501 us -> 169 us (0.34); the launches traced: 492 us -> 167 us
  waiting for transfers between devices: 264 us -> 53.6 us
  matrix products: 156 us -> 0 us
  Pallas kernels: 0 us -> 69 us
  blocking collectives: 39.2 us -> 0 us
  starting transfers between devices: 0.78 us -> 30.3 us
  between operations: 18.5 us -> 0.98 us
    psum x4 -> x0, waiting for transfers between devices: 264 us -> none  [the longest x2 187 us: local(): gram_a = lax.psum(gram_of(factor_a), 'grp')]
    dot_general x18 -> x0, matrix products: 156 us -> none  [the longest x2 57.8 us: local(): lax.dot_general(unfolded, khatri_rao, (((0,), (0,)), ((), ())), precision...]
    pallas_call x0 -> x22, Pallas kernels: none -> 69 us  [the longest x3 22.6 us: drive_products(): call(functools.partial(drive_kernel, start, started, last), 'drive_produc...]
    ppermute x0 -> x33, waiting for transfers between devices: none -> 53.6 us  [swap(): return lax.ppermute(value, axis, [(i, i ^ distance) for i in range(size)])]
    psum x1 -> x0, blocking collectives: 39.2 us -> none  [local(): lax.psum(jnp.einsum('ijr,ir->jr', contracted, factor_a, precision=precise...]
    ppermute x0 -> x33, starting transfers between devices: none -> 30.3 us  [swap(): return lax.ppermute(value, axis, [(i, i ^ distance) for i in range(size)])]
    unnamed x22 -> x31, local copies, waits for them, and re-layouts: 12.2 us -> 9.44 us
  transfers between devices with their start and end apart: 4 -> 33, of which waited for: 4 -> 14; matrix products, arithmetic and copies ran while one was open for 13% -> 2% of each run, Pallas kernels for 0% -> 29%
where the time goes in v1:
time: 169 us; the launch traced here: 167 us
  Pallas kernels  69 us (41%)
  waiting for transfers between devices  53.6 us (32%)
  starting transfers between devices  30.3 us (18%)
  local copies, waits for them, and re-layouts  9.61 us (6%)
  other arithmetic  3.73 us (2%)
    ppermute x33, waiting for transfers between devices, swap(): return lax.ppermute(value, axis, [(i, i ^ distance) for i in range(size)])  53.6 us
    ppermute x33, starting transfers between devices, swap(): return lax.ppermute(value, axis, [(i, i ^ distance) for i in range(size)])  30.3 us
    pallas_call x3, Pallas kernels, drive_products(): call(functools.partial(drive_kernel, start, started, last), 'drive_produc...  22.6 us
    pallas_call x7, Pallas kernels, mass_products(): call(functools.partial(mass_kernel, start), 'mass_products', (units,), [H...  21.2 us
    pallas_call x1, Pallas kernels, load(): call(load_kernel, 'load', (units,), [whole(a.shape), whole(b.shape), pl.B...  13.6 us
    unnamed x31, local copies, waits for them, and re-layouts  9.44 us
    pallas_call x5, Pallas kernels, last_step(): call(last_kernel, 'last_step', (mine.shape[0] // UNIT,), [whole(hessian.s...  7.56 us
  transfers between devices with their start and end apart: 33, of which 14 were waited for; matrix products, arithmetic and copies ran while one was open for 2% of the time, Pallas kernels for 29%

profile of v1, /device:TPU:1, one launch (start us, length us, event | category | flops | bytes accessed | tf_op | source)
XLA Modules:
  0.0 167.2 jit_solution(12736433921566804259)
XLA Ops:
  0.7 0.9 copy-done.4
  1.6 0.7 copy-done.9
  2.2 13.6 %load.1 = (bf16[8,1024,512]{2,1,0:T(8,128)(2,1)S(1)}, bf16[8,1024,512]{2,1,0:T(8,128)(2,1)S(1)}, bf16[512,1024]{1,0:T(8,128)(2,1)S(1)}, f32[264,256]{1,0:T(8,128)S(1)}) custom-call(s32[1]{0:T(128)} %bitcast.core_ref, f32[128,256]{1,0:T(8,128)S(1)} %copy-done.4, f32[8,256]{1,0:T(8,128)S(1)} %copy-done.9, f32[1024,4096]{1,0:T(8,128)} %bitcast.2, f32[4096,256]{1,0:T(8,128)} %c_ref.7), custom_call_target="tpu_custom_call" | custom-call | tf_op jit(solution)/shard_map/load/pallas_call | solution.py:152
  15.8 1.1 mass_products.7
  16.9 4.3 %mass_products.8 = (f32[768,256]{1,0:T(8,128)}, f32[768,256]{1,0:T(8,128)}) custom-call(s32[1]{0:T(128)} %bitcast.core_ref, bf16[512,1024]{1,0:T(8,128)(2,1)S(1)} %get-tuple-element.35.krt_ref, bf16[8,1024,512]{2,1,0:T(8,128)(2,1)S(1)} %get-tuple-element.36.high_ref, bf16[8,1024,512]{2,1,0:T(8,128)(2,1)S(1)} %get-tuple-element.37.low_ref, ...), custom_call_target="tpu_custom_call" | custom-call | tf_op jit(solution)/shard_map/mass_products/pallas_call | solution.py:179
  21.3 2.4 %collective-permute-done.8 = f32[768,256]{1,0:T(8,128)S(1)} collective-permute-done((f32[768,256]{1,0:T(8,128)}, f32[768,256]{1,0:T(8,128)S(1)}, u32[]{:S(2)}, u32[]{:S(2)}) %collective-permute-start.8) | collective-permute-done | bytes 786464 | tf_op jit(solution)/shard_map/ppermute | solution.py:359
  23.8 1.2 add.76
  25.0 2.4 %collective-permute-start.9 = (f32[768,256]{1,0:T(8,128)S(1)}, f32[768,256]{1,0:T(8,128)S(1)}, u32[]{:S(2)}, u32[]{:S(2)}) collective-permute-start(f32[768,256]{1,0:T(8,128)S(1)} %add.76), channel_id=1, source_target_pairs={{0,16},{8,24},{16,0},{24,8},{1,17},{9,25},{17,1},{25,9},{2,18},{10... | collective-permute-start | bytes 2359304 | tf_op jit(solution)/shard_map/ppermute | solution.py:359
  27.4 1.2 collective-permute-start.3
  28.7 0.9 collective-permute-start
  29.6 5.2 %collective-permute-done.3 = f32[264,256]{1,0:T(8,128)S(1)} collective-permute-done((f32[264,256]{1,0:T(8,128)S(1)}, f32[264,256]{1,0:T(8,128)S(1)}, u32[]{:S(2)}, u32[]{:S(2)}) %collective-permute-start.3) | collective-permute-done | bytes 270368 | tf_op jit(solution)/shard_map/ppermute | solution.py:359
  34.8 1.4 collective-permute-start.4
  36.2 1.1 copy-done.7
  37.3 5.3 %mass_products.10 = (f32[1024,256]{1,0:T(8,128)}, f32[1024,256]{1,0:T(8,128)}) custom-call(s32[1]{0:T(128)} %bitcast.core_ref, bf16[512,1024]{1,0:T(8,128)(2,1)S(1)} %get-tuple-element.35.krt_ref, bf16[8,1024,512]{2,1,0:T(8,128)(2,1)S(1)} %get-tuple-element.36.high_ref, bf16[8,1024,512]{2,1,0:T(8,128)(2,1)S(1)} %get-tuple-element.37.low_ref, ...), custom_call_target="tpu_custom_call" | custom-call | tf_op jit(solution)/shard_map/mass_products/pallas_call | solution.py:179
  42.6 1.8 %collective-permute-start.15 = (f32[1024,256]{1,0:T(8,128)}, f32[1024,256]{1,0:T(8,128)S(1)}, u32[]{:S(2)}, u32[]{:S(2)}) collective-permute-start(f32[1024,256]{1,0:T(8,128)} %get-tuple-element.52), channel_id=1, source_target_pairs={{0,8},{8,0},{16,24},{24,16},{1,9},{9,1},{17,25},{25,17},{2,10},{10... | collective-permute-start | bytes 3145736 | tf_op jit(solution)/shard_map/ppermute | solution.py:359
  44.9 2.4 %collective-permute-start.5 = (f32[264,256]{1,0:T(8,128)S(1)}, f32[264,256]{1,0:T(8,128)S(1)}, u32[]{:S(2)}, u32[]{:S(2)}) collective-permute-start(f32[264,256]{1,0:T(8,128)S(1)} %add.73.drive_ref), channel_id=1, source_target_pairs={{0,4},{1,5},{2,6},{3,7},{4,0},{5,1},{6,2},{7,3},{8,12},{9,13},{10,... | collective-permute-start | bytes 811016 | tf_op jit(solution)/shard_map/ppermute | solution.py:359
  47.4 0.6 collective-permute-start.10
  48.0 7.3 %collective-permute-done.1 = f32[384,256]{1,0:T(8,128)S(1)} collective-permute-done((f32[384,256]{1,0:T(8,128)S(1)}, f32[384,256]{1,0:T(8,128)S(1)}, u32[]{:S(2)}, u32[]{:S(2)}) %collective-permute-start.1) | collective-permute-done | bytes 393248 | tf_op jit(solution)/shard_map/ppermute | solution.py:359
  55.8 0.9 collective-permute-start.2
  56.6 3.3 %collective-permute-done.5.drive_far_ref = f32[264,256]{1,0:T(8,128)S(1)} collective-permute-done((f32[264,256]{1,0:T(8,128)S(1)}, f32[264,256]{1,0:T(8,128)S(1)}, u32[]{:S(2)}, u32[]{:S(2)}) %collective-permute-start.5) | collective-permute-done | bytes 270368 | tf_op jit(solution)/shard_map/ppermute | solution.py:359
  59.9 0.5 collective-permute-start.6
  60.8 1.3 collective-permute-start.16
  62.1 0.6 collective-permute-start.7
  63.2 3.8 %drive_products.3 = (f32[512,256]{1,0:T(8,128)S(1)}, f32[1024,256]{1,0:T(8,128)}, f32[128,256]{1,0:T(8,128)S(1)}) custom-call(s32[1]{0:T(128)} %bitcast.core_ref, f32[128,256]{1,0:T(8,128)S(1)} %copy-done.5, f32[8,256]{1,0:T(8,128)S(1)} %copy-done.10, f32[264,256]{1,0:T(8,128)S(1)} %mass_hessian.2.hessian_ref, ...), custom_call_target="tpu_custom_call" | custom-call | tf_op jit(solution)/shard_map/drive_products/pallas_call | solution.py:223
  67.1 0.9 copy-done.14
  68.0 8.4 %drive_products.4 = (f32[1536,256]{1,0:T(8,128)}, f32[1024,256]{1,0:T(8,128)}, f32[128,256]{1,0:T(8,128)S(1)}) custom-call(s32[1]{0:T(128)} %bitcast.core_ref, f32[128,256]{1,0:T(8,128)S(1)} %copy-done.5, f32[8,256]{1,0:T(8,128)S(1)} %copy-done.10, f32[264,256]{1,0:T(8,128)S(1)} %mass_hessian.2.hessian_ref, ...), custom_call_target="tpu_custom_call" | custom-call | tf_op jit(solution)/shard_map/drive_products/pallas_call | solution.py:223
  76.4 8.9 %collective-permute-done.7.drive_b_far_ref = f32[8,256]{1,0:T(8,128)S(1)} collective-permute-done((f32[8,256]{1,0:T(8,128)S(1)}, f32[8,256]{1,0:T(8,128)S(1)}, u32[]{:S(2)}, u32[]{:S(2)}) %collective-permute-start.7) | collective-permute-done | bytes 8224 | tf_op jit(solution)/shard_map/ppermute | solution.py:359
  85.3 1.2 copy-done.6
  86.5 1.1 small_step.2
  87.6 3.4 %copy-done.2 = bf16[8,1024,512]{2,1,0:T(8,128)(2,1)S(1)} copy-done((bf16[8,1024,512]{2,1,0:T(8,128)(2,1)S(1)}, bf16[8,1024,512]{2,1,0:T(8,128)(2,1)}, u32[]{:S(2)}) %copy-start.2) | copy-done | bytes 8388632
  91.0 5.3 %mass_products.9 = (f32[1024,256]{1,0:T(8,128)}, f32[1024,256]{1,0:T(8,128)}) custom-call(s32[1]{0:T(128)} %bitcast.core_ref, bf16[512,1024]{1,0:T(8,128)(2,1)S(1)} %get-tuple-element.48.krt_ref, bf16[8,1024,512]{2,1,0:T(8,128)(2,1)S(1)} %get-tuple-element.36.high_ref, bf16[8,1024,512]{2,1,0:T(8,128)(2,1)S(1)} %copy-done.2), custom_call_target="tpu_custom_call" | custom-call | tf_op jit(solution)/shard_map/mass_products/pallas_call | solution.py:179
  96.3 1.3 collective-permute-start.12
  97.8 2.3 %collective-permute-done.12 = f32[1024,256]{1,0:T(8,128)S(1)} collective-permute-done((f32[1024,256]{1,0:T(8,128)}, f32[1024,256]{1,0:T(8,128)S(1)}, u32[]{:S(2)}, u32[]{:S(2)}) %collective-permute-start.12) | collective-permute-done | bytes 1048608 | tf_op jit(solution)/shard_map/ppermute | solution.py:359
  100.1 1.4 add.79
  101.5 1.3 collective-permute-start.13
  102.8 2.9 %mass_products.11 = (f32[512,256]{1,0:T(8,128)S(1)}, f32[512,256]{1,0:T(8,128)}) custom-call(s32[1]{0:T(128)} %bitcast.core_ref, bf16[512,1024]{1,0:T(8,128)(2,1)S(1)} %get-tuple-element.48.krt_ref, bf16[8,1024,512]{2,1,0:T(8,128)(2,1)S(1)} %get-tuple-element.36.high_ref, bf16[8,1024,512]{2,1,0:T(8,128)(2,1)S(1)} %copy-done.2, ...), custom_call_target="tpu_custom_call" | custom-call | tf_op jit(solution)/shard_map/mass_products/pallas_call | solution.py:179
  105.8 0.7 collective-permute-start.29
  106.5 1.0 copy-done.13
  107.4 10.3 %drive_products.5 = (f32[2048,256]{1,0:T(8,128)}, f32[136,256]{1,0:T(8,128)S(1)}, f32[128,256]{1,0:T(8,128)S(1)}) custom-call(s32[1]{0:T(128)} %bitcast.core_ref, f32[128,256]{1,0:T(8,128)S(1)} %get-tuple-element.46.a_ref.after_ref, f32[8,256]{1,0:T(8,128)S(1)} %get-tuple-element.47.b_ref, f32[264,256]{1,0:T(8,128)S(1)} %mass_hessian.2.hessian_ref, ...), custom_call_target="tpu_custom_call" | custom-call | tf_op jit(solution)/shard_map/drive_products/pallas_call | solution.py:223
  117.8 1.3 collective-permute-start.18
  119.5 6.5 %collective-permute-done.18 = f32[264,256]{1,0:T(8,128)S(1)} collective-permute-done((f32[264,256]{1,0:T(8,128)S(1)}, f32[264,256]{1,0:T(8,128)S(1)}, u32[]{:S(2)}, u32[]{:S(2)}) %collective-permute-start.18) | collective-permute-done | bytes 270368 | tf_op jit(solution)/shard_map/ppermute | solution.py:359
  126.1 2.7 %collective-permute-done.13 = f32[1152,256]{1,0:T(8,128)S(1)} collective-permute-done((f32[1152,256]{1,0:T(8,128)S(1)}, f32[1152,256]{1,0:T(8,128)S(1)}, u32[]{:S(2)}, u32[]{:S(2)}) %collective-permute-start.13) | collective-permute-done | bytes 1179680 | tf_op jit(solution)/shard_map/ppermute | solution.py:359
  128.9 2.1 %collective-permute-start.32 = (f32[1024,256]{1,0:T(8,128)S(1)}, f32[1024,256]{1,0:T(8,128)S(1)}, u32[]{:S(2)}, u32[]{:S(2)}) collective-permute-start(f32[1024,256]{1,0:T(8,128)S(1)} %slice_add_fusion), channel_id=1, source_target_pairs={{0,8},{8,0},{16,24},{24,16},{1,9},{9,1},{17,25},{25,17},{2,10},{10... | collective-permute-start | bytes 3145736 | tf_op jit(solution)/shard_map/ppermute | solution.py:359
  131.0 2.3 %collective-permute-done.19 = f32[264,256]{1,0:T(8,128)S(1)} collective-permute-done((f32[264,256]{1,0:T(8,128)S(1)}, f32[264,256]{1,0:T(8,128)S(1)}, u32[]{:S(2)}, u32[]{:S(2)}) %collective-permute-start.19) | collective-permute-done | bytes 270368 | tf_op jit(solution)/shard_map/ppermute | solution.py:359
  133.3 1.5 collective-permute-start.20
  134.8 1.1 mass_products.12
  135.9 1.1 mass_products.13
  137.1 1.7 %collective-permute-start.23 = (f32[256,256]{1,0:T(8,128)S(1)}, f32[256,256]{1,0:T(8,128)S(1)}, u32[]{:S(2)}, u32[]{:S(2)}) collective-permute-start(f32[256,256]{1,0:T(8,128)S(1)} %get-tuple-element.62), channel_id=1, source_target_pairs={{0,8},{8,0},{16,24},{24,16},{1,9},{9,1},{17,25},{25,17},{2,10},{10... | collective-permute-start | bytes 786440 | tf_op jit(solution)/shard_map/ppermute | solution.py:359
  138.8 1.1 collective-permute-done.23
  140.3 1.3 collective-permute-start.27
  141.7 1.0 collective-permute-start.31
  142.7 5.8 %collective-permute-done.20.drive_far_ref = f32[264,256]{1,0:T(8,128)S(1)} collective-permute-done((f32[264,256]{1,0:T(8,128)S(1)}, f32[264,256]{1,0:T(8,128)S(1)}, u32[]{:S(2)}, u32[]{:S(2)}) %collective-permute-start.20) | collective-permute-done | bytes 270368 | tf_op jit(solution)/shard_map/ppermute | solution.py:359
  148.5 0.6 collective-permute-start.21
  149.5 3.7 %collective-permute-done.27 = f32[256,256]{1,0:T(8,128)S(1)} collective-permute-done((f32[256,256]{1,0:T(8,128)S(1)}, f32[256,256]{1,0:T(8,128)S(1)}, u32[]{:S(2)}, u32[]{:S(2)}) %collective-permute-start.27) | collective-permute-done | bytes 262176 | tf_op jit(solution)/shard_map/ppermute | solution.py:359
  153.2 1.2 collective-permute-start.14
  154.5 0.6 collective-permute-start.25
  155.9 0.5 mass_hessian.3.hessian_ref
  156.3 1.7 %collective-permute-done.22.drive_b_far_ref = f32[8,256]{1,0:T(8,128)S(1)} collective-permute-done((f32[8,256]{1,0:T(8,128)S(1)}, f32[8,256]{1,0:T(8,128)S(1)}, u32[]{:S(2)}, u32[]{:S(2)}) %collective-permute-start.22) | collective-permute-done | bytes 8224 | tf_op jit(solution)/shard_map/ppermute | solution.py:359
  158.0 1.3 small_step.3
  159.3 1.2 last_step.5.held_ref
  160.8 2.4 %last_step.6.held_ref = f32[4096,256]{1,0:T(8,128)} custom-call(s32[1]{0:T(128)} %bitcast.core_ref, f32[264,256]{1,0:T(8,128)S(1)} %mass_hessian.3.hessian_ref, f32[1536,256]{1,0:T(8,128)S(1)} %copy-done.8, f32[768,256]{1,0:T(8,128)S(1)} %slice.76.mine_ref, f32[768,256]{1,0:T(8,128)S(1)} %slice.77.theirs_ref, ...), custom_call_target="tpu_custom_call", output_to_operand_aliasing={{}: (5, {})} | custom-call | tf_op jit(solution)/shard_map/last_step/pallas_call | solution.py:259
  163.2 1.6 last_step.7.held_ref
  164.8 1.2 last_step.8.held_ref
  166.0 1.2 last_step.9
  (86 shorter events, 5.0 us)
Async XLA Ops:
  0.6 0.9 copy-start.4
  1.5 0.7 copy-start.9
  15.8 20.4 %copy-start = (bf16[8,1024,512]{2,1,0:T(8,128)(2,1)}, bf16[8,1024,512]{2,1,0:T(8,128)(2,1)S(1)}, u32[]{:S(2)}) copy-start(bf16[8,1024,512]{2,1,0:T(8,128)(2,1)S(1)} %get-tuple-element.37.low_ref) | copy-start | bytes 25165828
  21.3 2.5 %collective-permute-start.8 = (f32[768,256]{1,0:T(8,128)}, f32[768,256]{1,0:T(8,128)S(1)}, u32[]{:S(2)}, u32[]{:S(2)}) collective-permute-start(f32[768,256]{1,0:T(8,128)} %get-tuple-element.42), channel_id=1, source_target_pairs={{0,8},{8,0},{16,24},{24,16},{1,9},{9,1},{17,25},{25,17},{2,10},{10... | collective-permute-start | bytes 2359304 | tf_op jit(solution)/shard_map/ppermute | solution.py:359
  25.0 22.2 %collective-permute-start.9 = (f32[768,256]{1,0:T(8,128)S(1)}, f32[768,256]{1,0:T(8,128)S(1)}, u32[]{:S(2)}, u32[]{:S(2)}) collective-permute-start(f32[768,256]{1,0:T(8,128)S(1)} %add.76), channel_id=1, source_target_pairs={{0,16},{8,24},{16,0},{24,8},{1,17},{9,25},{17,1},{25,9},{2,18},{10... | collective-permute-start | bytes 2359304 | tf_op jit(solution)/shard_map/ppermute | solution.py:359
  27.4 7.4 %collective-permute-start.3 = (f32[264,256]{1,0:T(8,128)S(1)}, f32[264,256]{1,0:T(8,128)S(1)}, u32[]{:S(2)}, u32[]{:S(2)}) collective-permute-start(f32[264,256]{1,0:T(8,128)S(1)} %get-tuple-element.38.refs_0_), channel_id=1, source_target_pairs={{0,1},{1,0},{2,3},{3,2},{4,5},{5,4},{6,7},{7,6},{8,9},{9,8},{10,11... | collective-permute-start | bytes 811016 | tf_op jit(solution)/shard_map/ppermute | solution.py:359
  28.7 15.8 %collective-permute-start = (f32[256,256]{1,0:T(8,128)S(1)}, f32[256,256]{1,0:T(8,128)S(1)}, u32[]{:S(2)}, u32[]{:S(2)}) collective-permute-start(f32[256,256]{1,0:T(8,128)S(1)} %get-tuple-element.40), channel_id=1, source_target_pairs={{0,8},{8,0},{16,24},{24,16},{1,9},{9,1},{17,25},{25,17},{2,10},{10... | collective-permute-start | bytes 786440 | tf_op jit(solution)/shard_map/ppermute | solution.py:359
  34.8 10.0 %collective-permute-start.4 = (f32[264,256]{1,0:T(8,128)S(1)}, f32[264,256]{1,0:T(8,128)S(1)}, u32[]{:S(2)}, u32[]{:S(2)}) collective-permute-start(f32[264,256]{1,0:T(8,128)S(1)} %add.72), channel_id=1, source_target_pairs={{0,2},{1,3},{2,0},{3,1},{4,6},{5,7},{6,4},{7,5},{8,10},{9,11},{10,... | collective-permute-start | bytes 811016 | tf_op jit(solution)/shard_map/ppermute | solution.py:359
  36.2 1.1 copy-start.7
  42.6 18.0 %copy-start.12 = (f32[1024,256]{1,0:T(8,128)S(1)}, f32[1024,256]{1,0:T(8,128)}, u32[]{:S(2)}) copy-start(f32[1024,256]{1,0:T(8,128)} %get-tuple-element.51) | copy-start | bytes 3145732
  42.6 18.0 %collective-permute-start.15 = (f32[1024,256]{1,0:T(8,128)}, f32[1024,256]{1,0:T(8,128)S(1)}, u32[]{:S(2)}, u32[]{:S(2)}) collective-permute-start(f32[1024,256]{1,0:T(8,128)} %get-tuple-element.52), channel_id=1, source_target_pairs={{0,8},{8,0},{16,24},{24,16},{1,9},{9,1},{17,25},{25,17},{2,10},{10... | collective-permute-start | bytes 3145736 | tf_op jit(solution)/shard_map/ppermute | solution.py:359
  44.5 18.2 %copy-start.10 = (f32[8,256]{1,0:T(8,128)S(1)}, f32[8,256]{1,0:T(8,128)}, u32[]{:S(2)}) copy-start(f32[8,256]{1,0:T(8,128)} %b_ref.9) | copy-start | bytes 24580
  44.5 10.8 %collective-permute-start.1 = (f32[384,256]{1,0:T(8,128)S(1)}, f32[384,256]{1,0:T(8,128)S(1)}, u32[]{:S(2)}, u32[]{:S(2)}) collective-permute-start(f32[384,256]{1,0:T(8,128)S(1)} %pad_maximum_fusion.1), channel_id=1, source_target_pairs={{0,16},{8,24},{16,0},{24,8},{1,17},{9,25},{17,1},{25,9},{2,18},{10... | collective-permute-start | bytes 1179656 | tf_op jit(solution)/shard_map/ppermute | solution.py:359
  44.8 18.4 %copy-start.1 = (bf16[8,1024,512]{2,1,0:T(8,128)(2,1)S(1)}, bf16[8,1024,512]{2,1,0:T(8,128)(2,1)}, u32[]{:S(2)}) copy-start(bf16[8,1024,512]{2,1,0:T(8,128)(2,1)} %copy-done) | copy-start | bytes 25165828
  44.9 18.4 %copy-start.5 = (f32[128,256]{1,0:T(8,128)S(1)}, f32[128,256]{1,0:T(8,128)}, u32[]{:S(2)}) copy-start(f32[128,256]{1,0:T(8,128)} %a_ref.9) | copy-start | bytes 393220
  44.9 15.0 %collective-permute-start.5 = (f32[264,256]{1,0:T(8,128)S(1)}, f32[264,256]{1,0:T(8,128)S(1)}, u32[]{:S(2)}, u32[]{:S(2)}) collective-permute-start(f32[264,256]{1,0:T(8,128)S(1)} %add.73.drive_ref), channel_id=1, source_target_pairs={{0,4},{1,5},{2,6},{3,7},{4,0},{5,1},{6,2},{7,3},{8,12},{9,13},{10,... | collective-permute-start | bytes 811016 | tf_op jit(solution)/shard_map/ppermute | solution.py:359
  47.4 19.7 %collective-permute-start.10 = (f32[768,256]{1,0:T(8,128)S(1)}, f32[768,256]{1,0:T(8,128)S(1)}, u32[]{:S(2)}, u32[]{:S(2)}) collective-permute-start(f32[768,256]{1,0:T(8,128)S(1)} %add.77.mine_ref), channel_id=1, source_target_pairs={{0,8},{8,0},{16,24},{24,16},{1,9},{9,1},{17,25},{25,17},{2,10},{10... | collective-permute-start | bytes 2359304 | tf_op jit(solution)/shard_map/ppermute | solution.py:359
  55.8 7.0 %collective-permute-start.2 = (f32[256,256]{1,0:T(8,128)S(1)}, f32[256,256]{1,0:T(8,128)S(1)}, u32[]{:S(2)}, u32[]{:S(2)}) collective-permute-start(f32[256,256]{1,0:T(8,128)S(1)} %sample_gram.2.gram_ref.gram_a_ref), channel_id=1, source_target_pairs={{0,8},{8,0},{16,24},{24,16},{1,9},{9,1},{17,25},{25,17},{2,10},{10... | collective-permute-start | bytes 786440 | tf_op jit(solution)/shard_map/ppermute | solution.py:359
  59.9 2.2 %collective-permute-start.6 = (f32[136,256]{1,0:T(8,128)S(1)}, f32[136,256]{1,0:T(8,128)S(1)}, u32[]{:S(2)}, u32[]{:S(2)}) collective-permute-start(f32[136,256]{1,0:T(8,128)S(1)} %slice_add_fusion.3.gram_c_ref), channel_id=1, source_target_pairs={{0,8},{8,0},{16,24},{24,16},{1,9},{9,1},{17,25},{25,17},{2,10},{10... | collective-permute-start | bytes 417800 | tf_op jit(solution)/shard_map/ppermute | solution.py:359
  60.5 2.7 %collective-permute-start.11 = (f32[256,256]{1,0:T(8,128)S(1)}, f32[256,256]{1,0:T(8,128)S(1)}, u32[]{:S(2)}, u32[]{:S(2)}) collective-permute-start(f32[256,256]{1,0:T(8,128)S(1)} %slice_add_fusion.1.mine_ref.held_ref.gram_ref), channel_id=1, source_target_pairs={{0,8},{8,0},{16,24},{24,16},{1,9},{9,1},{17,25},{25,17},{2,10},{10... | collective-permute-start | bytes 786440 | tf_op jit(solution)/shard_map/ppermute | solution.py:359
  60.8 36.8 %collective-permute-start.16 = (f32[1024,256]{1,0:T(8,128)S(1)}, f32[1024,256]{1,0:T(8,128)S(1)}, u32[]{:S(2)}, u32[]{:S(2)}) collective-permute-start(f32[1024,256]{1,0:T(8,128)S(1)} %add.80), channel_id=1, source_target_pairs={{0,16},{8,24},{16,0},{24,8},{1,17},{9,25},{17,1},{25,9},{2,18},{10... | collective-permute-start | bytes 3145736 | tf_op jit(solution)/shard_map/ppermute | solution.py:359
  62.1 23.2 %collective-permute-start.7 = (f32[8,256]{1,0:T(8,128)S(1)}, f32[8,256]{1,0:T(8,128)S(1)}, u32[]{:S(2)}, u32[]{:S(2)}) collective-permute-start(f32[8,256]{1,0:T(8,128)S(1)} %slice_add_fusion.5.drive_b_ref), channel_id=1, source_target_pairs={{0,16},{8,24},{16,0},{24,8},{1,17},{9,25},{17,1},{25,9},{2,18},{10... | collective-permute-start | bytes 24584 | tf_op jit(solution)/shard_map/ppermute | solution.py:359
  67.1 0.9 copy-start.14
  85.3 1.2 copy-start.6
  87.6 3.4 %copy-start.2 = (bf16[8,1024,512]{2,1,0:T(8,128)(2,1)S(1)}, bf16[8,1024,512]{2,1,0:T(8,128)(2,1)}, u32[]{:S(2)}) copy-start(bf16[8,1024,512]{2,1,0:T(8,128)(2,1)} %copy-done) | copy-start | bytes 25165828
  96.3 3.8 %collective-permute-start.12 = (f32[1024,256]{1,0:T(8,128)}, f32[1024,256]{1,0:T(8,128)S(1)}, u32[]{:S(2)}, u32[]{:S(2)}) collective-permute-start(f32[1024,256]{1,0:T(8,128)} %get-tuple-element.50), channel_id=1, source_target_pairs={{0,8},{8,0},{16,24},{24,16},{1,9},{9,1},{17,25},{25,17},{2,10},{10... | collective-permute-start | bytes 3145736 | tf_op jit(solution)/shard_map/ppermute | solution.py:359
  97.7 8.7 %collective-permute-start.17 = (f32[1024,256]{1,0:T(8,128)S(1)}, f32[1024,256]{1,0:T(8,128)S(1)}, u32[]{:S(2)}, u32[]{:S(2)}) collective-permute-start(f32[1024,256]{1,0:T(8,128)S(1)} %add.81.mine_ref), channel_id=1, source_target_pairs={{0,8},{8,0},{16,24},{24,16},{1,9},{9,1},{17,25},{25,17},{2,10},{10... | collective-permute-start | bytes 3145736 | tf_op jit(solution)/shard_map/ppermute | solution.py:359
  101.5 27.2 %collective-permute-start.13 = (f32[1152,256]{1,0:T(8,128)S(1)}, f32[1152,256]{1,0:T(8,128)S(1)}, u32[]{:S(2)}, u32[]{:S(2)}) collective-permute-start(f32[1152,256]{1,0:T(8,128)S(1)} %pad_maximum_fusion), channel_id=1, source_target_pairs={{0,16},{8,24},{16,0},{24,8},{1,17},{9,25},{17,1},{25,9},{2,18},{10... | collective-permute-start | bytes 3538952 | tf_op jit(solution)/shard_map/ppermute | solution.py:359
  105.8 13.3 %collective-permute-start.29 = (f32[512,256]{1,0:T(8,128)S(1)}, f32[512,256]{1,0:T(8,128)S(1)}, u32[]{:S(2)}, u32[]{:S(2)}) collective-permute-start(f32[512,256]{1,0:T(8,128)S(1)} %get-tuple-element.64), channel_id=1, source_target_pairs={{0,8},{8,0},{16,24},{24,16},{1,9},{9,1},{17,25},{25,17},{2,10},{10... | collective-permute-start | bytes 1572872 | tf_op jit(solution)/shard_map/ppermute | solution.py:359
  106.4 1.0 copy-start.13
  107.4 11.7 %copy-start.11 = (f32[512,256]{1,0:T(8,128)S(1)}, f32[512,256]{1,0:T(8,128)}, u32[]{:S(2)}) copy-start(f32[512,256]{1,0:T(8,128)} %get-tuple-element.59.refs_0_) | copy-start | bytes 1572868
  117.8 8.2 %collective-permute-start.18 = (f32[264,256]{1,0:T(8,128)S(1)}, f32[264,256]{1,0:T(8,128)S(1)}, u32[]{:S(2)}, u32[]{:S(2)}) collective-permute-start(f32[264,256]{1,0:T(8,128)S(1)} %constant_dynamic-update-slice_fusion), channel_id=1, source_target_pairs={{0,1},{1,0},{2,3},{3,2},{4,5},{5,4},{6,7},{7,6},{8,9},{9,8},{10,11... | collective-permute-start | bytes 811016 | tf_op jit(solution)/shard_map/ppermute | solution.py:359
  119.2 22.4 %collective-permute-start.30 = (f32[512,256]{1,0:T(8,128)S(1)}, f32[512,256]{1,0:T(8,128)S(1)}, u32[]{:S(2)}, u32[]{:S(2)}) collective-permute-start(f32[512,256]{1,0:T(8,128)S(1)} %add.90), channel_id=1, source_target_pairs={{0,16},{8,24},{16,0},{24,8},{1,17},{9,25},{17,1},{25,9},{2,18},{10... | collective-permute-start | bytes 1572872 | tf_op jit(solution)/shard_map/ppermute | solution.py:359
  126.0 7.3 %collective-permute-start.19 = (f32[264,256]{1,0:T(8,128)S(1)}, f32[264,256]{1,0:T(8,128)S(1)}, u32[]{:S(2)}, u32[]{:S(2)}) collective-permute-start(f32[264,256]{1,0:T(8,128)S(1)} %add.82), channel_id=1, source_target_pairs={{0,2},{1,3},{2,0},{3,1},{4,6},{5,7},{6,4},{7,5},{8,10},{9,11},{10,... | collective-permute-start | bytes 811016 | tf_op jit(solution)/shard_map/ppermute | solution.py:359
  128.9 30.4 %collective-permute-start.32 = (f32[1024,256]{1,0:T(8,128)S(1)}, f32[1024,256]{1,0:T(8,128)S(1)}, u32[]{:S(2)}, u32[]{:S(2)}) collective-permute-start(f32[1024,256]{1,0:T(8,128)S(1)} %slice_add_fusion), channel_id=1, source_target_pairs={{0,8},{8,0},{16,24},{24,16},{1,9},{9,1},{17,25},{25,17},{2,10},{10... | collective-permute-start | bytes 3145736 | tf_op jit(solution)/shard_map/ppermute | solution.py:359
  133.3 15.1 %collective-permute-start.20 = (f32[264,256]{1,0:T(8,128)S(1)}, f32[264,256]{1,0:T(8,128)S(1)}, u32[]{:S(2)}, u32[]{:S(2)}) collective-permute-start(f32[264,256]{1,0:T(8,128)S(1)} %add.83.drive_ref), channel_id=1, source_target_pairs={{0,4},{1,5},{2,6},{3,7},{4,0},{5,1},{6,2},{7,3},{8,12},{9,13},{10,... | collective-permute-start | bytes 811016 | tf_op jit(solution)/shard_map/ppermute | solution.py:359
  137.1 2.9 %collective-permute-start.23 = (f32[256,256]{1,0:T(8,128)S(1)}, f32[256,256]{1,0:T(8,128)S(1)}, u32[]{:S(2)}, u32[]{:S(2)}) collective-permute-start(f32[256,256]{1,0:T(8,128)S(1)} %get-tuple-element.62), channel_id=1, source_target_pairs={{0,8},{8,0},{16,24},{24,16},{1,9},{9,1},{17,25},{25,17},{2,10},{10... | collective-permute-start | bytes 786440 | tf_op jit(solution)/shard_map/ppermute | solution.py:359
  138.8 1.5 collective-permute-start.26
  140.0 14.4 %collective-permute-start.24 = (f32[256,256]{1,0:T(8,128)S(1)}, f32[256,256]{1,0:T(8,128)S(1)}, u32[]{:S(2)}, u32[]{:S(2)}) collective-permute-start(f32[256,256]{1,0:T(8,128)S(1)} %add.86), channel_id=1, source_target_pairs={{0,16},{8,24},{16,0},{24,8},{1,17},{9,25},{17,1},{25,9},{2,18},{10... | collective-permute-start | bytes 786440 | tf_op jit(solution)/shard_map/ppermute | solution.py:359
  140.3 12.8 %collective-permute-start.27 = (f32[256,256]{1,0:T(8,128)S(1)}, f32[256,256]{1,0:T(8,128)S(1)}, u32[]{:S(2)}, u32[]{:S(2)}) collective-permute-start(f32[256,256]{1,0:T(8,128)S(1)} %add.88), channel_id=1, source_target_pairs={{0,16},{8,24},{16,0},{24,8},{1,17},{9,25},{17,1},{25,9},{2,18},{10... | collective-permute-start | bytes 786440 | tf_op jit(solution)/shard_map/ppermute | solution.py:359
  141.7 21.5 %collective-permute-start.31 = (f32[512,256]{1,0:T(8,128)S(1)}, f32[512,256]{1,0:T(8,128)S(1)}, u32[]{:S(2)}, u32[]{:S(2)}) collective-permute-start(f32[512,256]{1,0:T(8,128)S(1)} %add.91.mine_ref), channel_id=1, source_target_pairs={{0,8},{8,0},{16,24},{24,16},{1,9},{9,1},{17,25},{25,17},{2,10},{10... | collective-permute-start | bytes 1572872 | tf_op jit(solution)/shard_map/ppermute | solution.py:359
  148.5 6.1 %collective-permute-start.21 = (f32[136,256]{1,0:T(8,128)S(1)}, f32[136,256]{1,0:T(8,128)S(1)}, u32[]{:S(2)}, u32[]{:S(2)}) collective-permute-start(f32[136,256]{1,0:T(8,128)S(1)} %slice_add_fusion.2.gram_c_ref), channel_id=1, source_target_pairs={{0,8},{8,0},{16,24},{24,16},{1,9},{9,1},{17,25},{25,17},{2,10},{10... | collective-permute-start | bytes 417800 | tf_op jit(solution)/shard_map/ppermute | solution.py:359
  153.2 2.4 %collective-permute-start.14 = (f32[256,256]{1,0:T(8,128)S(1)}, f32[256,256]{1,0:T(8,128)S(1)}, u32[]{:S(2)}, u32[]{:S(2)}) collective-permute-start(f32[256,256]{1,0:T(8,128)S(1)} %sample_gram.3.gram_a_ref.gram_ref), channel_id=1, source_target_pairs={{0,8},{8,0},{16,24},{24,16},{1,9},{9,1},{17,25},{25,17},{2,10},{10... | collective-permute-start | bytes 786440 | tf_op jit(solution)/shard_map/ppermute | solution.py:359
  154.4 10.4 %collective-permute-start.28 = (f32[256,256]{1,0:T(8,128)S(1)}, f32[256,256]{1,0:T(8,128)S(1)}, u32[]{:S(2)}, u32[]{:S(2)}) collective-permute-start(f32[256,256]{1,0:T(8,128)S(1)} %add.89.mine_ref), channel_id=1, source_target_pairs={{0,8},{8,0},{16,24},{24,16},{1,9},{9,1},{17,25},{25,17},{2,10},{10... | collective-permute-start | bytes 786440 | tf_op jit(solution)/shard_map/ppermute | solution.py:359
  154.5 11.4 %collective-permute-start.25 = (f32[256,256]{1,0:T(8,128)S(1)}, f32[256,256]{1,0:T(8,128)S(1)}, u32[]{:S(2)}, u32[]{:S(2)}) collective-permute-start(f32[256,256]{1,0:T(8,128)S(1)} %add.87.mine_ref), channel_id=1, source_target_pairs={{0,8},{8,0},{16,24},{24,16},{1,9},{9,1},{17,25},{25,17},{2,10},{10... | collective-permute-start | bytes 786440 | tf_op jit(solution)/shard_map/ppermute | solution.py:359
  155.5 2.5 %collective-permute-start.22 = (f32[8,256]{1,0:T(8,128)S(1)}, f32[8,256]{1,0:T(8,128)S(1)}, u32[]{:S(2)}, u32[]{:S(2)}) collective-permute-start(f32[8,256]{1,0:T(8,128)S(1)} %slice_add_fusion.4.drive_b_ref), channel_id=1, source_target_pairs={{0,16},{8,24},{16,0},{24,8},{1,17},{9,25},{17,1},{25,9},{2,18},{10... | collective-permute-start | bytes 24584 | tf_op jit(solution)/shard_map/ppermute | solution.py:359
  159.3 1.5 copy-start.8
  160.8 2.4 %copy-start.3 = (f32[2048,256]{1,0:T(8,128)S(1)}, f32[2048,256]{1,0:T(8,128)}, u32[]{:S(2)}) copy-start(f32[2048,256]{1,0:T(8,128)} %get-tuple-element.58.c_ref) | copy-start | bytes 6291460

commit v2 on v0

v2 whole, which is shorter than its diff:
```python
import functools

import jax
import jax.numpy as jnp
from jax import lax
from jax.experimental import pallas as pl
from jax.experimental.pallas import tpu as pltpu
from jax.sharding import PartitionSpec as P

STEPS = 2
UNIT = 256
PAIR = 2 * UNIT
FIRST = (False, True, True, False)
LAST = ((0, 0, 2), (1, 0, 2), (2, 0, 2), (3, 0, 2))
F32 = jnp.float32
BF16 = jnp.bfloat16
VMEM_LIMIT = 6 << 20
LOAD_VMEM_LIMIT = 20 << 20
NOWHERE = pl.BlockSpec(memory_space=pl.ANY)
HELD = pl.BlockSpec(memory_space=pltpu.VMEM)


def split(value):
    high = value.astype(BF16)
    return high, (value - high.astype(F32)).astype(BF16)


def plain(a, b):
    return jnp.dot(a, b, preferred_element_type=F32)


def dot(a, b):
    a_high, a_low = split(a)
    b_high, b_low = split(b)
    return plain(a_high, b_high) + (plain(a_high, b_low) + plain(a_low, b_high))


def gram(factor):
    return dot(factor.T, factor)


def inverse_norm(matrix):
    return 1.0 / jnp.sqrt(jnp.sum(matrix * matrix, keepdims=True) + 1e-12)


def in_vmem(value):
    return pltpu.with_memory_space_constraint(value, pltpu.VMEM)


def shaped(*dims):
    return jax.ShapeDtypeStruct(dims, F32)


def whole(shape):
    return pl.BlockSpec(shape, lambda *_: (0,) * len(shape))


def in_hbm(value):
    return pltpu.with_memory_space_constraint(value, pltpu.HBM)


def rows_block(rows, rank, start=0):
    return pl.BlockSpec((rows, rank), lambda j, *_: (start + j, 0))


def call(kernel, name, grid, in_specs, out_specs, out_shape, scratch=(), aliases=None, kept=()):
    inputs = len(in_specs)

    def without_kept(core_ref, *refs):
        kernel(core_ref, *refs[:inputs], *refs[inputs + len(kept) :])

    run = pl.pallas_call(
        without_kept if kept else kernel,
        grid_spec=pltpu.PrefetchScalarGridSpec(
            num_scalar_prefetch=1,
            grid=grid,
            in_specs=list(in_specs) + [HELD for _ in kept],
            out_specs=out_specs,
            scratch_shapes=scratch,
        ),
        out_shape=out_shape,
        input_output_aliases=aliases or {},
        cost_estimate=pl.CostEstimate(flops=0, bytes_accessed=0, transcendentals=0),
        compiler_params=pltpu.CompilerParams(
            vmem_limit_bytes=LOAD_VMEM_LIMIT if name in ("load", "first_products") else VMEM_LIMIT
        ),
        name=name,
    )
    return lambda *args: run(*args, *(in_vmem(value) for value in kept))


def give_kernel(start, core_ref, x_ref, after_ref, out_ref, sem):
    bins = x_ref.shape[1]
    column = (1 - core_ref[0]) * (bins // 2) + start * PAIR
    copy = pltpu.make_async_copy(
        x_ref.at[:, pl.ds(pl.multiple_of(column, PAIR), PAIR)], out_ref, sem
    )
    copy.start()
    copy.wait()


def give(core, x, after, start):
    return call(
        functools.partial(give_kernel, start),
        "give",
        (1,),
        [NOWHERE, NOWHERE],
        HELD,
        pltpu.VMEM((x.shape[0], PAIR), F32),
        [pltpu.SemaphoreType.DMA],
    )(core, in_hbm(x), after)


def add_kernel(core_ref, near_ref, far_ref, *refs):
    refs[-1][...] = near_ref[...] + far_ref[...]


def add(core, near, far, after, kept):
    block = whole(near.shape)
    return call(
        add_kernel,
        "add",
        (1,),
        [block, block] + [NOWHERE for _ in after],
        block,
        shaped(*near.shape),
        kept=kept,
    )(core, near, far, *after)


def fill_khatri_rao(krt_ref, a, b):
    rank = a.shape[1]
    product = (a[:, None, :] * b[None, :, :]).reshape(-1, rank).T
    krt_ref[:rank], krt_ref[rank:] = split(product)


def mass_part(krt_ref, x_high, x_low):
    rank = krt_ref.shape[0] // 2
    both = plain(krt_ref[...], x_high)
    return (both[:rank] + (both[rank:] + plain(krt_ref[:rank], x_low))).T


def contract(x_high, x_low, c):
    rank = c.shape[1]
    c_high, c_low = split(c)
    both = plain(x_high, jnp.concatenate([c_high, c_low], 1))
    return both[:, :rank] + (both[:, rank:] + plain(x_low, c_high))


def store_sums(core, keep_ref, send_ref, total, squares, a, b):
    both = a.shape[0]
    rows, scans, half = both // 2, b.shape[0], squares.shape[0] // 2
    folded = total.reshape(both, scans, a.shape[1])
    drive = jnp.sum(folded * b[None], 1)
    drive_b = jnp.sum(folded * a[:, None, :], 0)
    keep_ref[:rows], send_ref[:rows] = drive[:rows], drive[rows:]
    keep_ref[rows : rows + scans] = drive_b
    send_ref[rows : rows + scans] = drive_b
    at_zero = core == 0
    keep_ref[rows + scans :] = jnp.where(at_zero, squares[:half], squares[half:])
    send_ref[rows + scans :] = jnp.where(at_zero, squares[half:], squares[:half])


def load_kernel(started, last, with_mass, core_ref, a_ref, b_ref, x_ref, other_ref, c_ref, krt_in_ref, total_in_ref, gram_in_ref, after_ref, *refs):
    high_ref, low_ref, *refs = refs
    if with_mass:
        mass_ref, *refs = refs
    if last:
        keep_ref, send_ref, *refs = refs
    total_ref, gram_ref, *refs = refs
    krt_ref = krt_in_ref if started else refs[0]
    step = pl.program_id(0)
    rows = x_ref.shape[0]

    @pl.when(step == 0)
    def _():
        total_ref[...] = total_in_ref[...] if started else jnp.zeros_like(total_ref)
        gram_ref[...] = gram_in_ref[...] if started else jnp.zeros_like(gram_ref)
        if not started:
            fill_khatri_rao(krt_ref, a_ref[...], b_ref[...])

    high_ref[step, :rows], low_ref[step, :rows] = split(x_ref[...])
    high_ref[step, rows:], low_ref[step, rows:] = split(other_ref[...])
    x_high, x_low = high_ref[step], low_ref[step]
    if with_mass:
        mass_ref[...] = mass_part(krt_ref, x_high, x_low)
    c = c_ref[...]
    total_ref[...] += contract(x_high, x_low, c)
    gram_ref[...] += gram(c)

    if last:

        @pl.when(step == pl.num_programs(0) - 1)
        def _():
            store_sums(
                core_ref[0], keep_ref, send_ref, total_ref[...], gram_ref[...], a_ref[...], b_ref[...]
            )


def load(core, a, b, x, other, c, krt, held, after, kept, start, last, with_mass):
    rows, bins = x.shape
    rank = c.shape[1]
    blocks = bins // (2 * PAIR)
    started = held is not None
    units = other.shape[1] // PAIR
    part = pltpu.VMEM((units, 2 * rows, PAIR), BF16)
    mass = [shaped(units * PAIR, rank)] if with_mass else []
    total, squares = shaped(2 * rows, rank), shaped(rank, rank)
    sums = shaped(a.shape[0] // 2 + b.shape[0] + rank // 2, rank)
    tail = [sums, sums] if last else [pltpu.VMEM(total.shape, F32), squares]
    tail_specs = [whole(sums.shape)] * 2 if last else [HELD, whole(squares.shape)]
    if not started:
        tail.append(pltpu.VMEM((2 * rank, 2 * rows), BF16))
        tail_specs.append(HELD)
    return call(
        functools.partial(load_kernel, started, last, with_mass),
        "load",
        (units,),
        [
            whole(a.shape),
            whole(b.shape),
            pl.BlockSpec((rows, PAIR), lambda j, core_ref: (0, core_ref[0] * blocks + start + j)),
            pl.BlockSpec((rows, PAIR), lambda j, core_ref: (0, j)),
            pl.BlockSpec((PAIR, rank), lambda j, core_ref: (core_ref[0] * blocks + start + j, 0)),
            HELD if started else NOWHERE,
            HELD if started else NOWHERE,
            whole(squares.shape) if started else NOWHERE,
            NOWHERE,
        ],
        [HELD, HELD] + [rows_block(PAIR, rank) for _ in mass] + tail_specs,
        [part, part] + mass + tail,
        [pltpu.VMEM(total.shape, F32), pltpu.VMEM(squares.shape, F32)] if last else [],
        kept=kept,
    )(
        core,
        a,
        b,
        in_hbm(x),
        in_hbm(other) if not started else other,
        in_hbm(c),
        in_vmem(krt) if started else after,
        in_vmem(held[0]) if started else after,
        held[1] if started else after,
        after,
    )


def first_kernel(core_ref, a_ref, b_ref, x_ref, other_ref, after_ref, out_ref, krt_ref):
    fill_khatri_rao(krt_ref, a_ref[...], b_ref[...])
    x_high, x_low = split(jnp.concatenate([x_ref[...], other_ref[...]], 0))
    out_ref[...] = mass_part(krt_ref, x_high, x_low)


def first_products(core, a, b, x, other, after):
    rows, bins = x.shape
    rank = a.shape[1]
    blocks = bins // (2 * PAIR)
    return call(
        first_kernel,
        "first_products",
        (1,),
        [
            whole(a.shape),
            whole(b.shape),
            pl.BlockSpec((rows, PAIR), lambda j, core_ref: (0, core_ref[0] * blocks)),
            whole(other.shape),
            NOWHERE,
        ],
        whole((PAIR, rank)),
        shaped(PAIR, rank),
        [pltpu.VMEM((2 * rank, 2 * rows), BF16)],
    )(core, a, b, in_hbm(x), other, after)


def mass_kernel(start, core_ref, krt_ref, high_ref, low_ref, after_ref, out_ref):
    unit = start + pl.program_id(0)
    columns = pl.ds(pl.multiple_of(unit % 2 * UNIT, UNIT), UNIT)
    out_ref[...] = mass_part(krt_ref, high_ref[unit // 2, :, columns], low_ref[unit // 2, :, columns])


def mass_products(core, krt, parts, after, kept, start, units):
    rank = krt.shape[0] // 2
    return call(
        functools.partial(mass_kernel, start),
        "mass_products",
        (units,),
        [HELD, HELD, HELD, NOWHERE],
        rows_block(UNIT, rank),
        shaped(units * UNIT, rank),
        kept=kept,
    )(core, in_vmem(krt), in_vmem(parts[0]), in_vmem(parts[1]), after)


def drive_kernel(start, started, last, core_ref, a_ref, b_ref, scale_ref, high_ref, low_ref, base_ref, near_ref, far_ref, total_in_ref, gram_in_ref, after_ref, *refs):
    if last:
        new_ref, keep_ref, send_ref, total_ref, gram_ref = refs
    else:
        new_ref, total_ref, gram_ref = refs
    step = pl.program_id(0)

    @pl.when(step == 0)
    def _():
        total_ref[...] = total_in_ref[...] if started else jnp.zeros_like(total_ref)
        gram_ref[...] = gram_in_ref[...] if started else jnp.zeros_like(gram_ref)

    place = pl.ds(pl.multiple_of((start + step) * PAIR, PAIR), PAIR)
    new = base_ref[place] + (near_ref[...] + far_ref[...]) * scale_ref[:1, :1]
    new_ref[pl.ds(pl.multiple_of(step * PAIR, PAIR), PAIR)] = new
    total_ref[...] += contract(high_ref[step], low_ref[step], new)
    gram_ref[...] += gram(new)

    if last:

        @pl.when(step == pl.num_programs(0) - 1)
        def _():
            store_sums(
                core_ref[0], keep_ref, send_ref, total_ref[...], gram_ref[...], a_ref[...], b_ref[...]
            )


def drive_products(core, a, b, scale, parts, base, near, far, held, after, kept, start, last):
    rank = a.shape[1]
    units, rows = parts[0].shape[:2]
    started = held is not None
    total, squares = shaped(rows, rank), shaped(rank, rank)
    sums = shaped(a.shape[0] // 2 + b.shape[0] + rank // 2, rank)
    tail = [sums, sums] if last else [pltpu.VMEM(total.shape, F32), squares]
    tail_specs = [whole(sums.shape)] * 2 if last else [HELD, whole(squares.shape)]
    return call(
        functools.partial(drive_kernel, start, started, last),
        "drive_products",
        (units,),
        [
            whole(a.shape),
            whole(b.shape),
            whole(scale.shape),
            HELD,
            HELD,
            HELD,
            rows_block(PAIR, rank),
            rows_block(PAIR, rank),
            HELD if started else NOWHERE,
            whole(squares.shape) if started else NOWHERE,
            NOWHERE,
        ],
        [HELD] + tail_specs,
        [pltpu.VMEM((units * PAIR, rank), F32)] + tail,
        [pltpu.VMEM(total.shape, F32), pltpu.VMEM(squares.shape, F32)] if last else [],
        kept=kept,
    )(
        core,
        a,
        b,
        scale,
        in_vmem(parts[0]),
        in_vmem(parts[1]),
        in_vmem(base),
        near,
        far,
        in_vmem(held[0]) if started else after,
        held[1] if started else after,
        after,
    )


def base_kernel(core_ref, gram_ref, other_ref, b_ref, after_ref, *refs):
    out_ref, scale_ref = refs[-2:]
    hessian = (gram_ref[...] + other_ref[...]) * gram(b_ref[...])
    scale = inverse_norm(hessian)
    hessian = hessian * scale
    scale_ref[...] = jnp.broadcast_to(scale, scale_ref.shape)
    done = 0
    for c_ref in refs[:-2]:
        for start in range(0, c_ref.shape[0], PAIR):
            c = c_ref[start : start + PAIR]
            out_ref[done : done + PAIR] = c - dot(c, hessian)
            done += PAIR


def mass_base(core, gram_a, gram_a_other, b, pieces, after, kept):
    rank = b.shape[1]
    square = whole((rank, rank))
    scale = shaped(8, rank)
    bins = sum(piece.shape[0] for piece in pieces)
    return call(
        base_kernel,
        "mass_base",
        (1,),
        [square, square, whole(b.shape), NOWHERE] + [HELD for _ in pieces],
        [HELD, whole(scale.shape)],
        (pltpu.VMEM((bins, rank), F32), scale),
        kept=kept,
    )(core, gram_a, gram_a_other, b, after, *(in_vmem(piece) for piece in pieces))


def last_kernel(start, core_ref, scale_ref, base_ref, near_ref, far_ref, *refs):
    place = pl.ds(pl.multiple_of((start + pl.program_id(0)) * UNIT, UNIT), UNIT)
    refs[-1][...] = base_ref[place] + (near_ref[...] + far_ref[...]) * scale_ref[:1, :1]


def last_step(core, scale, base, near, far, after, start):
    rank = base.shape[1]
    side = rows_block(UNIT, rank)
    return call(
        functools.partial(last_kernel, start),
        "last_step",
        (near.shape[0] // UNIT,),
        [whole(scale.shape), HELD, side, side] + [NOWHERE for _ in after],
        side,
        shaped(*near.shape),
    )(core, scale, in_vmem(base), near, far, *after)


def join_kernel(core_ref, mine_ref, theirs_ref, held_ref, after_ref, out_ref, done_ref):
    done_ref[...] = jnp.zeros_like(done_ref)

    @pl.when(pl.program_id(0) == 0)
    def _():
        out_ref[...] = mine_ref[...]

    @pl.when(pl.program_id(0) == 1)
    def _():
        out_ref[...] = theirs_ref[...]


def join(core, mine, theirs, held, after, chunk, bins):
    rows, rank = mine.shape
    chunks = bins // (2 * rows)
    first = held is None

    def place(side, core_ref):
        return jnp.where(side == 0, core_ref[0], 1 - core_ref[0]) * chunks + chunk, 0

    return call(
        join_kernel,
        "join",
        (2,),
        [whole(mine.shape), whole(mine.shape), NOWHERE, NOWHERE],
        [pl.BlockSpec((rows, rank), place), whole((8, 128))],
        (shaped(bins, rank), shaped(8, 128)),
        (),
        {} if first else {3: 0},
    )(core, mine, theirs, mine if first else held, after)


def sample_gram_kernel(core_ref, a_ref, far_ref, after_ref, out_ref):
    out_ref[...] = gram(a_ref[...]) + gram(far_ref[...])


def sample_gram(core, a, far, after, kept):
    rank = a.shape[1]
    return call(
        sample_gram_kernel,
        "sample_gram",
        (1,),
        [whole(a.shape), whole(a.shape), NOWHERE],
        whole((rank, rank)),
        shaped(rank, rank),
        kept=kept,
    )(core, a, far, after)


def small_step_kernel(
    core_ref,
    a_ref,
    b_ref,
    gram_a_ref,
    gram_a_other_ref,
    gram_c_ref,
    gram_c_other_ref,
    drive_ref,
    drive_other_ref,
    drive_b_ref,
    drive_b_far_ref,
    after_ref,
    new_a_ref,
    new_b_ref,
    *refs,
):
    a, b = a_ref[...], b_ref[...]
    gram_a = gram_a_ref[...] + gram_a_other_ref[...]
    at_zero = core_ref[0] == 0
    mine, other = gram_c_ref[...], gram_c_other_ref[...]
    gram_c = jnp.concatenate([jnp.where(at_zero, mine, other), jnp.where(at_zero, other, mine)], 0)
    hessian_a = gram(b) * gram_c
    hessian_b = gram_a * gram_c
    drive_a = jnp.concatenate([drive_ref[...], drive_other_ref[...]], 0)
    drive_b = drive_b_ref[...] + drive_b_far_ref[...]
    new_a = a - (dot(a, hessian_a) - drive_a) * inverse_norm(hessian_a)
    new_b = b - (dot(b, hessian_b) - drive_b) * inverse_norm(hessian_b)
    new_a_ref[...] = new_a[: new_a_ref.shape[0]]
    new_b_ref[...] = new_b
    if refs:
        fill_khatri_rao(refs[0], new_a, new_b)


def small_step(core, a, b, args, after, kept, last):
    rows = a.shape[0] // 2 if last else a.shape[0]
    outs = [shaped(rows, a.shape[1]), shaped(*b.shape)]
    specs = [whole(outs[0].shape), whole(b.shape)]
    if not last:
        outs.append(pltpu.VMEM((2 * a.shape[1], a.shape[0] * b.shape[0]), BF16))
        specs.append(HELD)
    return call(
        small_step_kernel,
        "small_step",
        (1,),
        [whole(v.shape) for v in (a, b, *args)] + [NOWHERE],
        specs,
        outs,
        kept=kept,
    )(core, a, b, *args, after)


def swap(value, axis, size, distance):
    return lax.ppermute(value, axis, [(i, i ^ distance) for i in range(size)])


def local(mz, intensities, sample_start, scan_start, mass_start):
    b, c = scan_start, mass_start
    bins, rank = c.shape
    rows, scans = sample_start.shape[0], b.shape[0]
    x = intensities.reshape(-1, bins)
    number = lax.axis_index("grp") % 2
    core = number.reshape(1).astype(jnp.int32)

    def over_core(value):
        return swap(value, "grp", 4, 1)

    def over_x(value):
        return swap(value, "grp", 4, 2)

    def sum_mz(value, first, befores, kept, done=0):
        values = []
        distances = [1 << i for i in range(mz.bit_length() - 1)]
        place = distances.index(first)
        for distance in (distances[place:] + distances[:place])[: len(distances) - done]:
            far = swap(value, "mz", mz, distance)
            after, *befores = befores or [None]
            value = value + far if after is None else add(core, value, far, (after,), kept)
            values.append(value)
        return value, values[0]

    def close(keep, send, before, befores, kept):
        total = add(core, keep, over_core(send), before, kept)
        gram_c, _ = sum_mz(total[rows + scans :], mz // 2, [], kept)
        drive, early = sum_mz(total[: rows + scans], 1, befores, kept)
        drive, drive_b = drive[:rows], drive[rows:]
        return (gram_c, over_core(gram_c), drive, over_core(drive), drive_b, over_x(drive_b)), early

    def grams(a, far, after, kept):
        part = sample_gram(core, a[:rows], far, after, kept)
        return part, over_core(part)

    places = range(len(FIRST))
    others, after = [], x
    for place in places[:2]:
        after = give(core, x, after, place)
        others.append(over_core(after))
    a = jnp.concatenate([sample_start, over_core(sample_start)], 0)
    far_a = over_x(sample_start)

    parts, nears = [], [first_products(core, a, b, x, others[0], after)]
    kept = ()
    after = nears[0]
    for place in places[2:]:
        after = give(core, x, after, place)
        others.append(over_core(after))
    krt, held = None, None
    for place in places:
        high, low, *rest = load(
            core, a, b, x, others[place], c, krt, held, after, kept, place, place == places[-1], FIRST[place]
        )
        if FIRST[place]:
            after, *rest = rest
            nears.append(after)
        if krt is None:
            krt = rest.pop()
        held = rest
        parts.append((high, low))
        kept += (high, low)
        if place == places[-1]:
            gram_a = grams(a, far_a, held[0], kept)
            c_mine = lax.dynamic_slice_in_dim(c, number * (bins // 2), bins // 2, 0)
            base, scale = mass_base(core, *gram_a, b, [c_mine], after, kept)

    fars = [over_x(near) for near in nears]
    news, sums = [], None
    kept_base = kept + (base,)

    def drives(place, after):
        nonlocal sums
        new, *sums = drive_products(
            core,
            a,
            b,
            scale,
            parts[place],
            base,
            nears[place],
            fars[place],
            sums,
            after,
            kept,
            place,
            place == places[-1],
        )
        news.append(new)
        return new

    old_a = a
    after = held[0]
    for place in places[len(nears) :]:
        after = mass_products(core, krt, parts[place], after, kept_base, 0, 2)
        nears.append(after)
        fars.append(over_x(nears[-1]))
    befores = [drives(0, nears[-1]), drives(1, nears[-1]), fars[2]]
    small, _ = close(*held, (fars[0], gram_a[0]), befores, kept_base)
    new_a, new_b, krt = small_step(core, a, b, (*gram_a, *small), news[-1], kept_base, False)

    a, b = new_a, new_b
    lasts, after = [], a
    for place, start, units in LAST:
        near = mass_products(core, krt, parts[place], after, kept_base, start, units)
        after = near
        if not lasts:
            far = over_x(jnp.concatenate([near, a[:rows]], 0))
            far, far_a = far[: units * UNIT], far[units * UNIT :]
        else:
            far = over_x(near)
        lasts.append((2 * place + start, near, far))
    for place in places[2:]:
        drives(place, after)
    total = add(core, sums[0], over_core(sums[1]), (news[-1],), ())
    drive, gram_c = total[: rows + scans], total[rows + scans :]
    drive = drive + swap(drive, "mz", mz, 1)
    gram_a = grams(a, far_a, drive, ())
    base, scale = mass_base(core, *gram_a, b, news, drive, ())
    stages = [[], [], []]
    for i in range(1, mz.bit_length() - 1):
        drive = drive + swap(drive, "mz", mz, 1 << i)
        stages[min(i, 2) - 1].append(drive)
    for i, distance in enumerate([mz >> 1] + [1 << i for i in range(mz.bit_length() - 2)]):
        gram_c = gram_c + swap(gram_c, "mz", mz, distance)
        stages[min(i, 2)].append(gram_c)
    drive, drive_b = drive[:rows], drive[rows:]
    small = gram_c, over_core(gram_c), drive, over_core(drive), drive_b, over_x(drive_b)
    stages[2] += small
    afters = [(scale,)] + stages
    mines = []
    out = None
    for place, (start, near, far) in enumerate(lasts):
        after = tuple(afters[place]) if place < len(afters) else ()
        if place > 1:
            after += (mark,)
        mine = last_step(core, scale, base, near, far, after, start)
        mines.append((mine, over_core(mine)))
        if place:
            out, mark = join(core, *mines[place - 1], out, mine, place - 1, bins)
    new_a, new_b = small_step(core, a, b, (*gram_a, *small), mines[-1][0], (), True)
    out, mark = join(core, *mines[-1], out, new_b, len(lasts) - 1, bins)
    return new_a, new_b, out


def solution(mesh):
    placed = (P("grp", None, "mz"), P("grp", None), P(), P("mz", None))
    return jax.shard_map(
        functools.partial(local, mesh.shape["mz"]),
        mesh=mesh,
        in_specs=placed,
        out_specs=(P("grp", None), P(), P("mz", None)),
        check_vma=False,
    )
```

time: 501 us -> 136 us (0.27); the launches traced: 492 us -> 136 us
  waiting for transfers between devices: 264 us -> 23.2 us
  matrix products: 156 us -> 0 us
  Pallas kernels: 0 us -> 69.1 us
  starting transfers between devices: 0.78 us -> 41.8 us
  blocking collectives: 39.2 us -> 0 us
  between operations: 18.5 us -> 1.19 us
  local copies, waits for them, and re-layouts: 13.2 us -> 0.3 us
    psum x4 -> x0, waiting for transfers between devices: 264 us -> none  [the longest x2 187 us: local(): gram_a = lax.psum(gram_of(factor_a), 'grp')]
    dot_general x18 -> x0, matrix products: 156 us -> none  [the longest x2 57.8 us: local(): lax.dot_general(unfolded, khatri_rao, (((0,), (0,)), ((), ())), precision...]
    pallas_call x0 -> x37, Pallas kernels: none -> 69.1 us  [call(): return lambda *args: run(*args, *(in_vmem(value) for value in kept))]
    ppermute x0 -> x40, starting transfers between devices: none -> 41.8 us  [swap(): return lax.ppermute(value, axis, [(i, i ^ distance) for i in range(size)])]
    psum x1 -> x0, blocking collectives: 39.2 us -> none  [local(): lax.psum(jnp.einsum('ijr,ir->jr', contracted, factor_a, precision=precise...]
    ppermute x0 -> x40, waiting for transfers between devices: none -> 23.2 us  [swap(): return lax.ppermute(value, axis, [(i, i ^ distance) for i in range(size)])]
    unnamed x22 -> x11, local copies, waits for them, and re-layouts: 12.2 us -> 0.03 us
  transfers between devices with their start and end apart: 4 -> 40, of which waited for: 4 -> 10; matrix products, arithmetic and copies ran while one was open for 13% -> 0% of each run, Pallas kernels for 0% -> 49%
where the time goes in v2:
time: 136 us
  Pallas kernels  69.1 us (51%)
  starting transfers between devices  41.8 us (31%)
  waiting for transfers between devices  23.2 us (17%)
    pallas_call x37, Pallas kernels, call(): return lambda *args: run(*args, *(in_vmem(value) for value in kept))  69.1 us
    ppermute x40, starting transfers between devices, swap(): return lax.ppermute(value, axis, [(i, i ^ distance) for i in range(size)])  41.8 us
    ppermute x40, waiting for transfers between devices, swap(): return lax.ppermute(value, axis, [(i, i ^ distance) for i in range(size)])  23.2 us
  transfers between devices with their start and end apart: 40, of which 10 were waited for; matrix products, arithmetic and copies ran while one was open for 0% of the time, Pallas kernels for 49%

profile of v2, /device:TPU:1, one launch (start us, length us, event | category | flops | bytes accessed | tf_op | source)
XLA Modules:
  0.0 135.8 jit_solution(15238888125505555682)
XLA Ops:
  0.7 1.6 %give.4.after_ref = f32[1024,512]{1,0:T(8,128)S(1)} custom-call(s32[1]{0:T(128)} %bitcast.core_ref, f32[1024,4096]{1,0:T(8,128)} %bitcast.2, f32[1024,4096]{1,0:T(8,128)} %bitcast.3), custom_call_target="tpu_custom_call" | custom-call | tf_op jit(solution)/shard_map/give/pallas_call | solution.py:89
  2.4 0.5 collective-permute-start
  2.9 2.9 %give.5.after_ref = f32[1024,512]{1,0:T(8,128)} custom-call(s32[1]{0:T(128)} %bitcast.core_ref, f32[1024,4096]{1,0:T(8,128)} %bitcast.4, f32[1024,512]{1,0:T(8,128)S(1)} %give.4.after_ref), custom_call_target="tpu_custom_call" | custom-call | tf_op jit(solution)/shard_map/give/pallas_call | solution.py:89
  6.0 0.7 collective-permute-done
  6.8 4.4 %first_products.1.after_ref.refs_6_ = f32[512,256]{1,0:T(8,128)S(1)} custom-call(s32[1]{0:T(128)} %bitcast.core_ref, f32[256,256]{1,0:T(8,128)S(1)} %constant_dynamic-update-slice_fusion.a_ref.refs_0_, f32[8,256]{1,0:T(8,128)S(1)} %copy-done.1, f32[1024,4096]{1,0:T(8,128)} %bitcast.5, f32[1024,512]{1,0:T(8,128)S(1)} %collective-permute-done.2.other_ref, ...), custom_call_target="tpu_custom_call" | custom-call | tf_op jit(solution)/shard_map/first_products/pallas_call | solution.py:89
  11.2 3.0 %give.6.after_ref = f32[1024,512]{1,0:T(8,128)} custom-call(s32[1]{0:T(128)} %bitcast.core_ref, f32[1024,4096]{1,0:T(8,128)} %bitcast.6, f32[512,256]{1,0:T(8,128)S(1)} %first_products.1.after_ref.refs_6_), custom_call_target="tpu_custom_call" | custom-call | tf_op jit(solution)/shard_map/give/pallas_call | solution.py:89
  14.4 1.6 %give.7.krt_in_ref.total_in_ref.gram_in_ref.after_ref.refs_8_ = f32[1024,512]{1,0:T(8,128)S(1)} custom-call(s32[1]{0:T(128)} %bitcast.core_ref, f32[1024,4096]{1,0:T(8,128)} %bitcast.7, f32[1024,512]{1,0:T(8,128)} %give.6.after_ref), custom_call_target="tpu_custom_call" | custom-call | tf_op jit(solution)/shard_map/give/pallas_call | solution.py:89
  16.0 0.4 collective-permute-start.3
  16.4 2.3 %collective-permute-start.8 = (f32[512,256]{1,0:T(8,128)S(1)}, f32[512,256]{1,0:T(8,128)S(1)}, u32[]{:S(2)}, u32[]{:S(2)}) collective-permute-start(f32[512,256]{1,0:T(8,128)S(1)} %first_products.1.after_ref.refs_6_), channel_id=1, source_target_pairs={{0,16},{8,24},{16,0},{24,8},{1,17},{9,25},{17,1},{25,9},{2,18},{10... | collective-permute-start | bytes 1572872 | tf_op jit(solution)/shard_map/ppermute | solution.py:516
  18.8 4.7 %load.4 = (bf16[1,2048,512]{2,1,0:T(8,128)(2,1)S(1)}, bf16[1,2048,512]{2,1,0:T(8,128)(2,1)S(1)}, f32[2048,256]{1,0:T(8,128)S(1)}, f32[256,256]{1,0:T(8,128)S(1)}, bf16[512,2048]{1,0:T(8,128)(2,1)S(1)}) custom-call(s32[1]{0:T(128)} %bitcast.core_ref, f32[256,256]{1,0:T(8,128)S(1)} %constant_dynamic-update-slice_fusion.a_ref.refs_0_, f32[8,256]{1,0:T(8,128)S(1)} %copy-done.1, ...), custom_call_target="tpu_custom_call" | custom-call | tf_op jit(solution)/shard_map/load/pallas_call | solution.py:89
  23.5 6.1 %load.5 = (bf16[1,2048,512]{2,1,0:T(8,128)(2,1)S(1)}, bf16[1,2048,512]{2,1,0:T(8,128)(2,1)S(1)}, f32[512,256]{1,0:T(8,128)S(1)}, f32[2048,256]{1,0:T(8,128)S(1)}, f32[256,256]{1,0:T(8,128)S(1)}) custom-call(s32[1]{0:T(128)} %bitcast.core_ref, f32[256,256]{1,0:T(8,128)S(1)} %constant_dynamic-update-slice_fusion.a_ref.refs_0_, f32[8,256]{1,0:T(8,128)S(1)} %copy-done.1, ...), custom_call_target="tpu_custom_call" | custom-call | tf_op jit(solution)/shard_map/load/pallas_call | solution.py:89
  29.6 1.5 %collective-permute-start.15 = (f32[512,256]{1,0:T(8,128)S(1)}, f32[512,256]{1,0:T(8,128)S(1)}, u32[]{:S(2)}, u32[]{:S(2)}) collective-permute-start(f32[512,256]{1,0:T(8,128)S(1)} %get-tuple-element.56.refs_8_.refs_6_), channel_id=1, source_target_pairs={{0,16},{8,24},{16,0},{24,8},{1,17},{9,25},{17,1},{25,9},{2,18},{10... | collective-permute-start | bytes 1572872 | tf_op jit(solution)/shard_map/ppermute | solution.py:516
  31.1 6.3 %load.6 = (bf16[1,2048,512]{2,1,0:T(8,128)(2,1)S(1)}, bf16[1,2048,512]{2,1,0:T(8,128)(2,1)S(1)}, f32[512,256]{1,0:T(8,128)S(1)}, f32[2048,256]{1,0:T(8,128)S(1)}, f32[256,256]{1,0:T(8,128)S(1)}) custom-call(s32[1]{0:T(128)} %bitcast.core_ref, f32[256,256]{1,0:T(8,128)S(1)} %constant_dynamic-update-slice_fusion.a_ref.refs_0_, f32[8,256]{1,0:T(8,128)S(1)} %copy-done.1, ...), custom_call_target="tpu_custom_call" | custom-call | tf_op jit(solution)/shard_map/load/pallas_call | solution.py:89
  37.4 5.2 %load.7 = (bf16[1,2048,512]{2,1,0:T(8,128)(2,1)S(1)}, bf16[1,2048,512]{2,1,0:T(8,128)(2,1)S(1)}, f32[264,256]{1,0:T(8,128)S(1)}, f32[264,256]{1,0:T(8,128)S(1)}) custom-call(s32[1]{0:T(128)} %bitcast.core_ref, f32[256,256]{1,0:T(8,128)S(1)} %constant_dynamic-update-slice_fusion.a_ref.refs_0_, f32[8,256]{1,0:T(8,128)S(1)} %copy-done.1, ...), custom_call_target="tpu_custom_call" | custom-call | tf_op jit(solution)/shard_map/load/pallas_call | solution.py:89
  42.6 1.5 %sample_gram.2.refs_0_.refs_3_.refs_2_ = f32[256,256]{1,0:T(8,128)S(1)} custom-call(s32[1]{0:T(128)} %bitcast.core_ref, f32[128,256]{1,0:T(8,128)S(1)} %copy-done.2, f32[128,256]{1,0:T(8,128)} %collective-permute-done.1.refs_1_, f32[264,256]{1,0:T(8,128)S(1)} %get-tuple-element.64.refs_2_.refs_0_.refs_3_, ...), custom_call_target="tpu_custom_call" | custom-call | tf_op jit(solution)/shard_map/sample_gram/pallas_call | solution.py:89
  44.1 1.3 collective-permute-start.6
  45.6 0.9 collective-permute-done.6.refs_1_.refs_3_
  46.5 1.6 %mass_base.2 = (f32[2048,256]{1,0:T(8,128)S(1)}, f32[8,256]{1,0:T(8,128)S(1)}) custom-call(s32[1]{0:T(128)} %bitcast.core_ref, f32[256,256]{1,0:T(8,128)S(1)} %sample_gram.2.refs_0_.refs_3_.refs_2_, f32[256,256]{1,0:T(8,128)S(1)} %collective-permute-done.6.refs_1_.refs_3_, f32[8,256]{1,0:T(8,128)S(1)} %copy-done.1, ...), custom_call_target="tpu_custom_call" | custom-call | tf_op jit(solution)/shard_map/mass_base/pallas_call | solution.py:89
  48.2 1.3 collective-permute-start.13
  49.6 2.4 %collective-permute-start.9 = (f32[128,256]{1,0:T(8,128)S(1)}, f32[128,256]{1,0:T(8,128)S(1)}, u32[]{:S(2)}, u32[]{:S(2)}) collective-permute-start(f32[128,256]{1,0:T(8,128)S(1)} %slice.45), channel_id=1, source_target_pairs={{0,4},{1,5},{2,6},{3,7},{4,0},{5,1},{6,2},{7,3},{8,12},{9,13},{10,... | collective-permute-start | bytes 393224 | tf_op jit(solution)/shard_map/ppermute | solution.py:516
  52.2 2.1 %mass_products.5.refs_8_.refs_9_.refs_10_.refs_6_ = f32[512,256]{1,0:T(8,128)S(1)} custom-call(s32[1]{0:T(128)} %bitcast.core_ref, bf16[512,2048]{1,0:T(8,128)(2,1)S(1)} %get-tuple-element.49.refs_5_.refs_0_, bf16[1,2048,512]{2,1,0:T(8,128)(2,1)S(1)} %get-tuple-element.65.refs_9_.refs_11_.refs_10_.refs_1_.refs_17_.refs_3_, ...), custom_call_target="tpu_custom_call" | custom-call | tf_op jit(solution)/shard_map/mass_products/pallas_call | solution.py:89
  54.3 2.2 %drive_products.4 = (f32[512,256]{1,0:T(8,128)S(1)}, f32[2048,256]{1,0:T(8,128)S(1)}, f32[256,256]{1,0:T(8,128)S(1)}) custom-call(s32[1]{0:T(128)} %bitcast.core_ref, f32[256,256]{1,0:T(8,128)S(1)} %constant_dynamic-update-slice_fusion.a_ref.refs_0_, f32[8,256]{1,0:T(8,128)S(1)} %copy-done.1, f32[8,256]{1,0:T(8,128)S(1)} %get-tuple-element.69.refs_2_, ...), custom_call_target="tpu_custom_call" | custom-call | tf_op jit(solution)/shard_map/drive_products/pallas_call | solution.py:89
  56.6 1.3 collective-permute-start.14
  58.2 1.2 collective-permute-start.21
  59.5 2.3 %drive_products.5 = (f32[512,256]{1,0:T(8,128)S(1)}, f32[2048,256]{1,0:T(8,128)S(1)}, f32[256,256]{1,0:T(8,128)S(1)}) custom-call(s32[1]{0:T(128)} %bitcast.core_ref, f32[256,256]{1,0:T(8,128)S(1)} %constant_dynamic-update-slice_fusion.a_ref.refs_0_, f32[8,256]{1,0:T(8,128)S(1)} %copy-done.1, f32[8,256]{1,0:T(8,128)S(1)} %get-tuple-element.69.refs_2_, ...), custom_call_target="tpu_custom_call" | custom-call | tf_op jit(solution)/shard_map/drive_products/pallas_call | solution.py:89
  61.8 1.3 collective-permute-start.16
  63.2 2.3 %collective-permute-start.11 = (f32[128,256]{1,0:T(8,128)S(1)}, f32[128,256]{1,0:T(8,128)S(1)}, u32[]{:S(2)}, u32[]{:S(2)}) collective-permute-start(f32[128,256]{1,0:T(8,128)S(1)} %add.42), channel_id=1, source_target_pairs={{0,2},{1,3},{2,0},{3,1},{4,6},{5,7},{6,4},{7,5},{8,10},{9,11},{10,... | collective-permute-start | bytes 393224 | tf_op jit(solution)/shard_map/ppermute | solution.py:516
  65.4 3.0 %collective-permute-done.11 = f32[128,256]{1,0:T(8,128)S(1)} collective-permute-done((f32[128,256]{1,0:T(8,128)S(1)}, f32[128,256]{1,0:T(8,128)S(1)}, u32[]{:S(2)}, u32[]{:S(2)}) %collective-permute-start.11) | collective-permute-done | bytes 131104 | tf_op jit(solution)/shard_map/ppermute | solution.py:516
  68.5 3.5 %collective-permute-start.12 = (f32[128,256]{1,0:T(8,128)S(1)}, f32[128,256]{1,0:T(8,128)S(1)}, u32[]{:S(2)}, u32[]{:S(2)}) collective-permute-start(f32[128,256]{1,0:T(8,128)S(1)} %add.43.refs_4_), channel_id=1, source_target_pairs={{0,8},{8,0},{16,24},{24,16},{1,9},{9,1},{17,25},{25,17},{2,10},{10... | collective-permute-start | bytes 393224 | tf_op jit(solution)/shard_map/ppermute | solution.py:516
  72.2 0.6 collective-permute-start.19
  72.8 3.1 %collective-permute-done.19.refs_9_ = f32[8,256]{1,0:T(8,128)S(1)} collective-permute-done((f32[8,256]{1,0:T(8,128)S(1)}, f32[8,256]{1,0:T(8,128)S(1)}, u32[]{:S(2)}, u32[]{:S(2)}) %collective-permute-start.19) | collective-permute-done | bytes 8224 | tf_op jit(solution)/shard_map/ppermute | solution.py:516
  75.9 1.3 small_step.2
  77.2 2.1 %mass_products.6.refs_3_.near_ref = f32[512,256]{1,0:T(8,128)S(1)} custom-call(s32[1]{0:T(128)} %bitcast.core_ref, bf16[512,2048]{1,0:T(8,128)(2,1)S(1)} %get-tuple-element.76.refs_0_, bf16[1,2048,512]{2,1,0:T(8,128)(2,1)S(1)} %get-tuple-element.52.refs_9_.refs_3_.refs_5_.refs_4_.refs_11_.refs_1_, ...), custom_call_target="tpu_custom_call" | custom-call | tf_op jit(solution)/shard_map/mass_products/pallas_call | solution.py:89
  79.7 2.1 %mass_products.7.refs_3_.near_ref = f32[512,256]{1,0:T(8,128)S(1)} custom-call(s32[1]{0:T(128)} %bitcast.core_ref, bf16[512,2048]{1,0:T(8,128)(2,1)S(1)} %get-tuple-element.76.refs_0_, bf16[1,2048,512]{2,1,0:T(8,128)(2,1)S(1)} %get-tuple-element.57.refs_11_.refs_5_.refs_7_.refs_6_.refs_13_.refs_3_.refs_1_, ...), custom_call_target="tpu_custom_call" | custom-call | tf_op jit(solution)/shard_map/mass_products/pallas_call | solution.py:89
  81.8 2.1 %mass_products.8.refs_3_.near_ref = f32[512,256]{1,0:T(8,128)S(1)} custom-call(s32[1]{0:T(128)} %bitcast.core_ref, bf16[512,2048]{1,0:T(8,128)(2,1)S(1)} %get-tuple-element.76.refs_0_, bf16[1,2048,512]{2,1,0:T(8,128)(2,1)S(1)} %get-tuple-element.62.refs_13_.refs_7_.refs_9_.refs_8_.refs_15_.refs_1_.refs_3_, ...), custom_call_target="tpu_custom_call" | custom-call | tf_op jit(solution)/shard_map/mass_products/pallas_call | solution.py:89
  84.0 2.4 %mass_products.9.refs_10_.near_ref = f32[512,256]{1,0:T(8,128)S(1)} custom-call(s32[1]{0:T(128)} %bitcast.core_ref, bf16[512,2048]{1,0:T(8,128)(2,1)S(1)} %get-tuple-element.76.refs_0_, bf16[1,2048,512]{2,1,0:T(8,128)(2,1)S(1)} %get-tuple-element.65.refs_9_.refs_11_.refs_10_.refs_1_.refs_17_.refs_3_, ...), custom_call_target="tpu_custom_call" | custom-call | tf_op jit(solution)/shard_map/mass_products/pallas_call | solution.py:89
  86.4 2.3 %drive_products.6 = (f32[512,256]{1,0:T(8,128)S(1)}, f32[2048,256]{1,0:T(8,128)S(1)}, f32[256,256]{1,0:T(8,128)S(1)}) custom-call(s32[1]{0:T(128)} %bitcast.core_ref, f32[256,256]{1,0:T(8,128)S(1)} %get-tuple-element.74.refs_3_.refs_0_.a_ref, f32[8,256]{1,0:T(8,128)S(1)} %get-tuple-element.75.refs_1_.b_ref, f32[8,256]{1,0:T(8,128)S(1)} %get-tuple-element.69.refs_2_, ...), custom_call_target="tpu_custom_call" | custom-call | tf_op jit(solution)/shard_map/drive_products/pallas_call | solution.py:89
  88.7 2.8 %drive_products.7 = (f32[512,256]{1,0:T(8,128)S(1)}, f32[264,256]{1,0:T(8,128)S(1)}, f32[264,256]{1,0:T(8,128)S(1)}) custom-call(s32[1]{0:T(128)} %bitcast.core_ref, f32[256,256]{1,0:T(8,128)S(1)} %get-tuple-element.74.refs_3_.refs_0_.a_ref, f32[8,256]{1,0:T(8,128)S(1)} %get-tuple-element.75.refs_1_.b_ref, f32[8,256]{1,0:T(8,128)S(1)} %get-tuple-element.69.refs_2_, ...), custom_call_target="tpu_custom_call" | custom-call | tf_op jit(solution)/shard_map/drive_products/pallas_call | solution.py:89
  91.4 2.2 %collective-permute-start.22 = (f32[264,256]{1,0:T(8,128)S(1)}, f32[264,256]{1,0:T(8,128)S(1)}, u32[]{:S(2)}, u32[]{:S(2)}) collective-permute-start(f32[264,256]{1,0:T(8,128)S(1)} %get-tuple-element.82), channel_id=1, source_target_pairs={{0,8},{8,0},{16,24},{24,16},{1,9},{9,1},{17,25},{25,17},{2,10},{10... | collective-permute-start | bytes 811016 | tf_op jit(solution)/shard_map/ppermute | solution.py:516
  93.6 1.2 collective-permute-done.22.far_ref
  95.1 1.3 collective-permute-start.34
  96.8 3.0 %collective-permute-done.23 = f32[136,256]{1,0:T(8,128)S(1)} collective-permute-done((f32[136,256]{1,0:T(8,128)S(1)}, f32[136,256]{1,0:T(8,128)S(1)}, u32[]{:S(2)}, u32[]{:S(2)}) %collective-permute-start.23) | collective-permute-done | bytes 139296 | tf_op jit(solution)/shard_map/ppermute | solution.py:516
  99.8 0.4 sample_gram.3.gram_ref.gram_a_ref
  100.3 1.3 collective-permute-start.24
  101.5 1.2 collective-permute-start.37
  102.8 1.3 collective-permute-start.29
  104.1 0.4 collective-permute-done.25
  104.5 1.3 collective-permute-start.26
  105.9 1.7 %mass_base.3 = (f32[2048,256]{1,0:T(8,128)S(1)}, f32[8,256]{1,0:T(8,128)S(1)}) custom-call(s32[1]{0:T(128)} %bitcast.core_ref, f32[256,256]{1,0:T(8,128)S(1)} %sample_gram.3.gram_ref.gram_a_ref, f32[256,256]{1,0:T(8,128)S(1)} %collective-permute-done.24.other_ref.gram_a_other_ref, f32[8,256]{1,0:T(8,128)S(1)} %get-tuple-element.75.refs_1_.b_ref, ...), custom_call_target="tpu_custom_call" | custom-call | tf_op jit(solution)/shard_map/mass_base/pallas_call | solution.py:89
  107.8 2.0 %collective-permute-start.36 = (f32[512,256]{1,0:T(8,128)S(1)}, f32[512,256]{1,0:T(8,128)S(1)}, u32[]{:S(2)}, u32[]{:S(2)}) collective-permute-start(f32[512,256]{1,0:T(8,128)S(1)} %last_step.5.mine_ref.held_ref), channel_id=1, source_target_pairs={{0,8},{8,0},{16,24},{24,16},{1,9},{9,1},{17,25},{25,17},{2,10},{10... | collective-permute-start | bytes 1572872 | tf_op jit(solution)/shard_map/ppermute | solution.py:516
  110.1 0.8 collective-permute-start.35
  110.9 1.3 collective-permute-start.33
  112.2 1.4 %collective-permute-start.27 = (f32[128,256]{1,0:T(8,128)S(1)}, f32[128,256]{1,0:T(8,128)S(1)}, u32[]{:S(2)}, u32[]{:S(2)}) collective-permute-start(f32[128,256]{1,0:T(8,128)S(1)} %add.46.refs_1_), channel_id=1, source_target_pairs={{0,2},{1,3},{2,0},{3,1},{4,6},{5,7},{6,4},{7,5},{8,10},{9,11},{10,... | collective-permute-start | bytes 393224 | tf_op jit(solution)/shard_map/ppermute | solution.py:516
  113.5 3.4 %collective-permute-done.27 = f32[128,256]{1,0:T(8,128)S(1)} collective-permute-done((f32[128,256]{1,0:T(8,128)S(1)}, f32[128,256]{1,0:T(8,128)S(1)}, u32[]{:S(2)}, u32[]{:S(2)}) %collective-permute-start.27) | collective-permute-done | bytes 131104 | tf_op jit(solution)/shard_map/ppermute | solution.py:516
  117.0 1.3 collective-permute-start.30
  118.3 7.0 %collective-permute-done.30 = f32[136,256]{1,0:T(8,128)S(1)} collective-permute-done((f32[136,256]{1,0:T(8,128)S(1)}, f32[136,256]{1,0:T(8,128)S(1)}, u32[]{:S(2)}, u32[]{:S(2)}) %collective-permute-start.30) | collective-permute-done | bytes 139296 | tf_op jit(solution)/shard_map/ppermute | solution.py:516
  125.4 1.6 %collective-permute-start.28 = (f32[128,256]{1,0:T(8,128)S(1)}, f32[128,256]{1,0:T(8,128)S(1)}, u32[]{:S(2)}, u32[]{:S(2)}) collective-permute-start(f32[128,256]{1,0:T(8,128)S(1)} %add.47.refs_0_.refs_1_.gram_c_ref), channel_id=1, source_target_pairs={{0,8},{8,0},{16,24},{24,16},{1,9},{9,1},{17,25},{25,17},{2,10},{10... | collective-permute-start | bytes 393224 | tf_op jit(solution)/shard_map/ppermute | solution.py:516
  127.4 1.0 join.4
  128.6 0.8 collective-permute-start.39
  129.4 1.0 join.5
  130.8 1.6 %collective-permute-start.38 = (f32[512,256]{1,0:T(8,128)S(1)}, f32[512,256]{1,0:T(8,128)S(1)}, u32[]{:S(2)}, u32[]{:S(2)}) collective-permute-start(f32[512,256]{1,0:T(8,128)S(1)} %last_step.7.after_ref.mine_ref), channel_id=1, source_target_pairs={{0,8},{8,0},{16,24},{24,16},{1,9},{9,1},{17,25},{25,17},{2,10},{10... | collective-permute-start | bytes 1572872 | tf_op jit(solution)/shard_map/ppermute | solution.py:516
  132.4 1.3 small_step.3
  133.7 1.0 join.6
  134.8 1.0 join.7
  (87 shorter events, 4.4 us)
Async XLA Ops:
  0.6 1.8 %copy-start.2 = (f32[128,256]{1,0:T(8,128)S(1)}, f32[128,256]{1,0:T(8,128)}, u32[]{:S(2)}) copy-start(f32[128,256]{1,0:T(8,128)} %refs_0_.1) | copy-start | bytes 393220
  2.3 4.5 %copy-start.1 = (f32[8,256]{1,0:T(8,128)S(1)}, f32[8,256]{1,0:T(8,128)}, u32[]{:S(2)}) copy-start(f32[8,256]{1,0:T(8,128)} %refs_1_.11) | copy-start | bytes 24580
  2.3 4.4 %collective-permute-start.2 = (f32[1024,512]{1,0:T(8,128)S(1)}, f32[1024,512]{1,0:T(8,128)S(1)}, u32[]{:S(2)}, u32[]{:S(2)}) collective-permute-start(f32[1024,512]{1,0:T(8,128)S(1)} %give.4.after_ref), channel_id=1, source_target_pairs={{0,8},{8,0},{16,24},{24,16},{1,9},{9,1},{17,25},{25,17},{2,10},{10... | collective-permute-start | bytes 6291464 | tf_op jit(solution)/shard_map/ppermute | solution.py:516
  2.4 4.3 %collective-permute-start = (f32[128,256]{1,0:T(8,128)S(1)}, f32[128,256]{1,0:T(8,128)S(1)}, u32[]{:S(2)}, u32[]{:S(2)}) collective-permute-start(f32[128,256]{1,0:T(8,128)S(1)} %copy-done.2), channel_id=1, source_target_pairs={{0,8},{8,0},{16,24},{24,16},{1,9},{9,1},{17,25},{25,17},{2,10},{10... | collective-permute-start | bytes 393224 | tf_op jit(solution)/shard_map/ppermute | solution.py:516
  5.8 17.7 %collective-permute-start.5 = (f32[1024,512]{1,0:T(8,128)}, f32[1024,512]{1,0:T(8,128)}, u32[]{:S(2)}, u32[]{:S(2)}) collective-permute-start(f32[1024,512]{1,0:T(8,128)} %give.5.after_ref), channel_id=1, source_target_pairs={{0,8},{8,0},{16,24},{24,16},{1,9},{9,1},{17,25},{25,17},{2,10},{10... | collective-permute-start | bytes 6291464 | tf_op jit(solution)/shard_map/ppermute | solution.py:516
  6.8 4.4 %copy-start = (f32[1024,512]{1,0:T(8,128)}, f32[1024,512]{1,0:T(8,128)S(1)}, u32[]{:S(2)}) copy-start(f32[1024,512]{1,0:T(8,128)S(1)} %collective-permute-done.2.other_ref) | copy-start | bytes 6291460
  14.2 16.9 %collective-permute-start.4 = (f32[1024,512]{1,0:T(8,128)}, f32[1024,512]{1,0:T(8,128)}, u32[]{:S(2)}, u32[]{:S(2)}) collective-permute-start(f32[1024,512]{1,0:T(8,128)} %give.6.after_ref), channel_id=1, source_target_pairs={{0,8},{8,0},{16,24},{24,16},{1,9},{9,1},{17,25},{25,17},{2,10},{10... | collective-permute-start | bytes 6291464 | tf_op jit(solution)/shard_map/ppermute | solution.py:516
  16.0 21.4 %collective-permute-start.3 = (f32[1024,512]{1,0:T(8,128)S(1)}, f32[1024,512]{1,0:T(8,128)}, u32[]{:S(2)}, u32[]{:S(2)}) collective-permute-start(f32[1024,512]{1,0:T(8,128)S(1)} %give.7.krt_in_ref.total_in_ref.gram_in_ref.after_ref.refs_8_), channel_id=1, source_target_pairs={{0,8},{8,0},{16,24},{24,16},{1,9},{9,1},{17,25},{25,17},{2,10},{10... | collective-permute-start | bytes 6291464 | tf_op jit(solution)/shard_map/ppermute | solution.py:516
  16.4 31.7 %collective-permute-start.8 = (f32[512,256]{1,0:T(8,128)S(1)}, f32[512,256]{1,0:T(8,128)S(1)}, u32[]{:S(2)}, u32[]{:S(2)}) collective-permute-start(f32[512,256]{1,0:T(8,128)S(1)} %first_products.1.after_ref.refs_6_), channel_id=1, source_target_pairs={{0,16},{8,24},{16,0},{24,8},{1,17},{9,25},{17,1},{25,9},{2,18},{10... | collective-permute-start | bytes 1572872 | tf_op jit(solution)/shard_map/ppermute | solution.py:516
  18.8 23.8 %collective-permute-start.1 = (f32[128,256]{1,0:T(8,128)S(1)}, f32[128,256]{1,0:T(8,128)}, u32[]{:S(2)}, u32[]{:S(2)}) collective-permute-start(f32[128,256]{1,0:T(8,128)S(1)} %copy-done.2), channel_id=1, source_target_pairs={{0,16},{8,24},{16,0},{24,8},{1,17},{9,25},{17,1},{25,9},{2,18},{10... | collective-permute-start | bytes 393224 | tf_op jit(solution)/shard_map/ppermute | solution.py:516
  29.6 29.9 %collective-permute-start.15 = (f32[512,256]{1,0:T(8,128)S(1)}, f32[512,256]{1,0:T(8,128)S(1)}, u32[]{:S(2)}, u32[]{:S(2)}) collective-permute-start(f32[512,256]{1,0:T(8,128)S(1)} %get-tuple-element.56.refs_8_.refs_6_), channel_id=1, source_target_pairs={{0,16},{8,24},{16,0},{24,8},{1,17},{9,25},{17,1},{25,9},{2,18},{10... | collective-permute-start | bytes 1572872 | tf_op jit(solution)/shard_map/ppermute | solution.py:516
  42.6 2.9 %copy-start.4 = (f32[4096,256]{1,0:T(8,128)S(1)}, f32[4096,256]{1,0:T(8,128)}, u32[]{:S(2)}) copy-start(f32[4096,256]{1,0:T(8,128)} %refs_4_.5) | copy-start | bytes 12582916
  44.1 2.4 %collective-permute-start.6 = (f32[256,256]{1,0:T(8,128)S(1)}, f32[256,256]{1,0:T(8,128)S(1)}, u32[]{:S(2)}, u32[]{:S(2)}) collective-permute-start(f32[256,256]{1,0:T(8,128)S(1)} %sample_gram.2.refs_0_.refs_3_.refs_2_), channel_id=1, source_target_pairs={{0,8},{8,0},{16,24},{24,16},{1,9},{9,1},{17,25},{25,17},{2,10},{10... | collective-permute-start | bytes 786440 | tf_op jit(solution)/shard_map/ppermute | solution.py:516
  45.3 2.8 %collective-permute-start.7 = (f32[264,256]{1,0:T(8,128)S(1)}, f32[264,256]{1,0:T(8,128)S(1)}, u32[]{:S(2)}, u32[]{:S(2)}) collective-permute-start(f32[264,256]{1,0:T(8,128)S(1)} %get-tuple-element.67), channel_id=1, source_target_pairs={{0,8},{8,0},{16,24},{24,16},{1,9},{9,1},{17,25},{25,17},{2,10},{10... | collective-permute-start | bytes 811016 | tf_op jit(solution)/shard_map/ppermute | solution.py:516
  48.2 8.3 %collective-permute-start.13 = (f32[136,256]{1,0:T(8,128)S(1)}, f32[136,256]{1,0:T(8,128)S(1)}, u32[]{:S(2)}, u32[]{:S(2)}) collective-permute-start(f32[136,256]{1,0:T(8,128)S(1)} %slice.46.refs_0_), channel_id=1, source_target_pairs={{0,1},{1,0},{2,3},{3,2},{4,5},{5,4},{6,7},{7,6},{8,9},{9,8},{10,11... | collective-permute-start | bytes 417800 | tf_op jit(solution)/shard_map/ppermute | solution.py:516
  49.6 8.3 %collective-permute-start.9 = (f32[128,256]{1,0:T(8,128)S(1)}, f32[128,256]{1,0:T(8,128)S(1)}, u32[]{:S(2)}, u32[]{:S(2)}) collective-permute-start(f32[128,256]{1,0:T(8,128)S(1)} %slice.45), channel_id=1, source_target_pairs={{0,4},{1,5},{2,6},{3,7},{4,0},{5,1},{6,2},{7,3},{8,12},{9,13},{10,... | collective-permute-start | bytes 393224 | tf_op jit(solution)/shard_map/ppermute | solution.py:516
  52.0 20.1 %collective-permute-start.17 = (f32[512,256]{1,0:T(8,128)S(1)}, f32[512,256]{1,0:T(8,128)S(1)}, u32[]{:S(2)}, u32[]{:S(2)}) collective-permute-start(f32[512,256]{1,0:T(8,128)S(1)} %get-tuple-element.61.refs_8_.refs_3_.refs_6_), channel_id=1, source_target_pairs={{0,16},{8,24},{16,0},{24,8},{1,17},{9,25},{17,1},{25,9},{2,18},{10... | collective-permute-start | bytes 1572872 | tf_op jit(solution)/shard_map/ppermute | solution.py:516
  56.6 5.2 %collective-permute-start.14 = (f32[136,256]{1,0:T(8,128)S(1)}, f32[136,256]{1,0:T(8,128)S(1)}, u32[]{:S(2)}, u32[]{:S(2)}) collective-permute-start(f32[136,256]{1,0:T(8,128)S(1)} %add.54.refs_0_), channel_id=1, source_target_pairs={{0,2},{1,3},{2,0},{3,1},{4,6},{5,7},{6,4},{7,5},{8,10},{9,11},{10,... | collective-permute-start | bytes 417800 | tf_op jit(solution)/shard_map/ppermute | solution.py:516
  57.9 5.2 %collective-permute-start.10 = (f32[128,256]{1,0:T(8,128)S(1)}, f32[128,256]{1,0:T(8,128)S(1)}, u32[]{:S(2)}, u32[]{:S(2)}) collective-permute-start(f32[128,256]{1,0:T(8,128)S(1)} %slice_add_fusion.1), channel_id=1, source_target_pairs={{0,1},{1,0},{2,3},{3,2},{4,5},{5,4},{6,7},{7,6},{8,9},{9,8},{10,11... | collective-permute-start | bytes 393224 | tf_op jit(solution)/shard_map/ppermute | solution.py:516
  58.2 30.4 %collective-permute-start.21 = (f32[512,256]{1,0:T(8,128)S(1)}, f32[512,256]{1,0:T(8,128)S(1)}, u32[]{:S(2)}, u32[]{:S(2)}) collective-permute-start(f32[512,256]{1,0:T(8,128)S(1)} %mass_products.5.refs_8_.refs_9_.refs_10_.refs_6_), channel_id=1, source_target_pairs={{0,16},{8,24},{16,0},{24,8},{1,17},{9,25},{17,1},{25,9},{2,18},{10... | collective-permute-start | bytes 1572872 | tf_op jit(solution)/shard_map/ppermute | solution.py:516
  61.8 10.2 %collective-permute-start.16 = (f32[136,256]{1,0:T(8,128)S(1)}, f32[136,256]{1,0:T(8,128)S(1)}, u32[]{:S(2)}, u32[]{:S(2)}) collective-permute-start(f32[136,256]{1,0:T(8,128)S(1)} %add.55.refs_0_), channel_id=1, source_target_pairs={{0,4},{1,5},{2,6},{3,7},{4,0},{5,1},{6,2},{7,3},{8,12},{9,13},{10,... | collective-permute-start | bytes 417800 | tf_op jit(solution)/shard_map/ppermute | solution.py:516
  63.2 5.3 %collective-permute-start.11 = (f32[128,256]{1,0:T(8,128)S(1)}, f32[128,256]{1,0:T(8,128)S(1)}, u32[]{:S(2)}, u32[]{:S(2)}) collective-permute-start(f32[128,256]{1,0:T(8,128)S(1)} %add.42), channel_id=1, source_target_pairs={{0,2},{1,3},{2,0},{3,1},{4,6},{5,7},{6,4},{7,5},{8,10},{9,11},{10,... | collective-permute-start | bytes 393224 | tf_op jit(solution)/shard_map/ppermute | solution.py:516
  68.5 7.4 %collective-permute-start.12 = (f32[128,256]{1,0:T(8,128)S(1)}, f32[128,256]{1,0:T(8,128)S(1)}, u32[]{:S(2)}, u32[]{:S(2)}) collective-permute-start(f32[128,256]{1,0:T(8,128)S(1)} %add.43.refs_4_), channel_id=1, source_target_pairs={{0,8},{8,0},{16,24},{24,16},{1,9},{9,1},{17,25},{25,17},{2,10},{10... | collective-permute-start | bytes 393224 | tf_op jit(solution)/shard_map/ppermute | solution.py:516
  72.1 3.8 %collective-permute-start.18 = (f32[128,256]{1,0:T(8,128)S(1)}, f32[128,256]{1,0:T(8,128)S(1)}, u32[]{:S(2)}, u32[]{:S(2)}) collective-permute-start(f32[128,256]{1,0:T(8,128)S(1)} %slice.47.refs_6_), channel_id=1, source_target_pairs={{0,8},{8,0},{16,24},{24,16},{1,9},{9,1},{17,25},{25,17},{2,10},{10... | collective-permute-start | bytes 393224 | tf_op jit(solution)/shard_map/ppermute | solution.py:516
  72.2 3.7 %collective-permute-start.19 = (f32[8,256]{1,0:T(8,128)S(1)}, f32[8,256]{1,0:T(8,128)S(1)}, u32[]{:S(2)}, u32[]{:S(2)}) collective-permute-start(f32[8,256]{1,0:T(8,128)S(1)} %slice.48.refs_8_), channel_id=1, source_target_pairs={{0,16},{8,24},{16,0},{24,8},{1,17},{9,25},{17,1},{25,9},{2,18},{10... | collective-permute-start | bytes 24584 | tf_op jit(solution)/shard_map/ppermute | solution.py:516
  79.4 20.4 %collective-permute-start.20 = (f32[640,256]{1,0:T(8,128)S(1)}, f32[640,256]{1,0:T(8,128)S(1)}, u32[]{:S(2)}, u32[]{:S(2)}) collective-permute-start(f32[640,256]{1,0:T(8,128)S(1)} %pad_maximum_fusion), channel_id=1, source_target_pairs={{0,16},{8,24},{16,0},{24,8},{1,17},{9,25},{17,1},{25,9},{2,18},{10... | collective-permute-start | bytes 1966088 | tf_op jit(solution)/shard_map/ppermute | solution.py:516
  91.4 3.4 %collective-permute-start.22 = (f32[264,256]{1,0:T(8,128)S(1)}, f32[264,256]{1,0:T(8,128)S(1)}, u32[]{:S(2)}, u32[]{:S(2)}) collective-permute-start(f32[264,256]{1,0:T(8,128)S(1)} %get-tuple-element.82), channel_id=1, source_target_pairs={{0,8},{8,0},{16,24},{24,16},{1,9},{9,1},{17,25},{25,17},{2,10},{10... | collective-permute-start | bytes 811016 | tf_op jit(solution)/shard_map/ppermute | solution.py:516
  94.8 5.0 %collective-permute-start.23 = (f32[136,256]{1,0:T(8,128)S(1)}, f32[136,256]{1,0:T(8,128)S(1)}, u32[]{:S(2)}, u32[]{:S(2)}) collective-permute-start(f32[136,256]{1,0:T(8,128)S(1)} %slice.50), channel_id=1, source_target_pairs={{0,1},{1,0},{2,3},{3,2},{4,5},{5,4},{6,7},{7,6},{8,9},{9,8},{10,11... | collective-permute-start | bytes 417800 | tf_op jit(solution)/shard_map/ppermute | solution.py:516
  95.1 14.7 %collective-permute-start.34 = (f32[512,256]{1,0:T(8,128)S(1)}, f32[512,256]{1,0:T(8,128)S(1)}, u32[]{:S(2)}, u32[]{:S(2)}) collective-permute-start(f32[512,256]{1,0:T(8,128)S(1)} %mass_products.7.refs_3_.near_ref), channel_id=1, source_target_pairs={{0,16},{8,24},{16,0},{24,8},{1,17},{9,25},{17,1},{25,9},{2,18},{10... | collective-permute-start | bytes 1572872 | tf_op jit(solution)/shard_map/ppermute | solution.py:516
  96.4 8.1 %collective-permute-start.25 = (f32[128,256]{1,0:T(8,128)S(1)}, f32[128,256]{1,0:T(8,128)S(1)}, u32[]{:S(2)}, u32[]{:S(2)}) collective-permute-start(f32[128,256]{1,0:T(8,128)S(1)} %slice.51), channel_id=1, source_target_pairs={{0,4},{1,5},{2,6},{3,7},{4,0},{5,1},{6,2},{7,3},{8,12},{9,13},{10,... | collective-permute-start | bytes 393224 | tf_op jit(solution)/shard_map/ppermute | solution.py:516
  100.3 5.6 %collective-permute-start.24 = (f32[256,256]{1,0:T(8,128)S(1)}, f32[256,256]{1,0:T(8,128)S(1)}, u32[]{:S(2)}, u32[]{:S(2)}) collective-permute-start(f32[256,256]{1,0:T(8,128)S(1)} %sample_gram.3.gram_ref.gram_a_ref), channel_id=1, source_target_pairs={{0,8},{8,0},{16,24},{24,16},{1,9},{9,1},{17,25},{25,17},{2,10},{10... | collective-permute-start | bytes 786440 | tf_op jit(solution)/shard_map/ppermute | solution.py:516
  101.5 25.5 %collective-permute-start.37 = (f32[512,256]{1,0:T(8,128)S(1)}, f32[512,256]{1,0:T(8,128)S(1)}, u32[]{:S(2)}, u32[]{:S(2)}) collective-permute-start(f32[512,256]{1,0:T(8,128)S(1)} %mass_products.8.refs_3_.near_ref), channel_id=1, source_target_pairs={{0,16},{8,24},{16,0},{24,8},{1,17},{9,25},{17,1},{25,9},{2,18},{10... | collective-permute-start | bytes 1572872 | tf_op jit(solution)/shard_map/ppermute | solution.py:516
  102.8 7.0 %collective-permute-start.29 = (f32[136,256]{1,0:T(8,128)S(1)}, f32[136,256]{1,0:T(8,128)S(1)}, u32[]{:S(2)}, u32[]{:S(2)}) collective-permute-start(f32[136,256]{1,0:T(8,128)S(1)} %slice_add_fusion.2.after_ref), channel_id=1, source_target_pairs={{0,2},{1,3},{2,0},{3,1},{4,6},{5,7},{6,4},{7,5},{8,10},{9,11},{10,... | collective-permute-start | bytes 417800 | tf_op jit(solution)/shard_map/ppermute | solution.py:516
  104.5 7.6 %collective-permute-start.26 = (f32[128,256]{1,0:T(8,128)S(1)}, f32[128,256]{1,0:T(8,128)S(1)}, u32[]{:S(2)}, u32[]{:S(2)}) collective-permute-start(f32[128,256]{1,0:T(8,128)S(1)} %slice_add_fusion.refs_1_), channel_id=1, source_target_pairs={{0,1},{1,0},{2,3},{3,2},{4,5},{5,4},{6,7},{7,6},{8,9},{9,8},{10,11... | collective-permute-start | bytes 393224 | tf_op jit(solution)/shard_map/ppermute | solution.py:516
  107.8 19.3 %collective-permute-start.36 = (f32[512,256]{1,0:T(8,128)S(1)}, f32[512,256]{1,0:T(8,128)S(1)}, u32[]{:S(2)}, u32[]{:S(2)}) collective-permute-start(f32[512,256]{1,0:T(8,128)S(1)} %last_step.5.mine_ref.held_ref), channel_id=1, source_target_pairs={{0,8},{8,0},{16,24},{24,16},{1,9},{9,1},{17,25},{25,17},{2,10},{10... | collective-permute-start | bytes 1572872 | tf_op jit(solution)/shard_map/ppermute | solution.py:516
  110.1 18.5 %collective-permute-start.35 = (f32[512,256]{1,0:T(8,128)S(1)}, f32[512,256]{1,0:T(8,128)S(1)}, u32[]{:S(2)}, u32[]{:S(2)}) collective-permute-start(f32[512,256]{1,0:T(8,128)S(1)} %last_step.4.after_ref.mine_ref), channel_id=1, source_target_pairs={{0,8},{8,0},{16,24},{24,16},{1,9},{9,1},{17,25},{25,17},{2,10},{10... | collective-permute-start | bytes 1572872 | tf_op jit(solution)/shard_map/ppermute | solution.py:516
  110.9 19.5 %collective-permute-start.33 = (f32[512,256]{1,0:T(8,128)S(1)}, f32[512,256]{1,0:T(8,128)S(1)}, u32[]{:S(2)}, u32[]{:S(2)}) collective-permute-start(f32[512,256]{1,0:T(8,128)S(1)} %mass_products.9.refs_10_.near_ref), channel_id=1, source_target_pairs={{0,16},{8,24},{16,0},{24,8},{1,17},{9,25},{17,1},{25,9},{2,18},{10... | collective-permute-start | bytes 1572872 | tf_op jit(solution)/shard_map/ppermute | solution.py:516
  112.2 4.8 %collective-permute-start.27 = (f32[128,256]{1,0:T(8,128)S(1)}, f32[128,256]{1,0:T(8,128)S(1)}, u32[]{:S(2)}, u32[]{:S(2)}) collective-permute-start(f32[128,256]{1,0:T(8,128)S(1)} %add.46.refs_1_), channel_id=1, source_target_pairs={{0,2},{1,3},{2,0},{3,1},{4,6},{5,7},{6,4},{7,5},{8,10},{9,11},{10,... | collective-permute-start | bytes 393224 | tf_op jit(solution)/shard_map/ppermute | solution.py:516
  117.0 8.4 %collective-permute-start.30 = (f32[136,256]{1,0:T(8,128)S(1)}, f32[136,256]{1,0:T(8,128)S(1)}, u32[]{:S(2)}, u32[]{:S(2)}) collective-permute-start(f32[136,256]{1,0:T(8,128)S(1)} %add.48.refs_0_), channel_id=1, source_target_pairs={{0,4},{1,5},{2,6},{3,7},{4,0},{5,1},{6,2},{7,3},{8,12},{9,13},{10,... | collective-permute-start | bytes 417800 | tf_op jit(solution)/shard_map/ppermute | solution.py:516
  125.4 5.2 %collective-permute-start.28 = (f32[128,256]{1,0:T(8,128)S(1)}, f32[128,256]{1,0:T(8,128)S(1)}, u32[]{:S(2)}, u32[]{:S(2)}) collective-permute-start(f32[128,256]{1,0:T(8,128)S(1)} %add.47.refs_0_.refs_1_.gram_c_ref), channel_id=1, source_target_pairs={{0,8},{8,0},{16,24},{24,16},{1,9},{9,1},{17,25},{25,17},{2,10},{10... | collective-permute-start | bytes 393224 | tf_op jit(solution)/shard_map/ppermute | solution.py:516
  127.0 3.6 %collective-permute-start.31 = (f32[128,256]{1,0:T(8,128)S(1)}, f32[128,256]{1,0:T(8,128)S(1)}, u32[]{:S(2)}, u32[]{:S(2)}) collective-permute-start(f32[128,256]{1,0:T(8,128)S(1)} %slice.52.refs_3_.drive_ref), channel_id=1, source_target_pairs={{0,8},{8,0},{16,24},{24,16},{1,9},{9,1},{17,25},{25,17},{2,10},{10... | collective-permute-start | bytes 393224 | tf_op jit(solution)/shard_map/ppermute | solution.py:516
  127.1 3.5 %collective-permute-start.32 = (f32[8,256]{1,0:T(8,128)S(1)}, f32[8,256]{1,0:T(8,128)S(1)}, u32[]{:S(2)}, u32[]{:S(2)}) collective-permute-start(f32[8,256]{1,0:T(8,128)S(1)} %slice.53.refs_5_.drive_b_ref), channel_id=1, source_target_pairs={{0,16},{8,24},{16,0},{24,8},{1,17},{9,25},{17,1},{25,9},{2,18},{10... | collective-permute-start | bytes 24584 | tf_op jit(solution)/shard_map/ppermute | solution.py:516
  128.6 5.1 %collective-permute-start.39 = (f32[512,256]{1,0:T(8,128)S(1)}, f32[512,256]{1,0:T(8,128)S(1)}, u32[]{:S(2)}, u32[]{:S(2)}) collective-permute-start(f32[512,256]{1,0:T(8,128)S(1)} %last_step.6.after_ref.mine_ref), channel_id=1, source_target_pairs={{0,8},{8,0},{16,24},{24,16},{1,9},{9,1},{17,25},{25,17},{2,10},{10... | collective-permute-start | bytes 1572872 | tf_op jit(solution)/shard_map/ppermute | solution.py:516
  130.8 4.0 %collective-permute-start.38 = (f32[512,256]{1,0:T(8,128)S(1)}, f32[512,256]{1,0:T(8,128)S(1)}, u32[]{:S(2)}, u32[]{:S(2)}) collective-permute-start(f32[512,256]{1,0:T(8,128)S(1)} %last_step.7.after_ref.mine_ref), channel_id=1, source_target_pairs={{0,8},{8,0},{16,24},{24,16},{1,9},{9,1},{17,25},{25,17},{2,10},{10... | collective-permute-start | bytes 1572872 | tf_op jit(solution)/shard_map/ppermute | solution.py:516
  133.7 1.0 copy-start.3

commit v3 on v2

--- a/solution.py
+++ b/solution.py
@@ -245,18 +245,32 @@
     )
 
 
-def first_kernel(core_ref, a_ref, b_ref, x_ref, other_ref, after_ref, out_ref, krt_ref):
+def first_kernel(start, core_ref, a_ref, b_ref, x_ref, other_ref, source_ref, after_ref, out_ref, *refs):
+    *given, krt_ref, sems = refs
+    bins = source_ref.shape[1]
+    copies = []
+    for place, given_ref in enumerate(given):
+        column = (1 - core_ref[0]) * (bins // 2) + (start + place) * PAIR
+        columns = pl.ds(pl.multiple_of(column, PAIR), PAIR)
+        copies.append(
+            pltpu.make_async_copy(source_ref.at[:, columns], given_ref, sems.at[place])
+        )
+    for copy in copies:
+        copy.start()
     fill_khatri_rao(krt_ref, a_ref[...], b_ref[...])
     x_high, x_low = split(jnp.concatenate([x_ref[...], other_ref[...]], 0))
     out_ref[...] = mass_part(krt_ref, x_high, x_low)
-
-
-def first_products(core, a, b, x, other, after):
+    for copy in copies:
+        copy.wait()
+
+
+def first_products(core, a, b, x, other, after, start):
     rows, bins = x.shape
     rank = a.shape[1]
     blocks = bins // (2 * PAIR)
-    return call(
-        first_kernel,
+    given = len(FIRST) - start
+    return call(
+        functools.partial(first_kernel, start),
         "first_products",
         (1,),
         [
@@ -265,11 +279,12 @@
             pl.BlockSpec((rows, PAIR), lambda j, core_ref: (0, core_ref[0] * blocks)),
             whole(other.shape),
             NOWHERE,
+            NOWHERE,
         ],
-        whole((PAIR, rank)),
-        shaped(PAIR, rank),
-        [pltpu.VMEM((2 * rank, 2 * rows), BF16)],
-    )(core, a, b, in_hbm(x), other, after)
+        [whole((PAIR, rank))] + [HELD] * given,
+        [shaped(PAIR, rank)] + [pltpu.VMEM((rows, PAIR), F32)] * given,
+        [pltpu.VMEM((2 * rank, 2 * rows), BF16), pltpu.SemaphoreType.DMA((given,))],
+    )(core, a, b, in_hbm(x), other, in_hbm(x), after)
 
 
 def mass_kernel(start, core_ref, krt_ref, high_ref, low_ref, after_ref, out_ref):
@@ -560,12 +575,11 @@
     a = jnp.concatenate([sample_start, over_core(sample_start)], 0)
     far_a = over_x(sample_start)
 
-    parts, nears = [], [first_products(core, a, b, x, others[0], after)]
+    near, *given = first_products(core, a, b, x, others[0], after, len(others))
+    others += [over_core(value) for value in given]
+    parts, nears = [], [near]
     kept = ()
-    after = nears[0]
-    for place in places[2:]:
-        after = give(core, x, after, place)
-        others.append(over_core(after))
+    after = near
     krt, held = None, None
     for place in places:
         high, low, *rest = load(

time: 136 us -> 135 us (level)
  Pallas kernels: 69.1 us -> 66.4 us
  waiting for transfers between devices: 23.2 us -> 24.6 us
    pallas_call x37 -> x35, Pallas kernels: 69.1 us -> 66.4 us  [call(): return lambda *args: run(*args, *(in_vmem(value) for value in kept))]
    ppermute x40, waiting for transfers between devices: 23.2 us -> 24.6 us  [swap(): return lax.ppermute(value, axis, [(i, i ^ distance) for i in range(size)])]
  transfers between devices with their start and end apart: 40 -> 40, of which waited for: 10 -> 10; matrix products, arithmetic and copies ran while one was open for 0% -> 0% of each run, Pallas kernels for 49% -> 47%
where the time goes in v3:
time: 135 us
  Pallas kernels  66.4 us (49%)
  starting transfers between devices  41.8 us (31%)
  waiting for transfers between devices  24.6 us (18%)
    pallas_call x35, Pallas kernels, call(): return lambda *args: run(*args, *(in_vmem(value) for value in kept))  66.4 us
    ppermute x40, starting transfers between devices, swap(): return lax.ppermute(value, axis, [(i, i ^ distance) for i in range(size)])  41.8 us
    ppermute x40, waiting for transfers between devices, swap(): return lax.ppermute(value, axis, [(i, i ^ distance) for i in range(size)])  24.6 us
  transfers between devices with their start and end apart: 40, of which 10 were waited for; matrix products, arithmetic and copies ran while one was open for 0% of the time, Pallas kernels for 47%

profile of v3, /device:TPU:1, one launch (start us, length us, event | category | flops | bytes accessed | tf_op | source)
XLA Modules:
  0.0 134.6 jit_solution(2504118789022084491)
XLA Ops:
  0.7 1.6 %give.2.after_ref = f32[1024,512]{1,0:T(8,128)S(1)} custom-call(s32[1]{0:T(128)} %bitcast.core_ref, f32[1024,4096]{1,0:T(8,128)} %bitcast.2, f32[1024,4096]{1,0:T(8,128)} %bitcast.3), custom_call_target="tpu_custom_call" | custom-call | tf_op jit(solution)/shard_map/give/pallas_call | solution.py:89
  2.4 0.5 collective-permute-start
  2.9 1.6 %give.3.after_ref = f32[1024,512]{1,0:T(8,128)S(1)} custom-call(s32[1]{0:T(128)} %bitcast.core_ref, f32[1024,4096]{1,0:T(8,128)} %bitcast.4, f32[1024,512]{1,0:T(8,128)S(1)} %give.2.after_ref), custom_call_target="tpu_custom_call" | custom-call | tf_op jit(solution)/shard_map/give/pallas_call | solution.py:89
  4.7 2.3 %collective-permute-done = f32[128,256]{1,0:T(8,128)S(1)} collective-permute-done((f32[128,256]{1,0:T(8,128)S(1)}, f32[128,256]{1,0:T(8,128)S(1)}, u32[]{:S(2)}, u32[]{:S(2)}) %collective-permute-start) | collective-permute-done | bytes 131104 | tf_op jit(solution)/shard_map/ppermute | solution.py:531
  7.0 7.6 %first_products.1 = (f32[512,256]{1,0:T(8,128)S(1)}, f32[1024,512]{1,0:T(8,128)}, f32[1024,512]{1,0:T(8,128)}) custom-call(s32[1]{0:T(128)} %bitcast.core_ref, f32[256,256]{1,0:T(8,128)S(1)} %constant_dynamic-update-slice_fusion.a_ref.refs_0_, f32[8,256]{1,0:T(8,128)S(1)} %copy-done.1, f32[1024,4096]{1,0:T(8,128)} %bitcast.5, ...), custom_call_target="tpu_custom_call" | custom-call | tf_op jit(solution)/shard_map/first_products/pallas_call | solution.py:89
  14.8 0.4 collective-permute-start.3
  15.2 2.3 %collective-permute-start.8 = (f32[512,256]{1,0:T(8,128)S(1)}, f32[512,256]{1,0:T(8,128)S(1)}, u32[]{:S(2)}, u32[]{:S(2)}) collective-permute-start(f32[512,256]{1,0:T(8,128)S(1)} %get-tuple-element.53.krt_in_ref.total_in_ref.gram_in_ref.after_ref.refs_8_.refs_6_), channel_id=1, source_target_pairs={{0,16},{8,24},{16,0},{24,8},{1,17},{9,25},{17,1},{25,9},{2,18},{10... | collective-permute-start | bytes 1572872 | tf_op jit(solution)/shard_map/ppermute | solution.py:531
  17.5 4.7 %load.4 = (bf16[1,2048,512]{2,1,0:T(8,128)(2,1)S(1)}, bf16[1,2048,512]{2,1,0:T(8,128)(2,1)S(1)}, f32[2048,256]{1,0:T(8,128)S(1)}, f32[256,256]{1,0:T(8,128)S(1)}, bf16[512,2048]{1,0:T(8,128)(2,1)S(1)}) custom-call(s32[1]{0:T(128)} %bitcast.core_ref, f32[256,256]{1,0:T(8,128)S(1)} %constant_dynamic-update-slice_fusion.a_ref.refs_0_, f32[8,256]{1,0:T(8,128)S(1)} %copy-done.1, ...), custom_call_target="tpu_custom_call" | custom-call | tf_op jit(solution)/shard_map/load/pallas_call | solution.py:89
  22.2 6.1 %load.5 = (bf16[1,2048,512]{2,1,0:T(8,128)(2,1)S(1)}, bf16[1,2048,512]{2,1,0:T(8,128)(2,1)S(1)}, f32[512,256]{1,0:T(8,128)S(1)}, f32[2048,256]{1,0:T(8,128)S(1)}, f32[256,256]{1,0:T(8,128)S(1)}) custom-call(s32[1]{0:T(128)} %bitcast.core_ref, f32[256,256]{1,0:T(8,128)S(1)} %constant_dynamic-update-slice_fusion.a_ref.refs_0_, f32[8,256]{1,0:T(8,128)S(1)} %copy-done.1, ...), custom_call_target="tpu_custom_call" | custom-call | tf_op jit(solution)/shard_map/load/pallas_call | solution.py:89
  28.3 1.5 %collective-permute-start.15 = (f32[512,256]{1,0:T(8,128)S(1)}, f32[512,256]{1,0:T(8,128)S(1)}, u32[]{:S(2)}, u32[]{:S(2)}) collective-permute-start(f32[512,256]{1,0:T(8,128)S(1)} %get-tuple-element.62.refs_8_.refs_6_), channel_id=1, source_target_pairs={{0,16},{8,24},{16,0},{24,8},{1,17},{9,25},{17,1},{25,9},{2,18},{10... | collective-permute-start | bytes 1572872 | tf_op jit(solution)/shard_map/ppermute | solution.py:531
  29.8 6.3 %load.6 = (bf16[1,2048,512]{2,1,0:T(8,128)(2,1)S(1)}, bf16[1,2048,512]{2,1,0:T(8,128)(2,1)S(1)}, f32[512,256]{1,0:T(8,128)S(1)}, f32[2048,256]{1,0:T(8,128)S(1)}, f32[256,256]{1,0:T(8,128)S(1)}) custom-call(s32[1]{0:T(128)} %bitcast.core_ref, f32[256,256]{1,0:T(8,128)S(1)} %constant_dynamic-update-slice_fusion.a_ref.refs_0_, f32[8,256]{1,0:T(8,128)S(1)} %copy-done.1, ...), custom_call_target="tpu_custom_call" | custom-call | tf_op jit(solution)/shard_map/load/pallas_call | solution.py:89
  36.1 5.2 %load.7 = (bf16[1,2048,512]{2,1,0:T(8,128)(2,1)S(1)}, bf16[1,2048,512]{2,1,0:T(8,128)(2,1)S(1)}, f32[264,256]{1,0:T(8,128)S(1)}, f32[264,256]{1,0:T(8,128)S(1)}) custom-call(s32[1]{0:T(128)} %bitcast.core_ref, f32[256,256]{1,0:T(8,128)S(1)} %constant_dynamic-update-slice_fusion.a_ref.refs_0_, f32[8,256]{1,0:T(8,128)S(1)} %copy-done.1, ...), custom_call_target="tpu_custom_call" | custom-call | tf_op jit(solution)/shard_map/load/pallas_call | solution.py:89
  41.3 1.5 %sample_gram.2.refs_0_.refs_3_.refs_2_ = f32[256,256]{1,0:T(8,128)S(1)} custom-call(s32[1]{0:T(128)} %bitcast.core_ref, f32[128,256]{1,0:T(8,128)S(1)} %copy-done.2, f32[128,256]{1,0:T(8,128)} %collective-permute-done.1.refs_1_, f32[264,256]{1,0:T(8,128)S(1)} %get-tuple-element.70.refs_2_.refs_0_.refs_3_, ...), custom_call_target="tpu_custom_call" | custom-call | tf_op jit(solution)/shard_map/sample_gram/pallas_call | solution.py:89
  42.8 1.3 collective-permute-start.6
  44.3 0.9 collective-permute-done.6.refs_1_.refs_3_
  45.2 1.6 %mass_base.2 = (f32[2048,256]{1,0:T(8,128)S(1)}, f32[8,256]{1,0:T(8,128)S(1)}) custom-call(s32[1]{0:T(128)} %bitcast.core_ref, f32[256,256]{1,0:T(8,128)S(1)} %sample_gram.2.refs_0_.refs_3_.refs_2_, f32[256,256]{1,0:T(8,128)S(1)} %collective-permute-done.6.refs_1_.refs_3_, f32[8,256]{1,0:T(8,128)S(1)} %copy-done.1, ...), custom_call_target="tpu_custom_call" | custom-call | tf_op jit(solution)/shard_map/mass_base/pallas_call | solution.py:89
  47.0 1.3 collective-permute-start.13
  48.3 2.4 %collective-permute-start.9 = (f32[128,256]{1,0:T(8,128)S(1)}, f32[128,256]{1,0:T(8,128)S(1)}, u32[]{:S(2)}, u32[]{:S(2)}) collective-permute-start(f32[128,256]{1,0:T(8,128)S(1)} %slice.45), channel_id=1, source_target_pairs={{0,4},{1,5},{2,6},{3,7},{4,0},{5,1},{6,2},{7,3},{8,12},{9,13},{10,... | collective-permute-start | bytes 393224 | tf_op jit(solution)/shard_map/ppermute | solution.py:531
  50.9 2.1 %mass_products.5.refs_8_.refs_9_.refs_10_.refs_6_ = f32[512,256]{1,0:T(8,128)S(1)} custom-call(s32[1]{0:T(128)} %bitcast.core_ref, bf16[512,2048]{1,0:T(8,128)(2,1)S(1)} %get-tuple-element.54.refs_5_.refs_0_, bf16[1,2048,512]{2,1,0:T(8,128)(2,1)S(1)} %get-tuple-element.71.refs_9_.refs_11_.refs_10_.refs_1_.refs_17_.refs_3_, ...), custom_call_target="tpu_custom_call" | custom-call | tf_op jit(solution)/shard_map/mass_products/pallas_call | solution.py:89
  53.1 2.2 %drive_products.4 = (f32[512,256]{1,0:T(8,128)S(1)}, f32[2048,256]{1,0:T(8,128)S(1)}, f32[256,256]{1,0:T(8,128)S(1)}) custom-call(s32[1]{0:T(128)} %bitcast.core_ref, f32[256,256]{1,0:T(8,128)S(1)} %constant_dynamic-update-slice_fusion.a_ref.refs_0_, f32[8,256]{1,0:T(8,128)S(1)} %copy-done.1, f32[8,256]{1,0:T(8,128)S(1)} %get-tuple-element.75.refs_2_, ...), custom_call_target="tpu_custom_call" | custom-call | tf_op jit(solution)/shard_map/drive_products/pallas_call | solution.py:89
  55.3 1.4 %collective-permute-start.14 = (f32[136,256]{1,0:T(8,128)S(1)}, f32[136,256]{1,0:T(8,128)S(1)}, u32[]{:S(2)}, u32[]{:S(2)}) collective-permute-start(f32[136,256]{1,0:T(8,128)S(1)} %add.54.refs_0_), channel_id=1, source_target_pairs={{0,2},{1,3},{2,0},{3,1},{4,6},{5,7},{6,4},{7,5},{8,10},{9,11},{10,... | collective-permute-start | bytes 417800 | tf_op jit(solution)/shard_map/ppermute | solution.py:531
  57.0 1.3 collective-permute-start.21
  58.2 2.3 %drive_products.5 = (f32[512,256]{1,0:T(8,128)S(1)}, f32[2048,256]{1,0:T(8,128)S(1)}, f32[256,256]{1,0:T(8,128)S(1)}) custom-call(s32[1]{0:T(128)} %bitcast.core_ref, f32[256,256]{1,0:T(8,128)S(1)} %constant_dynamic-update-slice_fusion.a_ref.refs_0_, f32[8,256]{1,0:T(8,128)S(1)} %copy-done.1, f32[8,256]{1,0:T(8,128)S(1)} %get-tuple-element.75.refs_2_, ...), custom_call_target="tpu_custom_call" | custom-call | tf_op jit(solution)/shard_map/drive_products/pallas_call | solution.py:89
  60.5 1.3 collective-permute-start.16
  61.9 2.3 %collective-permute-start.11 = (f32[128,256]{1,0:T(8,128)S(1)}, f32[128,256]{1,0:T(8,128)S(1)}, u32[]{:S(2)}, u32[]{:S(2)}) collective-permute-start(f32[128,256]{1,0:T(8,128)S(1)} %add.42), channel_id=1, source_target_pairs={{0,2},{1,3},{2,0},{3,1},{4,6},{5,7},{6,4},{7,5},{8,10},{9,11},{10,... | collective-permute-start | bytes 393224 | tf_op jit(solution)/shard_map/ppermute | solution.py:531
  64.2 3.1 %collective-permute-done.11 = f32[128,256]{1,0:T(8,128)S(1)} collective-permute-done((f32[128,256]{1,0:T(8,128)S(1)}, f32[128,256]{1,0:T(8,128)S(1)}, u32[]{:S(2)}, u32[]{:S(2)}) %collective-permute-start.11) | collective-permute-done | bytes 131104 | tf_op jit(solution)/shard_map/ppermute | solution.py:531
  67.2 3.5 %collective-permute-start.12 = (f32[128,256]{1,0:T(8,128)S(1)}, f32[128,256]{1,0:T(8,128)S(1)}, u32[]{:S(2)}, u32[]{:S(2)}) collective-permute-start(f32[128,256]{1,0:T(8,128)S(1)} %add.43.refs_4_), channel_id=1, source_target_pairs={{0,8},{8,0},{16,24},{24,16},{1,9},{9,1},{17,25},{25,17},{2,10},{10... | collective-permute-start | bytes 393224 | tf_op jit(solution)/shard_map/ppermute | solution.py:531
  70.9 0.6 collective-permute-start.19
  71.5 3.1 %collective-permute-done.19.refs_9_ = f32[8,256]{1,0:T(8,128)S(1)} collective-permute-done((f32[8,256]{1,0:T(8,128)S(1)}, f32[8,256]{1,0:T(8,128)S(1)}, u32[]{:S(2)}, u32[]{:S(2)}) %collective-permute-start.19) | collective-permute-done | bytes 8224 | tf_op jit(solution)/shard_map/ppermute | solution.py:531
  74.6 1.3 small_step.2
  75.9 2.1 %mass_products.6.refs_3_.near_ref = f32[512,256]{1,0:T(8,128)S(1)} custom-call(s32[1]{0:T(128)} %bitcast.core_ref, bf16[512,2048]{1,0:T(8,128)(2,1)S(1)} %get-tuple-element.82.refs_0_, bf16[1,2048,512]{2,1,0:T(8,128)(2,1)S(1)} %get-tuple-element.58.refs_9_.refs_3_.refs_5_.refs_4_.refs_11_.refs_1_, ...), custom_call_target="tpu_custom_call" | custom-call | tf_op jit(solution)/shard_map/mass_products/pallas_call | solution.py:89
  78.1 0.3 collective-permute-start.20
  78.4 2.1 %mass_products.7.refs_3_.near_ref = f32[512,256]{1,0:T(8,128)S(1)} custom-call(s32[1]{0:T(128)} %bitcast.core_ref, bf16[512,2048]{1,0:T(8,128)(2,1)S(1)} %get-tuple-element.82.refs_0_, bf16[1,2048,512]{2,1,0:T(8,128)(2,1)S(1)} %get-tuple-element.63.refs_11_.refs_5_.refs_7_.refs_6_.refs_13_.refs_3_.refs_1_, ...), custom_call_target="tpu_custom_call" | custom-call | tf_op jit(solution)/shard_map/mass_products/pallas_call | solution.py:89
  80.6 2.1 %mass_products.8.refs_3_.near_ref = f32[512,256]{1,0:T(8,128)S(1)} custom-call(s32[1]{0:T(128)} %bitcast.core_ref, bf16[512,2048]{1,0:T(8,128)(2,1)S(1)} %get-tuple-element.82.refs_0_, bf16[1,2048,512]{2,1,0:T(8,128)(2,1)S(1)} %get-tuple-element.68.refs_13_.refs_7_.refs_9_.refs_8_.refs_15_.refs_1_.refs_3_, ...), custom_call_target="tpu_custom_call" | custom-call | tf_op jit(solution)/shard_map/mass_products/pallas_call | solution.py:89
  82.7 2.4 %mass_products.9.refs_10_.near_ref = f32[512,256]{1,0:T(8,128)S(1)} custom-call(s32[1]{0:T(128)} %bitcast.core_ref, bf16[512,2048]{1,0:T(8,128)(2,1)S(1)} %get-tuple-element.82.refs_0_, bf16[1,2048,512]{2,1,0:T(8,128)(2,1)S(1)} %get-tuple-element.71.refs_9_.refs_11_.refs_10_.refs_1_.refs_17_.refs_3_, ...), custom_call_target="tpu_custom_call" | custom-call | tf_op jit(solution)/shard_map/mass_products/pallas_call | solution.py:89
  85.1 2.3 %drive_products.6 = (f32[512,256]{1,0:T(8,128)S(1)}, f32[2048,256]{1,0:T(8,128)S(1)}, f32[256,256]{1,0:T(8,128)S(1)}) custom-call(s32[1]{0:T(128)} %bitcast.core_ref, f32[256,256]{1,0:T(8,128)S(1)} %get-tuple-element.80.refs_3_.refs_0_.a_ref, f32[8,256]{1,0:T(8,128)S(1)} %get-tuple-element.81.refs_1_.b_ref, f32[8,256]{1,0:T(8,128)S(1)} %get-tuple-element.75.refs_2_, ...), custom_call_target="tpu_custom_call" | custom-call | tf_op jit(solution)/shard_map/drive_products/pallas_call | solution.py:89
  87.4 2.8 %drive_products.7 = (f32[512,256]{1,0:T(8,128)S(1)}, f32[264,256]{1,0:T(8,128)S(1)}, f32[264,256]{1,0:T(8,128)S(1)}) custom-call(s32[1]{0:T(128)} %bitcast.core_ref, f32[256,256]{1,0:T(8,128)S(1)} %get-tuple-element.80.refs_3_.refs_0_.a_ref, f32[8,256]{1,0:T(8,128)S(1)} %get-tuple-element.81.refs_1_.b_ref, f32[8,256]{1,0:T(8,128)S(1)} %get-tuple-element.75.refs_2_, ...), custom_call_target="tpu_custom_call" | custom-call | tf_op jit(solution)/shard_map/drive_products/pallas_call | solution.py:89
  90.1 2.2 %collective-permute-start.22 = (f32[264,256]{1,0:T(8,128)S(1)}, f32[264,256]{1,0:T(8,128)S(1)}, u32[]{:S(2)}, u32[]{:S(2)}) collective-permute-start(f32[264,256]{1,0:T(8,128)S(1)} %get-tuple-element.88), channel_id=1, source_target_pairs={{0,8},{8,0},{16,24},{24,16},{1,9},{9,1},{17,25},{25,17},{2,10},{10... | collective-permute-start | bytes 811016 | tf_op jit(solution)/shard_map/ppermute | solution.py:531
  92.3 1.2 collective-permute-done.22.far_ref
  93.9 1.2 collective-permute-start.34
  95.1 0.4 collective-permute-start.25
  95.5 3.0 %collective-permute-done.23 = f32[136,256]{1,0:T(8,128)S(1)} collective-permute-done((f32[136,256]{1,0:T(8,128)S(1)}, f32[136,256]{1,0:T(8,128)S(1)}, u32[]{:S(2)}, u32[]{:S(2)}) %collective-permute-start.23) | collective-permute-done | bytes 139296 | tf_op jit(solution)/shard_map/ppermute | solution.py:531
  98.6 0.4 sample_gram.3.gram_ref.gram_a_ref
  99.0 1.3 collective-permute-start.24
  100.3 1.2 collective-permute-start.37
  101.5 1.3 collective-permute-start.29
  102.8 0.4 collective-permute-done.25
  103.2 1.3 collective-permute-start.26
  104.6 1.7 %mass_base.3 = (f32[2048,256]{1,0:T(8,128)S(1)}, f32[8,256]{1,0:T(8,128)S(1)}) custom-call(s32[1]{0:T(128)} %bitcast.core_ref, f32[256,256]{1,0:T(8,128)S(1)} %sample_gram.3.gram_ref.gram_a_ref, f32[256,256]{1,0:T(8,128)S(1)} %collective-permute-done.24.other_ref.gram_a_other_ref, f32[8,256]{1,0:T(8,128)S(1)} %get-tuple-element.81.refs_1_.b_ref, ...), custom_call_target="tpu_custom_call" | custom-call | tf_op jit(solution)/shard_map/mass_base/pallas_call | solution.py:89
  106.5 2.0 %collective-permute-start.36 = (f32[512,256]{1,0:T(8,128)S(1)}, f32[512,256]{1,0:T(8,128)S(1)}, u32[]{:S(2)}, u32[]{:S(2)}) collective-permute-start(f32[512,256]{1,0:T(8,128)S(1)} %last_step.5.mine_ref.held_ref), channel_id=1, source_target_pairs={{0,8},{8,0},{16,24},{24,16},{1,9},{9,1},{17,25},{25,17},{2,10},{10... | collective-permute-start | bytes 1572872 | tf_op jit(solution)/shard_map/ppermute | solution.py:531
  108.8 0.8 collective-permute-start.35
  109.6 1.2 collective-permute-start.33
  110.9 1.4 %collective-permute-start.27 = (f32[128,256]{1,0:T(8,128)S(1)}, f32[128,256]{1,0:T(8,128)S(1)}, u32[]{:S(2)}, u32[]{:S(2)}) collective-permute-start(f32[128,256]{1,0:T(8,128)S(1)} %add.46.refs_1_), channel_id=1, source_target_pairs={{0,2},{1,3},{2,0},{3,1},{4,6},{5,7},{6,4},{7,5},{8,10},{9,11},{10,... | collective-permute-start | bytes 393224 | tf_op jit(solution)/shard_map/ppermute | solution.py:531
  112.3 3.4 %collective-permute-done.27 = f32[128,256]{1,0:T(8,128)S(1)} collective-permute-done((f32[128,256]{1,0:T(8,128)S(1)}, f32[128,256]{1,0:T(8,128)S(1)}, u32[]{:S(2)}, u32[]{:S(2)}) %collective-permute-start.27) | collective-permute-done | bytes 131104 | tf_op jit(solution)/shard_map/ppermute | solution.py:531
  115.7 1.3 collective-permute-start.30
  117.0 7.0 %collective-permute-done.30 = f32[136,256]{1,0:T(8,128)S(1)} collective-permute-done((f32[136,256]{1,0:T(8,128)S(1)}, f32[136,256]{1,0:T(8,128)S(1)}, u32[]{:S(2)}, u32[]{:S(2)}) %collective-permute-start.30) | collective-permute-done | bytes 139296 | tf_op jit(solution)/shard_map/ppermute | solution.py:531
  124.1 1.6 %collective-permute-start.28 = (f32[128,256]{1,0:T(8,128)S(1)}, f32[128,256]{1,0:T(8,128)S(1)}, u32[]{:S(2)}, u32[]{:S(2)}) collective-permute-start(f32[128,256]{1,0:T(8,128)S(1)} %add.47.refs_0_.refs_1_.gram_c_ref), channel_id=1, source_target_pairs={{0,8},{8,0},{16,24},{24,16},{1,9},{9,1},{17,25},{25,17},{2,10},{10... | collective-permute-start | bytes 393224 | tf_op jit(solution)/shard_map/ppermute | solution.py:531
  126.1 1.0 join.4
  127.4 0.8 collective-permute-start.39
  128.1 1.0 join.5
  129.5 1.6 %collective-permute-start.38 = (f32[512,256]{1,0:T(8,128)S(1)}, f32[512,256]{1,0:T(8,128)S(1)}, u32[]{:S(2)}, u32[]{:S(2)}) collective-permute-start(f32[512,256]{1,0:T(8,128)S(1)} %last_step.7.after_ref.mine_ref), channel_id=1, source_target_pairs={{0,8},{8,0},{16,24},{24,16},{1,9},{9,1},{17,25},{25,17},{2,10},{10... | collective-permute-start | bytes 1572872 | tf_op jit(solution)/shard_map/ppermute | solution.py:531
  131.1 1.3 small_step.3
  132.5 1.0 join.6
  133.5 1.0 join.7
  (85 shorter events, 3.7 us)
Async XLA Ops:
  0.6 1.8 %copy-start.2 = (f32[128,256]{1,0:T(8,128)S(1)}, f32[128,256]{1,0:T(8,128)}, u32[]{:S(2)}) copy-start(f32[128,256]{1,0:T(8,128)} %refs_0_.1) | copy-start | bytes 393220
  2.3 4.6 %copy-start.1 = (f32[8,256]{1,0:T(8,128)S(1)}, f32[8,256]{1,0:T(8,128)}, u32[]{:S(2)}) copy-start(f32[8,256]{1,0:T(8,128)} %refs_1_.11) | copy-start | bytes 24580
  2.3 4.6 %collective-permute-start.2 = (f32[1024,512]{1,0:T(8,128)S(1)}, f32[1024,512]{1,0:T(8,128)S(1)}, u32[]{:S(2)}, u32[]{:S(2)}) collective-permute-start(f32[1024,512]{1,0:T(8,128)S(1)} %give.2.after_ref), channel_id=1, source_target_pairs={{0,8},{8,0},{16,24},{24,16},{1,9},{9,1},{17,25},{25,17},{2,10},{10... | collective-permute-start | bytes 6291464 | tf_op jit(solution)/shard_map/ppermute | solution.py:531
  2.4 4.5 %collective-permute-start = (f32[128,256]{1,0:T(8,128)S(1)}, f32[128,256]{1,0:T(8,128)S(1)}, u32[]{:S(2)}, u32[]{:S(2)}) collective-permute-start(f32[128,256]{1,0:T(8,128)S(1)} %copy-done.2), channel_id=1, source_target_pairs={{0,8},{8,0},{16,24},{24,16},{1,9},{9,1},{17,25},{25,17},{2,10},{10... | collective-permute-start | bytes 393224 | tf_op jit(solution)/shard_map/ppermute | solution.py:531
  4.5 17.7 %collective-permute-start.5 = (f32[1024,512]{1,0:T(8,128)S(1)}, f32[1024,512]{1,0:T(8,128)}, u32[]{:S(2)}, u32[]{:S(2)}) collective-permute-start(f32[1024,512]{1,0:T(8,128)S(1)} %give.3.after_ref), channel_id=1, source_target_pairs={{0,8},{8,0},{16,24},{24,16},{1,9},{9,1},{17,25},{25,17},{2,10},{10... | collective-permute-start | bytes 6291464 | tf_op jit(solution)/shard_map/ppermute | solution.py:531
  6.9 7.6 %copy-start = (f32[1024,512]{1,0:T(8,128)}, f32[1024,512]{1,0:T(8,128)S(1)}, u32[]{:S(2)}) copy-start(f32[1024,512]{1,0:T(8,128)S(1)} %collective-permute-done.2.other_ref) | copy-start | bytes 6291460
  14.6 15.3 %collective-permute-start.4 = (f32[1024,512]{1,0:T(8,128)}, f32[1024,512]{1,0:T(8,128)}, u32[]{:S(2)}, u32[]{:S(2)}) collective-permute-start(f32[1024,512]{1,0:T(8,128)} %get-tuple-element.55), channel_id=1, source_target_pairs={{0,8},{8,0},{16,24},{24,16},{1,9},{9,1},{17,25},{25,17},{2,10},{10... | collective-permute-start | bytes 6291464 | tf_op jit(solution)/shard_map/ppermute | solution.py:531
  14.8 21.3 %collective-permute-start.3 = (f32[1024,512]{1,0:T(8,128)}, f32[1024,512]{1,0:T(8,128)}, u32[]{:S(2)}, u32[]{:S(2)}) collective-permute-start(f32[1024,512]{1,0:T(8,128)} %get-tuple-element.52), channel_id=1, source_target_pairs={{0,8},{8,0},{16,24},{24,16},{1,9},{9,1},{17,25},{25,17},{2,10},{10... | collective-permute-start | bytes 6291464 | tf_op jit(solution)/shard_map/ppermute | solution.py:531
  15.2 31.8 %collective-permute-start.8 = (f32[512,256]{1,0:T(8,128)S(1)}, f32[512,256]{1,0:T(8,128)S(1)}, u32[]{:S(2)}, u32[]{:S(2)}) collective-permute-start(f32[512,256]{1,0:T(8,128)S(1)} %get-tuple-element.53.krt_in_ref.total_in_ref.gram_in_ref.after_ref.refs_8_.refs_6_), channel_id=1, source_target_pairs={{0,16},{8,24},{16,0},{24,8},{1,17},{9,25},{17,1},{25,9},{2,18},{10... | collective-permute-start | bytes 1572872 | tf_op jit(solution)/shard_map/ppermute | solution.py:531
  17.5 23.8 %collective-permute-start.1 = (f32[128,256]{1,0:T(8,128)S(1)}, f32[128,256]{1,0:T(8,128)}, u32[]{:S(2)}, u32[]{:S(2)}) collective-permute-start(f32[128,256]{1,0:T(8,128)S(1)} %copy-done.2), channel_id=1, source_target_pairs={{0,16},{8,24},{16,0},{24,8},{1,17},{9,25},{17,1},{25,9},{2,18},{10... | collective-permute-start | bytes 393224 | tf_op jit(solution)/shard_map/ppermute | solution.py:531
  28.3 29.9 %collective-permute-start.15 = (f32[512,256]{1,0:T(8,128)S(1)}, f32[512,256]{1,0:T(8,128)S(1)}, u32[]{:S(2)}, u32[]{:S(2)}) collective-permute-start(f32[512,256]{1,0:T(8,128)S(1)} %get-tuple-element.62.refs_8_.refs_6_), channel_id=1, source_target_pairs={{0,16},{8,24},{16,0},{24,8},{1,17},{9,25},{17,1},{25,9},{2,18},{10... | collective-permute-start | bytes 1572872 | tf_op jit(solution)/shard_map/ppermute | solution.py:531
  41.3 2.9 %copy-start.4 = (f32[4096,256]{1,0:T(8,128)S(1)}, f32[4096,256]{1,0:T(8,128)}, u32[]{:S(2)}) copy-start(f32[4096,256]{1,0:T(8,128)} %refs_4_.5) | copy-start | bytes 12582916
  42.8 2.4 %collective-permute-start.6 = (f32[256,256]{1,0:T(8,128)S(1)}, f32[256,256]{1,0:T(8,128)S(1)}, u32[]{:S(2)}, u32[]{:S(2)}) collective-permute-start(f32[256,256]{1,0:T(8,128)S(1)} %sample_gram.2.refs_0_.refs_3_.refs_2_), channel_id=1, source_target_pairs={{0,8},{8,0},{16,24},{24,16},{1,9},{9,1},{17,25},{25,17},{2,10},{10... | collective-permute-start | bytes 786440 | tf_op jit(solution)/shard_map/ppermute | solution.py:531
  44.1 2.8 %collective-permute-start.7 = (f32[264,256]{1,0:T(8,128)S(1)}, f32[264,256]{1,0:T(8,128)S(1)}, u32[]{:S(2)}, u32[]{:S(2)}) collective-permute-start(f32[264,256]{1,0:T(8,128)S(1)} %get-tuple-element.73), channel_id=1, source_target_pairs={{0,8},{8,0},{16,24},{24,16},{1,9},{9,1},{17,25},{25,17},{2,10},{10... | collective-permute-start | bytes 811016 | tf_op jit(solution)/shard_map/ppermute | solution.py:531
  47.0 8.3 %collective-permute-start.13 = (f32[136,256]{1,0:T(8,128)S(1)}, f32[136,256]{1,0:T(8,128)S(1)}, u32[]{:S(2)}, u32[]{:S(2)}) collective-permute-start(f32[136,256]{1,0:T(8,128)S(1)} %slice.46.refs_0_), channel_id=1, source_target_pairs={{0,1},{1,0},{2,3},{3,2},{4,5},{5,4},{6,7},{7,6},{8,9},{9,8},{10,11... | collective-permute-start | bytes 417800 | tf_op jit(solution)/shard_map/ppermute | solution.py:531
  48.3 8.4 %collective-permute-start.9 = (f32[128,256]{1,0:T(8,128)S(1)}, f32[128,256]{1,0:T(8,128)S(1)}, u32[]{:S(2)}, u32[]{:S(2)}) collective-permute-start(f32[128,256]{1,0:T(8,128)S(1)} %slice.45), channel_id=1, source_target_pairs={{0,4},{1,5},{2,6},{3,7},{4,0},{5,1},{6,2},{7,3},{8,12},{9,13},{10,... | collective-permute-start | bytes 393224 | tf_op jit(solution)/shard_map/ppermute | solution.py:531
  50.7 20.1 %collective-permute-start.17 = (f32[512,256]{1,0:T(8,128)S(1)}, f32[512,256]{1,0:T(8,128)S(1)}, u32[]{:S(2)}, u32[]{:S(2)}) collective-permute-start(f32[512,256]{1,0:T(8,128)S(1)} %get-tuple-element.67.refs_8_.refs_3_.refs_6_), channel_id=1, source_target_pairs={{0,16},{8,24},{16,0},{24,8},{1,17},{9,25},{17,1},{25,9},{2,18},{10... | collective-permute-start | bytes 1572872 | tf_op jit(solution)/shard_map/ppermute | solution.py:531
  55.3 5.2 %collective-permute-start.14 = (f32[136,256]{1,0:T(8,128)S(1)}, f32[136,256]{1,0:T(8,128)S(1)}, u32[]{:S(2)}, u32[]{:S(2)}) collective-permute-start(f32[136,256]{1,0:T(8,128)S(1)} %add.54.refs_0_), channel_id=1, source_target_pairs={{0,2},{1,3},{2,0},{3,1},{4,6},{5,7},{6,4},{7,5},{8,10},{9,11},{10,... | collective-permute-start | bytes 417800 | tf_op jit(solution)/shard_map/ppermute | solution.py:531
  56.7 5.2 %collective-permute-start.10 = (f32[128,256]{1,0:T(8,128)S(1)}, f32[128,256]{1,0:T(8,128)S(1)}, u32[]{:S(2)}, u32[]{:S(2)}) collective-permute-start(f32[128,256]{1,0:T(8,128)S(1)} %slice_add_fusion.1), channel_id=1, source_target_pairs={{0,1},{1,0},{2,3},{3,2},{4,5},{5,4},{6,7},{7,6},{8,9},{9,8},{10,11... | collective-permute-start | bytes 393224 | tf_op jit(solution)/shard_map/ppermute | solution.py:531
  57.0 30.4 %collective-permute-start.21 = (f32[512,256]{1,0:T(8,128)S(1)}, f32[512,256]{1,0:T(8,128)S(1)}, u32[]{:S(2)}, u32[]{:S(2)}) collective-permute-start(f32[512,256]{1,0:T(8,128)S(1)} %mass_products.5.refs_8_.refs_9_.refs_10_.refs_6_), channel_id=1, source_target_pairs={{0,16},{8,24},{16,0},{24,8},{1,17},{9,25},{17,1},{25,9},{2,18},{10... | collective-permute-start | bytes 1572872 | tf_op jit(solution)/shard_map/ppermute | solution.py:531
  60.5 10.2 %collective-permute-start.16 = (f32[136,256]{1,0:T(8,128)S(1)}, f32[136,256]{1,0:T(8,128)S(1)}, u32[]{:S(2)}, u32[]{:S(2)}) collective-permute-start(f32[136,256]{1,0:T(8,128)S(1)} %add.55.refs_0_), channel_id=1, source_target_pairs={{0,4},{1,5},{2,6},{3,7},{4,0},{5,1},{6,2},{7,3},{8,12},{9,13},{10,... | collective-permute-start | bytes 417800 | tf_op jit(solution)/shard_map/ppermute | solution.py:531
  61.9 5.3 %collective-permute-start.11 = (f32[128,256]{1,0:T(8,128)S(1)}, f32[128,256]{1,0:T(8,128)S(1)}, u32[]{:S(2)}, u32[]{:S(2)}) collective-permute-start(f32[128,256]{1,0:T(8,128)S(1)} %add.42), channel_id=1, source_target_pairs={{0,2},{1,3},{2,0},{3,1},{4,6},{5,7},{6,4},{7,5},{8,10},{9,11},{10,... | collective-permute-start | bytes 393224 | tf_op jit(solution)/shard_map/ppermute | solution.py:531
  67.2 7.4 %collective-permute-start.12 = (f32[128,256]{1,0:T(8,128)S(1)}, f32[128,256]{1,0:T(8,128)S(1)}, u32[]{:S(2)}, u32[]{:S(2)}) collective-permute-start(f32[128,256]{1,0:T(8,128)S(1)} %add.43.refs_4_), channel_id=1, source_target_pairs={{0,8},{8,0},{16,24},{24,16},{1,9},{9,1},{17,25},{25,17},{2,10},{10... | collective-permute-start | bytes 393224 | tf_op jit(solution)/shard_map/ppermute | solution.py:531
  70.8 3.8 %collective-permute-start.18 = (f32[128,256]{1,0:T(8,128)S(1)}, f32[128,256]{1,0:T(8,128)S(1)}, u32[]{:S(2)}, u32[]{:S(2)}) collective-permute-start(f32[128,256]{1,0:T(8,128)S(1)} %slice.47.refs_6_), channel_id=1, source_target_pairs={{0,8},{8,0},{16,24},{24,16},{1,9},{9,1},{17,25},{25,17},{2,10},{10... | collective-permute-start | bytes 393224 | tf_op jit(solution)/shard_map/ppermute | solution.py:531
  70.9 3.7 %collective-permute-start.19 = (f32[8,256]{1,0:T(8,128)S(1)}, f32[8,256]{1,0:T(8,128)S(1)}, u32[]{:S(2)}, u32[]{:S(2)}) collective-permute-start(f32[8,256]{1,0:T(8,128)S(1)} %slice.48.refs_8_), channel_id=1, source_target_pairs={{0,16},{8,24},{16,0},{24,8},{1,17},{9,25},{17,1},{25,9},{2,18},{10... | collective-permute-start | bytes 24584 | tf_op jit(solution)/shard_map/ppermute | solution.py:531
  78.1 20.4 %collective-permute-start.20 = (f32[640,256]{1,0:T(8,128)S(1)}, f32[640,256]{1,0:T(8,128)S(1)}, u32[]{:S(2)}, u32[]{:S(2)}) collective-permute-start(f32[640,256]{1,0:T(8,128)S(1)} %pad_maximum_fusion), channel_id=1, source_target_pairs={{0,16},{8,24},{16,0},{24,8},{1,17},{9,25},{17,1},{25,9},{2,18},{10... | collective-permute-start | bytes 1966088 | tf_op jit(solution)/shard_map/ppermute | solution.py:531
  90.1 3.4 %collective-permute-start.22 = (f32[264,256]{1,0:T(8,128)S(1)}, f32[264,256]{1,0:T(8,128)S(1)}, u32[]{:S(2)}, u32[]{:S(2)}) collective-permute-start(f32[264,256]{1,0:T(8,128)S(1)} %get-tuple-element.88), channel_id=1, source_target_pairs={{0,8},{8,0},{16,24},{24,16},{1,9},{9,1},{17,25},{25,17},{2,10},{10... | collective-permute-start | bytes 811016 | tf_op jit(solution)/shard_map/ppermute | solution.py:531
  93.6 5.0 %collective-permute-start.23 = (f32[136,256]{1,0:T(8,128)S(1)}, f32[136,256]{1,0:T(8,128)S(1)}, u32[]{:S(2)}, u32[]{:S(2)}) collective-permute-start(f32[136,256]{1,0:T(8,128)S(1)} %slice.50), channel_id=1, source_target_pairs={{0,1},{1,0},{2,3},{3,2},{4,5},{5,4},{6,7},{7,6},{8,9},{9,8},{10,11... | collective-permute-start | bytes 417800 | tf_op jit(solution)/shard_map/ppermute | solution.py:531
  93.9 14.7 %collective-permute-start.34 = (f32[512,256]{1,0:T(8,128)S(1)}, f32[512,256]{1,0:T(8,128)S(1)}, u32[]{:S(2)}, u32[]{:S(2)}) collective-permute-start(f32[512,256]{1,0:T(8,128)S(1)} %mass_products.7.refs_3_.near_ref), channel_id=1, source_target_pairs={{0,16},{8,24},{16,0},{24,8},{1,17},{9,25},{17,1},{25,9},{2,18},{10... | collective-permute-start | bytes 1572872 | tf_op jit(solution)/shard_map/ppermute | solution.py:531
  95.1 8.1 %collective-permute-start.25 = (f32[128,256]{1,0:T(8,128)S(1)}, f32[128,256]{1,0:T(8,128)S(1)}, u32[]{:S(2)}, u32[]{:S(2)}) collective-permute-start(f32[128,256]{1,0:T(8,128)S(1)} %slice.51), channel_id=1, source_target_pairs={{0,4},{1,5},{2,6},{3,7},{4,0},{5,1},{6,2},{7,3},{8,12},{9,13},{10,... | collective-permute-start | bytes 393224 | tf_op jit(solution)/shard_map/ppermute | solution.py:531
  99.0 5.6 %collective-permute-start.24 = (f32[256,256]{1,0:T(8,128)S(1)}, f32[256,256]{1,0:T(8,128)S(1)}, u32[]{:S(2)}, u32[]{:S(2)}) collective-permute-start(f32[256,256]{1,0:T(8,128)S(1)} %sample_gram.3.gram_ref.gram_a_ref), channel_id=1, source_target_pairs={{0,8},{8,0},{16,24},{24,16},{1,9},{9,1},{17,25},{25,17},{2,10},{10... | collective-permute-start | bytes 786440 | tf_op jit(solution)/shard_map/ppermute | solution.py:531
  100.3 25.4 %collective-permute-start.37 = (f32[512,256]{1,0:T(8,128)S(1)}, f32[512,256]{1,0:T(8,128)S(1)}, u32[]{:S(2)}, u32[]{:S(2)}) collective-permute-start(f32[512,256]{1,0:T(8,128)S(1)} %mass_products.8.refs_3_.near_ref), channel_id=1, source_target_pairs={{0,16},{8,24},{16,0},{24,8},{1,17},{9,25},{17,1},{25,9},{2,18},{10... | collective-permute-start | bytes 1572872 | tf_op jit(solution)/shard_map/ppermute | solution.py:531
  101.5 7.0 %collective-permute-start.29 = (f32[136,256]{1,0:T(8,128)S(1)}, f32[136,256]{1,0:T(8,128)S(1)}, u32[]{:S(2)}, u32[]{:S(2)}) collective-permute-start(f32[136,256]{1,0:T(8,128)S(1)} %slice_add_fusion.2.after_ref), channel_id=1, source_target_pairs={{0,2},{1,3},{2,0},{3,1},{4,6},{5,7},{6,4},{7,5},{8,10},{9,11},{10,... | collective-permute-start | bytes 417800 | tf_op jit(solution)/shard_map/ppermute | solution.py:531
  103.2 7.6 %collective-permute-start.26 = (f32[128,256]{1,0:T(8,128)S(1)}, f32[128,256]{1,0:T(8,128)S(1)}, u32[]{:S(2)}, u32[]{:S(2)}) collective-permute-start(f32[128,256]{1,0:T(8,128)S(1)} %slice_add_fusion.refs_1_), channel_id=1, source_target_pairs={{0,1},{1,0},{2,3},{3,2},{4,5},{5,4},{6,7},{7,6},{8,9},{9,8},{10,11... | collective-permute-start | bytes 393224 | tf_op jit(solution)/shard_map/ppermute | solution.py:531
  106.5 19.3 %collective-permute-start.36 = (f32[512,256]{1,0:T(8,128)S(1)}, f32[512,256]{1,0:T(8,128)S(1)}, u32[]{:S(2)}, u32[]{:S(2)}) collective-permute-start(f32[512,256]{1,0:T(8,128)S(1)} %last_step.5.mine_ref.held_ref), channel_id=1, source_target_pairs={{0,8},{8,0},{16,24},{24,16},{1,9},{9,1},{17,25},{25,17},{2,10},{10... | collective-permute-start | bytes 1572872 | tf_op jit(solution)/shard_map/ppermute | solution.py:531
  108.8 18.5 %collective-permute-start.35 = (f32[512,256]{1,0:T(8,128)S(1)}, f32[512,256]{1,0:T(8,128)S(1)}, u32[]{:S(2)}, u32[]{:S(2)}) collective-permute-start(f32[512,256]{1,0:T(8,128)S(1)} %last_step.4.after_ref.mine_ref), channel_id=1, source_target_pairs={{0,8},{8,0},{16,24},{24,16},{1,9},{9,1},{17,25},{25,17},{2,10},{10... | collective-permute-start | bytes 1572872 | tf_op jit(solution)/shard_map/ppermute | solution.py:531
  109.6 19.5 %collective-permute-start.33 = (f32[512,256]{1,0:T(8,128)S(1)}, f32[512,256]{1,0:T(8,128)S(1)}, u32[]{:S(2)}, u32[]{:S(2)}) collective-permute-start(f32[512,256]{1,0:T(8,128)S(1)} %mass_products.9.refs_10_.near_ref), channel_id=1, source_target_pairs={{0,16},{8,24},{16,0},{24,8},{1,17},{9,25},{17,1},{25,9},{2,18},{10... | collective-permute-start | bytes 1572872 | tf_op jit(solution)/shard_map/ppermute | solution.py:531
  110.9 4.8 %collective-permute-start.27 = (f32[128,256]{1,0:T(8,128)S(1)}, f32[128,256]{1,0:T(8,128)S(1)}, u32[]{:S(2)}, u32[]{:S(2)}) collective-permute-start(f32[128,256]{1,0:T(8,128)S(1)} %add.46.refs_1_), channel_id=1, source_target_pairs={{0,2},{1,3},{2,0},{3,1},{4,6},{5,7},{6,4},{7,5},{8,10},{9,11},{10,... | collective-permute-start | bytes 393224 | tf_op jit(solution)/shard_map/ppermute | solution.py:531
  115.7 8.4 %collective-permute-start.30 = (f32[136,256]{1,0:T(8,128)S(1)}, f32[136,256]{1,0:T(8,128)S(1)}, u32[]{:S(2)}, u32[]{:S(2)}) collective-permute-start(f32[136,256]{1,0:T(8,128)S(1)} %add.48.refs_0_), channel_id=1, source_target_pairs={{0,4},{1,5},{2,6},{3,7},{4,0},{5,1},{6,2},{7,3},{8,12},{9,13},{10,... | collective-permute-start | bytes 417800 | tf_op jit(solution)/shard_map/ppermute | solution.py:531
  124.1 5.2 %collective-permute-start.28 = (f32[128,256]{1,0:T(8,128)S(1)}, f32[128,256]{1,0:T(8,128)S(1)}, u32[]{:S(2)}, u32[]{:S(2)}) collective-permute-start(f32[128,256]{1,0:T(8,128)S(1)} %add.47.refs_0_.refs_1_.gram_c_ref), channel_id=1, source_target_pairs={{0,8},{8,0},{16,24},{24,16},{1,9},{9,1},{17,25},{25,17},{2,10},{10... | collective-permute-start | bytes 393224 | tf_op jit(solution)/shard_map/ppermute | solution.py:531
  125.7 3.6 %collective-permute-start.31 = (f32[128,256]{1,0:T(8,128)S(1)}, f32[128,256]{1,0:T(8,128)S(1)}, u32[]{:S(2)}, u32[]{:S(2)}) collective-permute-start(f32[128,256]{1,0:T(8,128)S(1)} %slice.52.refs_3_.drive_ref), channel_id=1, source_target_pairs={{0,8},{8,0},{16,24},{24,16},{1,9},{9,1},{17,25},{25,17},{2,10},{10... | collective-permute-start | bytes 393224 | tf_op jit(solution)/shard_map/ppermute | solution.py:531
  125.8 3.5 %collective-permute-start.32 = (f32[8,256]{1,0:T(8,128)S(1)}, f32[8,256]{1,0:T(8,128)S(1)}, u32[]{:S(2)}, u32[]{:S(2)}) collective-permute-start(f32[8,256]{1,0:T(8,128)S(1)} %slice.53.refs_5_.drive_b_ref), channel_id=1, source_target_pairs={{0,16},{8,24},{16,0},{24,8},{1,17},{9,25},{17,1},{25,9},{2,18},{10... | collective-permute-start | bytes 24584 | tf_op jit(solution)/shard_map/ppermute | solution.py:531
  127.4 5.1 %collective-permute-start.39 = (f32[512,256]{1,0:T(8,128)S(1)}, f32[512,256]{1,0:T(8,128)S(1)}, u32[]{:S(2)}, u32[]{:S(2)}) collective-permute-start(f32[512,256]{1,0:T(8,128)S(1)} %last_step.6.after_ref.mine_ref), channel_id=1, source_target_pairs={{0,8},{8,0},{16,24},{24,16},{1,9},{9,1},{17,25},{25,17},{2,10},{10... | collective-permute-start | bytes 1572872 | tf_op jit(solution)/shard_map/ppermute | solution.py:531
  129.5 4.0 %collective-permute-start.38 = (f32[512,256]{1,0:T(8,128)S(1)}, f32[512,256]{1,0:T(8,128)S(1)}, u32[]{:S(2)}, u32[]{:S(2)}) collective-permute-start(f32[512,256]{1,0:T(8,128)S(1)} %last_step.7.after_ref.mine_ref), channel_id=1, source_target_pairs={{0,8},{8,0},{16,24},{24,16},{1,9},{9,1},{17,25},{25,17},{2,10},{10... | collective-permute-start | bytes 1572872 | tf_op jit(solution)/shard_map/ppermute | solution.py:531
  132.5 1.0 copy-start.3

commit v4 on v3

--- a/solution.py
+++ b/solution.py
@@ -569,7 +569,7 @@
 
     places = range(len(FIRST))
     others, after = [], x
-    for place in places[:2]:
+    for place in places[:3]:
         after = give(core, x, after, place)
         others.append(over_core(after))
     a = jnp.concatenate([sample_start, over_core(sample_start)], 0)

time: 135 us -> 134 us (level)
  waiting for transfers between devices: 24.6 us -> 22.5 us
    ppermute x40, waiting for transfers between devices: 24.6 us -> 22.5 us  [swap(): return lax.ppermute(value, axis, [(i, i ^ distance) for i in range(size)])]
    pallas_call x35 -> x36, Pallas kernels: 66.4 us -> 67.5 us  [call(): return lambda *args: run(*args, *(in_vmem(value) for value in kept))]
  transfers between devices with their start and end apart: 40 -> 40, of which waited for: 10 -> 9; matrix products, arithmetic and copies ran while one was open for 0% -> 0% of each run, Pallas kernels for 47% -> 49%
where the time goes in v4:
time: 134 us; the launch traced here: 133 us
  Pallas kernels  67.5 us (50%)
  starting transfers between devices  41.8 us (31%)
  waiting for transfers between devices  22.5 us (17%)
    pallas_call x36, Pallas kernels, call(): return lambda *args: run(*args, *(in_vmem(value) for value in kept))  67.5 us
    ppermute x40, starting transfers between devices, swap(): return lax.ppermute(value, axis, [(i, i ^ distance) for i in range(size)])  41.8 us
    ppermute x40, waiting for transfers between devices, swap(): return lax.ppermute(value, axis, [(i, i ^ distance) for i in range(size)])  22.5 us
  transfers between devices with their start and end apart: 40, of which 9 were waited for; matrix products, arithmetic and copies ran while one was open for 0% of the time, Pallas kernels for 49%

profile of v4, /device:TPU:1, one launch (start us, length us, event | category | flops | bytes accessed | tf_op | source)
XLA Modules:
  0.0 133.5 jit_solution(5637527406913315190)
XLA Ops:
  0.7 1.6 %give.3.after_ref = f32[1024,512]{1,0:T(8,128)S(1)} custom-call(s32[1]{0:T(128)} %bitcast.core_ref, f32[1024,4096]{1,0:T(8,128)} %bitcast.2, f32[1024,4096]{1,0:T(8,128)} %bitcast.3), custom_call_target="tpu_custom_call" | custom-call | tf_op jit(solution)/shard_map/give/pallas_call | solution.py:89
  2.4 0.5 collective-permute-start
  2.9 2.9 %give.4.after_ref = f32[1024,512]{1,0:T(8,128)} custom-call(s32[1]{0:T(128)} %bitcast.core_ref, f32[1024,4096]{1,0:T(8,128)} %bitcast.4, f32[1024,512]{1,0:T(8,128)S(1)} %give.3.after_ref), custom_call_target="tpu_custom_call" | custom-call | tf_op jit(solution)/shard_map/give/pallas_call | solution.py:89
  6.0 1.6 %give.5.after_ref = f32[1024,512]{1,0:T(8,128)S(1)} custom-call(s32[1]{0:T(128)} %bitcast.core_ref, f32[1024,4096]{1,0:T(8,128)} %bitcast.5, f32[1024,512]{1,0:T(8,128)} %give.4.after_ref), custom_call_target="tpu_custom_call" | custom-call | tf_op jit(solution)/shard_map/give/pallas_call | solution.py:89
  7.6 0.5 collective-permute-start.4
  8.1 5.8 %first_products.1 = (f32[512,256]{1,0:T(8,128)S(1)}, f32[1024,512]{1,0:T(8,128)}) custom-call(s32[1]{0:T(128)} %bitcast.core_ref, f32[256,256]{1,0:T(8,128)S(1)} %constant_dynamic-update-slice_fusion.a_ref.refs_0_, f32[8,256]{1,0:T(8,128)S(1)} %copy-done.1, f32[1024,4096]{1,0:T(8,128)} %bitcast.6, f32[1024,512]{1,0:T(8,128)S(1)} %collective-permute-done.2.other_ref, ...), custom_call_target="tpu_custom_call" | custom-call | tf_op jit(solution)/shard_map/first_products/pallas_call | solution.py:89
  14.1 2.6 %collective-permute-start.8 = (f32[512,256]{1,0:T(8,128)S(1)}, f32[512,256]{1,0:T(8,128)S(1)}, u32[]{:S(2)}, u32[]{:S(2)}) collective-permute-start(f32[512,256]{1,0:T(8,128)S(1)} %get-tuple-element.52.krt_in_ref.total_in_ref.gram_in_ref.after_ref.refs_8_.refs_6_), channel_id=1, source_target_pairs={{0,16},{8,24},{16,0},{24,8},{1,17},{9,25},{17,1},{25,9},{2,18},{10... | collective-permute-start | bytes 1572872 | tf_op jit(solution)/shard_map/ppermute | solution.py:531
  16.7 4.7 %load.4 = (bf16[1,2048,512]{2,1,0:T(8,128)(2,1)S(1)}, bf16[1,2048,512]{2,1,0:T(8,128)(2,1)S(1)}, f32[2048,256]{1,0:T(8,128)S(1)}, f32[256,256]{1,0:T(8,128)S(1)}, bf16[512,2048]{1,0:T(8,128)(2,1)S(1)}) custom-call(s32[1]{0:T(128)} %bitcast.core_ref, f32[256,256]{1,0:T(8,128)S(1)} %constant_dynamic-update-slice_fusion.a_ref.refs_0_, f32[8,256]{1,0:T(8,128)S(1)} %copy-done.1, ...), custom_call_target="tpu_custom_call" | custom-call | tf_op jit(solution)/shard_map/load/pallas_call | solution.py:89
  21.4 6.1 %load.5 = (bf16[1,2048,512]{2,1,0:T(8,128)(2,1)S(1)}, bf16[1,2048,512]{2,1,0:T(8,128)(2,1)S(1)}, f32[512,256]{1,0:T(8,128)S(1)}, f32[2048,256]{1,0:T(8,128)S(1)}, f32[256,256]{1,0:T(8,128)S(1)}) custom-call(s32[1]{0:T(128)} %bitcast.core_ref, f32[256,256]{1,0:T(8,128)S(1)} %constant_dynamic-update-slice_fusion.a_ref.refs_0_, f32[8,256]{1,0:T(8,128)S(1)} %copy-done.1, ...), custom_call_target="tpu_custom_call" | custom-call | tf_op jit(solution)/shard_map/load/pallas_call | solution.py:89
  27.5 1.5 %collective-permute-start.15 = (f32[512,256]{1,0:T(8,128)S(1)}, f32[512,256]{1,0:T(8,128)S(1)}, u32[]{:S(2)}, u32[]{:S(2)}) collective-permute-start(f32[512,256]{1,0:T(8,128)S(1)} %get-tuple-element.60.refs_8_.refs_6_), channel_id=1, source_target_pairs={{0,16},{8,24},{16,0},{24,8},{1,17},{9,25},{17,1},{25,9},{2,18},{10... | collective-permute-start | bytes 1572872 | tf_op jit(solution)/shard_map/ppermute | solution.py:531
  29.1 6.3 %load.6 = (bf16[1,2048,512]{2,1,0:T(8,128)(2,1)S(1)}, bf16[1,2048,512]{2,1,0:T(8,128)(2,1)S(1)}, f32[512,256]{1,0:T(8,128)S(1)}, f32[2048,256]{1,0:T(8,128)S(1)}, f32[256,256]{1,0:T(8,128)S(1)}) custom-call(s32[1]{0:T(128)} %bitcast.core_ref, f32[256,256]{1,0:T(8,128)S(1)} %constant_dynamic-update-slice_fusion.a_ref.refs_0_, f32[8,256]{1,0:T(8,128)S(1)} %copy-done.1, ...), custom_call_target="tpu_custom_call" | custom-call | tf_op jit(solution)/shard_map/load/pallas_call | solution.py:89
  35.4 5.2 %load.7 = (bf16[1,2048,512]{2,1,0:T(8,128)(2,1)S(1)}, bf16[1,2048,512]{2,1,0:T(8,128)(2,1)S(1)}, f32[264,256]{1,0:T(8,128)S(1)}, f32[264,256]{1,0:T(8,128)S(1)}) custom-call(s32[1]{0:T(128)} %bitcast.core_ref, f32[256,256]{1,0:T(8,128)S(1)} %constant_dynamic-update-slice_fusion.a_ref.refs_0_, f32[8,256]{1,0:T(8,128)S(1)} %copy-done.1, ...), custom_call_target="tpu_custom_call" | custom-call | tf_op jit(solution)/shard_map/load/pallas_call | solution.py:89
  40.5 1.5 %sample_gram.2.refs_0_.refs_3_.refs_2_ = f32[256,256]{1,0:T(8,128)S(1)} custom-call(s32[1]{0:T(128)} %bitcast.core_ref, f32[128,256]{1,0:T(8,128)S(1)} %copy-done.2, f32[128,256]{1,0:T(8,128)} %collective-permute-done.1.refs_1_, f32[264,256]{1,0:T(8,128)S(1)} %get-tuple-element.68.refs_2_.refs_0_.refs_3_, ...), custom_call_target="tpu_custom_call" | custom-call | tf_op jit(solution)/shard_map/sample_gram/pallas_call | solution.py:89
  42.0 1.0 collective-permute-start.6
  43.2 0.9 collective-permute-done.6.refs_1_.refs_3_
  44.2 1.6 %mass_base.2 = (f32[2048,256]{1,0:T(8,128)S(1)}, f32[8,256]{1,0:T(8,128)S(1)}) custom-call(s32[1]{0:T(128)} %bitcast.core_ref, f32[256,256]{1,0:T(8,128)S(1)} %sample_gram.2.refs_0_.refs_3_.refs_2_, f32[256,256]{1,0:T(8,128)S(1)} %collective-permute-done.6.refs_1_.refs_3_, f32[8,256]{1,0:T(8,128)S(1)} %copy-done.1, ...), custom_call_target="tpu_custom_call" | custom-call | tf_op jit(solution)/shard_map/mass_base/pallas_call | solution.py:89
  45.9 1.3 collective-permute-start.13
  47.2 2.4 %collective-permute-start.9 = (f32[128,256]{1,0:T(8,128)S(1)}, f32[128,256]{1,0:T(8,128)S(1)}, u32[]{:S(2)}, u32[]{:S(2)}) collective-permute-start(f32[128,256]{1,0:T(8,128)S(1)} %slice.45), channel_id=1, source_target_pairs={{0,4},{1,5},{2,6},{3,7},{4,0},{5,1},{6,2},{7,3},{8,12},{9,13},{10,... | collective-permute-start | bytes 393224 | tf_op jit(solution)/shard_map/ppermute | solution.py:531
  49.8 2.1 %mass_products.5.refs_8_.refs_9_.refs_10_.refs_6_ = f32[512,256]{1,0:T(8,128)S(1)} custom-call(s32[1]{0:T(128)} %bitcast.core_ref, bf16[512,2048]{1,0:T(8,128)(2,1)S(1)} %get-tuple-element.53.refs_5_.refs_0_, bf16[1,2048,512]{2,1,0:T(8,128)(2,1)S(1)} %get-tuple-element.69.refs_9_.refs_11_.refs_10_.refs_1_.refs_17_.refs_3_, ...), custom_call_target="tpu_custom_call" | custom-call | tf_op jit(solution)/shard_map/mass_products/pallas_call | solution.py:89
  52.0 2.2 %drive_products.4 = (f32[512,256]{1,0:T(8,128)S(1)}, f32[2048,256]{1,0:T(8,128)S(1)}, f32[256,256]{1,0:T(8,128)S(1)}) custom-call(s32[1]{0:T(128)} %bitcast.core_ref, f32[256,256]{1,0:T(8,128)S(1)} %constant_dynamic-update-slice_fusion.a_ref.refs_0_, f32[8,256]{1,0:T(8,128)S(1)} %copy-done.1, f32[8,256]{1,0:T(8,128)S(1)} %get-tuple-element.73.refs_2_, ...), custom_call_target="tpu_custom_call" | custom-call | tf_op jit(solution)/shard_map/drive_products/pallas_call | solution.py:89
  54.2 1.4 %collective-permute-start.14 = (f32[136,256]{1,0:T(8,128)S(1)}, f32[136,256]{1,0:T(8,128)S(1)}, u32[]{:S(2)}, u32[]{:S(2)}) collective-permute-start(f32[136,256]{1,0:T(8,128)S(1)} %add.54.refs_0_), channel_id=1, source_target_pairs={{0,2},{1,3},{2,0},{3,1},{4,6},{5,7},{6,4},{7,5},{8,10},{9,11},{10,... | collective-permute-start | bytes 417800 | tf_op jit(solution)/shard_map/ppermute | solution.py:531
  55.9 1.2 collective-permute-start.21
  57.1 2.3 %drive_products.5 = (f32[512,256]{1,0:T(8,128)S(1)}, f32[2048,256]{1,0:T(8,128)S(1)}, f32[256,256]{1,0:T(8,128)S(1)}) custom-call(s32[1]{0:T(128)} %bitcast.core_ref, f32[256,256]{1,0:T(8,128)S(1)} %constant_dynamic-update-slice_fusion.a_ref.refs_0_, f32[8,256]{1,0:T(8,128)S(1)} %copy-done.1, f32[8,256]{1,0:T(8,128)S(1)} %get-tuple-element.73.refs_2_, ...), custom_call_target="tpu_custom_call" | custom-call | tf_op jit(solution)/shard_map/drive_products/pallas_call | solution.py:89
  59.4 1.3 %collective-permute-start.16 = (f32[136,256]{1,0:T(8,128)S(1)}, f32[136,256]{1,0:T(8,128)S(1)}, u32[]{:S(2)}, u32[]{:S(2)}) collective-permute-start(f32[136,256]{1,0:T(8,128)S(1)} %add.55.refs_0_), channel_id=1, source_target_pairs={{0,4},{1,5},{2,6},{3,7},{4,0},{5,1},{6,2},{7,3},{8,12},{9,13},{10,... | collective-permute-start | bytes 417800 | tf_op jit(solution)/shard_map/ppermute | solution.py:531
  60.8 2.3 %collective-permute-start.11 = (f32[128,256]{1,0:T(8,128)S(1)}, f32[128,256]{1,0:T(8,128)S(1)}, u32[]{:S(2)}, u32[]{:S(2)}) collective-permute-start(f32[128,256]{1,0:T(8,128)S(1)} %add.42), channel_id=1, source_target_pairs={{0,2},{1,3},{2,0},{3,1},{4,6},{5,7},{6,4},{7,5},{8,10},{9,11},{10,... | collective-permute-start | bytes 393224 | tf_op jit(solution)/shard_map/ppermute | solution.py:531
  63.1 3.1 %collective-permute-done.11 = f32[128,256]{1,0:T(8,128)S(1)} collective-permute-done((f32[128,256]{1,0:T(8,128)S(1)}, f32[128,256]{1,0:T(8,128)S(1)}, u32[]{:S(2)}, u32[]{:S(2)}) %collective-permute-start.11) | collective-permute-done | bytes 131104 | tf_op jit(solution)/shard_map/ppermute | solution.py:531
  66.2 3.5 %collective-permute-start.12 = (f32[128,256]{1,0:T(8,128)S(1)}, f32[128,256]{1,0:T(8,128)S(1)}, u32[]{:S(2)}, u32[]{:S(2)}) collective-permute-start(f32[128,256]{1,0:T(8,128)S(1)} %add.43.refs_4_), channel_id=1, source_target_pairs={{0,8},{8,0},{16,24},{24,16},{1,9},{9,1},{17,25},{25,17},{2,10},{10... | collective-permute-start | bytes 393224 | tf_op jit(solution)/shard_map/ppermute | solution.py:531
  69.8 0.6 collective-permute-start.19
  70.4 3.1 %collective-permute-done.19.refs_9_ = f32[8,256]{1,0:T(8,128)S(1)} collective-permute-done((f32[8,256]{1,0:T(8,128)S(1)}, f32[8,256]{1,0:T(8,128)S(1)}, u32[]{:S(2)}, u32[]{:S(2)}) %collective-permute-start.19) | collective-permute-done | bytes 8224 | tf_op jit(solution)/shard_map/ppermute | solution.py:531
  73.5 1.3 small_step.2
  74.8 2.1 %mass_products.6.refs_3_.near_ref = f32[512,256]{1,0:T(8,128)S(1)} custom-call(s32[1]{0:T(128)} %bitcast.core_ref, bf16[512,2048]{1,0:T(8,128)(2,1)S(1)} %get-tuple-element.80.refs_0_, bf16[1,2048,512]{2,1,0:T(8,128)(2,1)S(1)} %get-tuple-element.56.refs_9_.refs_3_.refs_5_.refs_4_.refs_11_.refs_1_, ...), custom_call_target="tpu_custom_call" | custom-call | tf_op jit(solution)/shard_map/mass_products/pallas_call | solution.py:89
  77.3 2.1 %mass_products.7.refs_3_.near_ref = f32[512,256]{1,0:T(8,128)S(1)} custom-call(s32[1]{0:T(128)} %bitcast.core_ref, bf16[512,2048]{1,0:T(8,128)(2,1)S(1)} %get-tuple-element.80.refs_0_, bf16[1,2048,512]{2,1,0:T(8,128)(2,1)S(1)} %get-tuple-element.61.refs_11_.refs_5_.refs_7_.refs_6_.refs_13_.refs_3_.refs_1_, ...), custom_call_target="tpu_custom_call" | custom-call | tf_op jit(solution)/shard_map/mass_products/pallas_call | solution.py:89
  79.5 2.1 %mass_products.8.refs_3_.near_ref = f32[512,256]{1,0:T(8,128)S(1)} custom-call(s32[1]{0:T(128)} %bitcast.core_ref, bf16[512,2048]{1,0:T(8,128)(2,1)S(1)} %get-tuple-element.80.refs_0_, bf16[1,2048,512]{2,1,0:T(8,128)(2,1)S(1)} %get-tuple-element.66.refs_13_.refs_7_.refs_9_.refs_8_.refs_15_.refs_1_.refs_3_, ...), custom_call_target="tpu_custom_call" | custom-call | tf_op jit(solution)/shard_map/mass_products/pallas_call | solution.py:89
  81.6 2.4 %mass_products.9.refs_10_.near_ref = f32[512,256]{1,0:T(8,128)S(1)} custom-call(s32[1]{0:T(128)} %bitcast.core_ref, bf16[512,2048]{1,0:T(8,128)(2,1)S(1)} %get-tuple-element.80.refs_0_, bf16[1,2048,512]{2,1,0:T(8,128)(2,1)S(1)} %get-tuple-element.69.refs_9_.refs_11_.refs_10_.refs_1_.refs_17_.refs_3_, ...), custom_call_target="tpu_custom_call" | custom-call | tf_op jit(solution)/shard_map/mass_products/pallas_call | solution.py:89
  84.0 2.3 %drive_products.6 = (f32[512,256]{1,0:T(8,128)S(1)}, f32[2048,256]{1,0:T(8,128)S(1)}, f32[256,256]{1,0:T(8,128)S(1)}) custom-call(s32[1]{0:T(128)} %bitcast.core_ref, f32[256,256]{1,0:T(8,128)S(1)} %get-tuple-element.78.refs_3_.refs_0_.a_ref, f32[8,256]{1,0:T(8,128)S(1)} %get-tuple-element.79.refs_1_.b_ref, f32[8,256]{1,0:T(8,128)S(1)} %get-tuple-element.73.refs_2_, ...), custom_call_target="tpu_custom_call" | custom-call | tf_op jit(solution)/shard_map/drive_products/pallas_call | solution.py:89
  86.3 2.8 %drive_products.7 = (f32[512,256]{1,0:T(8,128)S(1)}, f32[264,256]{1,0:T(8,128)S(1)}, f32[264,256]{1,0:T(8,128)S(1)}) custom-call(s32[1]{0:T(128)} %bitcast.core_ref, f32[256,256]{1,0:T(8,128)S(1)} %get-tuple-element.78.refs_3_.refs_0_.a_ref, f32[8,256]{1,0:T(8,128)S(1)} %get-tuple-element.79.refs_1_.b_ref, f32[8,256]{1,0:T(8,128)S(1)} %get-tuple-element.73.refs_2_, ...), custom_call_target="tpu_custom_call" | custom-call | tf_op jit(solution)/shard_map/drive_products/pallas_call | solution.py:89
  89.1 2.2 %collective-permute-start.22 = (f32[264,256]{1,0:T(8,128)S(1)}, f32[264,256]{1,0:T(8,128)S(1)}, u32[]{:S(2)}, u32[]{:S(2)}) collective-permute-start(f32[264,256]{1,0:T(8,128)S(1)} %get-tuple-element.86), channel_id=1, source_target_pairs={{0,8},{8,0},{16,24},{24,16},{1,9},{9,1},{17,25},{25,17},{2,10},{10... | collective-permute-start | bytes 811016 | tf_op jit(solution)/shard_map/ppermute | solution.py:531
  91.3 1.2 collective-permute-done.22.far_ref
  92.8 1.2 collective-permute-start.34
  94.0 0.4 collective-permute-start.25
  94.4 3.0 %collective-permute-done.23 = f32[136,256]{1,0:T(8,128)S(1)} collective-permute-done((f32[136,256]{1,0:T(8,128)S(1)}, f32[136,256]{1,0:T(8,128)S(1)}, u32[]{:S(2)}, u32[]{:S(2)}) %collective-permute-start.23) | collective-permute-done | bytes 139296 | tf_op jit(solution)/shard_map/ppermute | solution.py:531
  97.5 0.4 sample_gram.3.gram_ref.gram_a_ref
  97.9 1.3 collective-permute-start.24
  99.2 1.2 collective-permute-start.37
  100.4 1.3 collective-permute-start.29
  101.7 0.4 collective-permute-done.25
  102.2 1.3 collective-permute-start.26
  103.5 1.7 %mass_base.3 = (f32[2048,256]{1,0:T(8,128)S(1)}, f32[8,256]{1,0:T(8,128)S(1)}) custom-call(s32[1]{0:T(128)} %bitcast.core_ref, f32[256,256]{1,0:T(8,128)S(1)} %sample_gram.3.gram_ref.gram_a_ref, f32[256,256]{1,0:T(8,128)S(1)} %collective-permute-done.24.other_ref.gram_a_other_ref, f32[8,256]{1,0:T(8,128)S(1)} %get-tuple-element.79.refs_1_.b_ref, ...), custom_call_target="tpu_custom_call" | custom-call | tf_op jit(solution)/shard_map/mass_base/pallas_call | solution.py:89
  105.4 2.0 %collective-permute-start.36 = (f32[512,256]{1,0:T(8,128)S(1)}, f32[512,256]{1,0:T(8,128)S(1)}, u32[]{:S(2)}, u32[]{:S(2)}) collective-permute-start(f32[512,256]{1,0:T(8,128)S(1)} %last_step.5.mine_ref.held_ref), channel_id=1, source_target_pairs={{0,8},{8,0},{16,24},{24,16},{1,9},{9,1},{17,25},{25,17},{2,10},{10... | collective-permute-start | bytes 1572872 | tf_op jit(solution)/shard_map/ppermute | solution.py:531
  107.7 0.8 collective-permute-start.35
  108.5 1.2 collective-permute-start.33
  109.8 1.4 %collective-permute-start.27 = (f32[128,256]{1,0:T(8,128)S(1)}, f32[128,256]{1,0:T(8,128)S(1)}, u32[]{:S(2)}, u32[]{:S(2)}) collective-permute-start(f32[128,256]{1,0:T(8,128)S(1)} %add.46.refs_1_), channel_id=1, source_target_pairs={{0,2},{1,3},{2,0},{3,1},{4,6},{5,7},{6,4},{7,5},{8,10},{9,11},{10,... | collective-permute-start | bytes 393224 | tf_op jit(solution)/shard_map/ppermute | solution.py:531
  111.2 3.4 %collective-permute-done.27 = f32[128,256]{1,0:T(8,128)S(1)} collective-permute-done((f32[128,256]{1,0:T(8,128)S(1)}, f32[128,256]{1,0:T(8,128)S(1)}, u32[]{:S(2)}, u32[]{:S(2)}) %collective-permute-start.27) | collective-permute-done | bytes 131104 | tf_op jit(solution)/shard_map/ppermute | solution.py:531
  114.6 1.3 collective-permute-start.30
  115.9 7.1 %collective-permute-done.30 = f32[136,256]{1,0:T(8,128)S(1)} collective-permute-done((f32[136,256]{1,0:T(8,128)S(1)}, f32[136,256]{1,0:T(8,128)S(1)}, u32[]{:S(2)}, u32[]{:S(2)}) %collective-permute-start.30) | collective-permute-done | bytes 139296 | tf_op jit(solution)/shard_map/ppermute | solution.py:531
  123.0 1.6 %collective-permute-start.28 = (f32[128,256]{1,0:T(8,128)S(1)}, f32[128,256]{1,0:T(8,128)S(1)}, u32[]{:S(2)}, u32[]{:S(2)}) collective-permute-start(f32[128,256]{1,0:T(8,128)S(1)} %add.47.refs_0_.refs_1_.gram_c_ref), channel_id=1, source_target_pairs={{0,8},{8,0},{16,24},{24,16},{1,9},{9,1},{17,25},{25,17},{2,10},{10... | collective-permute-start | bytes 393224 | tf_op jit(solution)/shard_map/ppermute | solution.py:531
  124.7 0.3 collective-permute-start.32
  125.0 1.0 join.4
  126.3 0.8 collective-permute-start.39
  127.0 1.0 join.5
  128.5 1.6 %collective-permute-start.38 = (f32[512,256]{1,0:T(8,128)S(1)}, f32[512,256]{1,0:T(8,128)S(1)}, u32[]{:S(2)}, u32[]{:S(2)}) collective-permute-start(f32[512,256]{1,0:T(8,128)S(1)} %last_step.7.after_ref.mine_ref), channel_id=1, source_target_pairs={{0,8},{8,0},{16,24},{24,16},{1,9},{9,1},{17,25},{25,17},{2,10},{10... | collective-permute-start | bytes 1572872 | tf_op jit(solution)/shard_map/ppermute | solution.py:531
  130.1 1.3 %small_step.3 = (f32[128,256]{1,0:T(8,128)}, f32[8,256]{1,0:T(8,128)}) custom-call(s32[1]{0:T(128)} %bitcast.core_ref, f32[256,256]{1,0:T(8,128)S(1)} %get-tuple-element.78.refs_3_.refs_0_.a_ref, f32[8,256]{1,0:T(8,128)S(1)} %get-tuple-element.79.refs_1_.b_ref, f32[256,256]{1,0:T(8,128)S(1)} %sample_gram.3.gram_ref.gram_a_ref, ...), custom_call_target="tpu_custom_call" | custom-call | tf_op jit(solution)/shard_map/small_step/pallas_call | solution.py:89
  131.4 1.0 join.6
  132.5 1.0 join.7
  (86 shorter events, 3.7 us)
Async XLA Ops:
  0.6 1.8 %copy-start.2 = (f32[128,256]{1,0:T(8,128)S(1)}, f32[128,256]{1,0:T(8,128)}, u32[]{:S(2)}) copy-start(f32[128,256]{1,0:T(8,128)} %refs_0_.1) | copy-start | bytes 393220
  2.3 5.8 %collective-permute-start.2 = (f32[1024,512]{1,0:T(8,128)S(1)}, f32[1024,512]{1,0:T(8,128)S(1)}, u32[]{:S(2)}, u32[]{:S(2)}) collective-permute-start(f32[1024,512]{1,0:T(8,128)S(1)} %give.3.after_ref), channel_id=1, source_target_pairs={{0,8},{8,0},{16,24},{24,16},{1,9},{9,1},{17,25},{25,17},{2,10},{10... | collective-permute-start | bytes 6291464 | tf_op jit(solution)/shard_map/ppermute | solution.py:531
  2.4 5.7 %collective-permute-start = (f32[128,256]{1,0:T(8,128)S(1)}, f32[128,256]{1,0:T(8,128)S(1)}, u32[]{:S(2)}, u32[]{:S(2)}) collective-permute-start(f32[128,256]{1,0:T(8,128)S(1)} %copy-done.2), channel_id=1, source_target_pairs={{0,8},{8,0},{16,24},{24,16},{1,9},{9,1},{17,25},{25,17},{2,10},{10... | collective-permute-start | bytes 393224 | tf_op jit(solution)/shard_map/ppermute | solution.py:531
  5.8 2.3 %copy-start.1 = (f32[8,256]{1,0:T(8,128)S(1)}, f32[8,256]{1,0:T(8,128)}, u32[]{:S(2)}) copy-start(f32[8,256]{1,0:T(8,128)} %refs_1_.11) | copy-start | bytes 24580
  5.8 15.6 %collective-permute-start.5 = (f32[1024,512]{1,0:T(8,128)}, f32[1024,512]{1,0:T(8,128)}, u32[]{:S(2)}, u32[]{:S(2)}) collective-permute-start(f32[1024,512]{1,0:T(8,128)} %give.4.after_ref), channel_id=1, source_target_pairs={{0,8},{8,0},{16,24},{24,16},{1,9},{9,1},{17,25},{25,17},{2,10},{10... | collective-permute-start | bytes 6291464 | tf_op jit(solution)/shard_map/ppermute | solution.py:531
  7.6 21.5 %collective-permute-start.4 = (f32[1024,512]{1,0:T(8,128)S(1)}, f32[1024,512]{1,0:T(8,128)}, u32[]{:S(2)}, u32[]{:S(2)}) collective-permute-start(f32[1024,512]{1,0:T(8,128)S(1)} %give.5.after_ref), channel_id=1, source_target_pairs={{0,8},{8,0},{16,24},{24,16},{1,9},{9,1},{17,25},{25,17},{2,10},{10... | collective-permute-start | bytes 6291464 | tf_op jit(solution)/shard_map/ppermute | solution.py:531
  8.1 5.8 %copy-start = (f32[1024,512]{1,0:T(8,128)}, f32[1024,512]{1,0:T(8,128)S(1)}, u32[]{:S(2)}) copy-start(f32[1024,512]{1,0:T(8,128)S(1)} %collective-permute-done.2.other_ref) | copy-start | bytes 6291460
  13.9 21.4 %collective-permute-start.3 = (f32[1024,512]{1,0:T(8,128)}, f32[1024,512]{1,0:T(8,128)}, u32[]{:S(2)}, u32[]{:S(2)}) collective-permute-start(f32[1024,512]{1,0:T(8,128)} %get-tuple-element.51), channel_id=1, source_target_pairs={{0,8},{8,0},{16,24},{24,16},{1,9},{9,1},{17,25},{25,17},{2,10},{10... | collective-permute-start | bytes 6291464 | tf_op jit(solution)/shard_map/ppermute | solution.py:531
  14.1 31.8 %collective-permute-start.8 = (f32[512,256]{1,0:T(8,128)S(1)}, f32[512,256]{1,0:T(8,128)S(1)}, u32[]{:S(2)}, u32[]{:S(2)}) collective-permute-start(f32[512,256]{1,0:T(8,128)S(1)} %get-tuple-element.52.krt_in_ref.total_in_ref.gram_in_ref.after_ref.refs_8_.refs_6_), channel_id=1, source_target_pairs={{0,16},{8,24},{16,0},{24,8},{1,17},{9,25},{17,1},{25,9},{2,18},{10... | collective-permute-start | bytes 1572872 | tf_op jit(solution)/shard_map/ppermute | solution.py:531
  16.7 23.8 %collective-permute-start.1 = (f32[128,256]{1,0:T(8,128)S(1)}, f32[128,256]{1,0:T(8,128)}, u32[]{:S(2)}, u32[]{:S(2)}) collective-permute-start(f32[128,256]{1,0:T(8,128)S(1)} %copy-done.2), channel_id=1, source_target_pairs={{0,16},{8,24},{16,0},{24,8},{1,17},{9,25},{17,1},{25,9},{2,18},{10... | collective-permute-start | bytes 393224 | tf_op jit(solution)/shard_map/ppermute | solution.py:531
  27.5 29.6 %collective-permute-start.15 = (f32[512,256]{1,0:T(8,128)S(1)}, f32[512,256]{1,0:T(8,128)S(1)}, u32[]{:S(2)}, u32[]{:S(2)}) collective-permute-start(f32[512,256]{1,0:T(8,128)S(1)} %get-tuple-element.60.refs_8_.refs_6_), channel_id=1, source_target_pairs={{0,16},{8,24},{16,0},{24,8},{1,17},{9,25},{17,1},{25,9},{2,18},{10... | collective-permute-start | bytes 1572872 | tf_op jit(solution)/shard_map/ppermute | solution.py:531
  40.5 2.6 %copy-start.4 = (f32[4096,256]{1,0:T(8,128)S(1)}, f32[4096,256]{1,0:T(8,128)}, u32[]{:S(2)}) copy-start(f32[4096,256]{1,0:T(8,128)} %refs_4_.5) | copy-start | bytes 12582916
  42.0 2.1 %collective-permute-start.6 = (f32[256,256]{1,0:T(8,128)S(1)}, f32[256,256]{1,0:T(8,128)S(1)}, u32[]{:S(2)}, u32[]{:S(2)}) collective-permute-start(f32[256,256]{1,0:T(8,128)S(1)} %sample_gram.2.refs_0_.refs_3_.refs_2_), channel_id=1, source_target_pairs={{0,8},{8,0},{16,24},{24,16},{1,9},{9,1},{17,25},{25,17},{2,10},{10... | collective-permute-start | bytes 786440 | tf_op jit(solution)/shard_map/ppermute | solution.py:531
  43.0 2.8 %collective-permute-start.7 = (f32[264,256]{1,0:T(8,128)S(1)}, f32[264,256]{1,0:T(8,128)S(1)}, u32[]{:S(2)}, u32[]{:S(2)}) collective-permute-start(f32[264,256]{1,0:T(8,128)S(1)} %get-tuple-element.71), channel_id=1, source_target_pairs={{0,8},{8,0},{16,24},{24,16},{1,9},{9,1},{17,25},{25,17},{2,10},{10... | collective-permute-start | bytes 811016 | tf_op jit(solution)/shard_map/ppermute | solution.py:531
  45.9 8.3 %collective-permute-start.13 = (f32[136,256]{1,0:T(8,128)S(1)}, f32[136,256]{1,0:T(8,128)S(1)}, u32[]{:S(2)}, u32[]{:S(2)}) collective-permute-start(f32[136,256]{1,0:T(8,128)S(1)} %slice.46.refs_0_), channel_id=1, source_target_pairs={{0,1},{1,0},{2,3},{3,2},{4,5},{5,4},{6,7},{7,6},{8,9},{9,8},{10,11... | collective-permute-start | bytes 417800 | tf_op jit(solution)/shard_map/ppermute | solution.py:531
  47.2 8.4 %collective-permute-start.9 = (f32[128,256]{1,0:T(8,128)S(1)}, f32[128,256]{1,0:T(8,128)S(1)}, u32[]{:S(2)}, u32[]{:S(2)}) collective-permute-start(f32[128,256]{1,0:T(8,128)S(1)} %slice.45), channel_id=1, source_target_pairs={{0,4},{1,5},{2,6},{3,7},{4,0},{5,1},{6,2},{7,3},{8,12},{9,13},{10,... | collective-permute-start | bytes 393224 | tf_op jit(solution)/shard_map/ppermute | solution.py:531
  49.6 20.1 %collective-permute-start.17 = (f32[512,256]{1,0:T(8,128)S(1)}, f32[512,256]{1,0:T(8,128)S(1)}, u32[]{:S(2)}, u32[]{:S(2)}) collective-permute-start(f32[512,256]{1,0:T(8,128)S(1)} %get-tuple-element.65.refs_8_.refs_3_.refs_6_), channel_id=1, source_target_pairs={{0,16},{8,24},{16,0},{24,8},{1,17},{9,25},{17,1},{25,9},{2,18},{10... | collective-permute-start | bytes 1572872 | tf_op jit(solution)/shard_map/ppermute | solution.py:531
  54.2 5.2 %collective-permute-start.14 = (f32[136,256]{1,0:T(8,128)S(1)}, f32[136,256]{1,0:T(8,128)S(1)}, u32[]{:S(2)}, u32[]{:S(2)}) collective-permute-start(f32[136,256]{1,0:T(8,128)S(1)} %add.54.refs_0_), channel_id=1, source_target_pairs={{0,2},{1,3},{2,0},{3,1},{4,6},{5,7},{6,4},{7,5},{8,10},{9,11},{10,... | collective-permute-start | bytes 417800 | tf_op jit(solution)/shard_map/ppermute | solution.py:531
  55.6 5.2 %collective-permute-start.10 = (f32[128,256]{1,0:T(8,128)S(1)}, f32[128,256]{1,0:T(8,128)S(1)}, u32[]{:S(2)}, u32[]{:S(2)}) collective-permute-start(f32[128,256]{1,0:T(8,128)S(1)} %slice_add_fusion.1), channel_id=1, source_target_pairs={{0,1},{1,0},{2,3},{3,2},{4,5},{5,4},{6,7},{7,6},{8,9},{9,8},{10,11... | collective-permute-start | bytes 393224 | tf_op jit(solution)/shard_map/ppermute | solution.py:531
  55.9 30.4 %collective-permute-start.21 = (f32[512,256]{1,0:T(8,128)S(1)}, f32[512,256]{1,0:T(8,128)S(1)}, u32[]{:S(2)}, u32[]{:S(2)}) collective-permute-start(f32[512,256]{1,0:T(8,128)S(1)} %mass_products.5.refs_8_.refs_9_.refs_10_.refs_6_), channel_id=1, source_target_pairs={{0,16},{8,24},{16,0},{24,8},{1,17},{9,25},{17,1},{25,9},{2,18},{10... | collective-permute-start | bytes 1572872 | tf_op jit(solution)/shard_map/ppermute | solution.py:531
  59.4 10.2 %collective-permute-start.16 = (f32[136,256]{1,0:T(8,128)S(1)}, f32[136,256]{1,0:T(8,128)S(1)}, u32[]{:S(2)}, u32[]{:S(2)}) collective-permute-start(f32[136,256]{1,0:T(8,128)S(1)} %add.55.refs_0_), channel_id=1, source_target_pairs={{0,4},{1,5},{2,6},{3,7},{4,0},{5,1},{6,2},{7,3},{8,12},{9,13},{10,... | collective-permute-start | bytes 417800 | tf_op jit(solution)/shard_map/ppermute | solution.py:531
  60.8 5.3 %collective-permute-start.11 = (f32[128,256]{1,0:T(8,128)S(1)}, f32[128,256]{1,0:T(8,128)S(1)}, u32[]{:S(2)}, u32[]{:S(2)}) collective-permute-start(f32[128,256]{1,0:T(8,128)S(1)} %add.42), channel_id=1, source_target_pairs={{0,2},{1,3},{2,0},{3,1},{4,6},{5,7},{6,4},{7,5},{8,10},{9,11},{10,... | collective-permute-start | bytes 393224 | tf_op jit(solution)/shard_map/ppermute | solution.py:531
  66.2 7.3 %collective-permute-start.12 = (f32[128,256]{1,0:T(8,128)S(1)}, f32[128,256]{1,0:T(8,128)S(1)}, u32[]{:S(2)}, u32[]{:S(2)}) collective-permute-start(f32[128,256]{1,0:T(8,128)S(1)} %add.43.refs_4_), channel_id=1, source_target_pairs={{0,8},{8,0},{16,24},{24,16},{1,9},{9,1},{17,25},{25,17},{2,10},{10... | collective-permute-start | bytes 393224 | tf_op jit(solution)/shard_map/ppermute | solution.py:531
  69.7 3.8 %collective-permute-start.18 = (f32[128,256]{1,0:T(8,128)S(1)}, f32[128,256]{1,0:T(8,128)S(1)}, u32[]{:S(2)}, u32[]{:S(2)}) collective-permute-start(f32[128,256]{1,0:T(8,128)S(1)} %slice.47.refs_6_), channel_id=1, source_target_pairs={{0,8},{8,0},{16,24},{24,16},{1,9},{9,1},{17,25},{25,17},{2,10},{10... | collective-permute-start | bytes 393224 | tf_op jit(solution)/shard_map/ppermute | solution.py:531
  69.8 3.7 %collective-permute-start.19 = (f32[8,256]{1,0:T(8,128)S(1)}, f32[8,256]{1,0:T(8,128)S(1)}, u32[]{:S(2)}, u32[]{:S(2)}) collective-permute-start(f32[8,256]{1,0:T(8,128)S(1)} %slice.48.refs_8_), channel_id=1, source_target_pairs={{0,16},{8,24},{16,0},{24,8},{1,17},{9,25},{17,1},{25,9},{2,18},{10... | collective-permute-start | bytes 24584 | tf_op jit(solution)/shard_map/ppermute | solution.py:531
  77.0 20.4 %collective-permute-start.20 = (f32[640,256]{1,0:T(8,128)S(1)}, f32[640,256]{1,0:T(8,128)S(1)}, u32[]{:S(2)}, u32[]{:S(2)}) collective-permute-start(f32[640,256]{1,0:T(8,128)S(1)} %pad_maximum_fusion), channel_id=1, source_target_pairs={{0,16},{8,24},{16,0},{24,8},{1,17},{9,25},{17,1},{25,9},{2,18},{10... | collective-permute-start | bytes 1966088 | tf_op jit(solution)/shard_map/ppermute | solution.py:531
  89.1 3.4 %collective-permute-start.22 = (f32[264,256]{1,0:T(8,128)S(1)}, f32[264,256]{1,0:T(8,128)S(1)}, u32[]{:S(2)}, u32[]{:S(2)}) collective-permute-start(f32[264,256]{1,0:T(8,128)S(1)} %get-tuple-element.86), channel_id=1, source_target_pairs={{0,8},{8,0},{16,24},{24,16},{1,9},{9,1},{17,25},{25,17},{2,10},{10... | collective-permute-start | bytes 811016 | tf_op jit(solution)/shard_map/ppermute | solution.py:531
  92.5 5.0 %collective-permute-start.23 = (f32[136,256]{1,0:T(8,128)S(1)}, f32[136,256]{1,0:T(8,128)S(1)}, u32[]{:S(2)}, u32[]{:S(2)}) collective-permute-start(f32[136,256]{1,0:T(8,128)S(1)} %slice.50), channel_id=1, source_target_pairs={{0,1},{1,0},{2,3},{3,2},{4,5},{5,4},{6,7},{7,6},{8,9},{9,8},{10,11... | collective-permute-start | bytes 417800 | tf_op jit(solution)/shard_map/ppermute | solution.py:531
  92.8 14.7 %collective-permute-start.34 = (f32[512,256]{1,0:T(8,128)S(1)}, f32[512,256]{1,0:T(8,128)S(1)}, u32[]{:S(2)}, u32[]{:S(2)}) collective-permute-start(f32[512,256]{1,0:T(8,128)S(1)} %mass_products.7.refs_3_.near_ref), channel_id=1, source_target_pairs={{0,16},{8,24},{16,0},{24,8},{1,17},{9,25},{17,1},{25,9},{2,18},{10... | collective-permute-start | bytes 1572872 | tf_op jit(solution)/shard_map/ppermute | solution.py:531
  94.0 8.1 %collective-permute-start.25 = (f32[128,256]{1,0:T(8,128)S(1)}, f32[128,256]{1,0:T(8,128)S(1)}, u32[]{:S(2)}, u32[]{:S(2)}) collective-permute-start(f32[128,256]{1,0:T(8,128)S(1)} %slice.51), channel_id=1, source_target_pairs={{0,4},{1,5},{2,6},{3,7},{4,0},{5,1},{6,2},{7,3},{8,12},{9,13},{10,... | collective-permute-start | bytes 393224 | tf_op jit(solution)/shard_map/ppermute | solution.py:531
  97.9 5.6 %collective-permute-start.24 = (f32[256,256]{1,0:T(8,128)S(1)}, f32[256,256]{1,0:T(8,128)S(1)}, u32[]{:S(2)}, u32[]{:S(2)}) collective-permute-start(f32[256,256]{1,0:T(8,128)S(1)} %sample_gram.3.gram_ref.gram_a_ref), channel_id=1, source_target_pairs={{0,8},{8,0},{16,24},{24,16},{1,9},{9,1},{17,25},{25,17},{2,10},{10... | collective-permute-start | bytes 786440 | tf_op jit(solution)/shard_map/ppermute | solution.py:531
  99.2 25.4 %collective-permute-start.37 = (f32[512,256]{1,0:T(8,128)S(1)}, f32[512,256]{1,0:T(8,128)S(1)}, u32[]{:S(2)}, u32[]{:S(2)}) collective-permute-start(f32[512,256]{1,0:T(8,128)S(1)} %mass_products.8.refs_3_.near_ref), channel_id=1, source_target_pairs={{0,16},{8,24},{16,0},{24,8},{1,17},{9,25},{17,1},{25,9},{2,18},{10... | collective-permute-start | bytes 1572872 | tf_op jit(solution)/shard_map/ppermute | solution.py:531
  100.4 7.0 %collective-permute-start.29 = (f32[136,256]{1,0:T(8,128)S(1)}, f32[136,256]{1,0:T(8,128)S(1)}, u32[]{:S(2)}, u32[]{:S(2)}) collective-permute-start(f32[136,256]{1,0:T(8,128)S(1)} %slice_add_fusion.2.after_ref), channel_id=1, source_target_pairs={{0,2},{1,3},{2,0},{3,1},{4,6},{5,7},{6,4},{7,5},{8,10},{9,11},{10,... | collective-permute-start | bytes 417800 | tf_op jit(solution)/shard_map/ppermute | solution.py:531
  102.2 7.6 %collective-permute-start.26 = (f32[128,256]{1,0:T(8,128)S(1)}, f32[128,256]{1,0:T(8,128)S(1)}, u32[]{:S(2)}, u32[]{:S(2)}) collective-permute-start(f32[128,256]{1,0:T(8,128)S(1)} %slice_add_fusion.refs_1_), channel_id=1, source_target_pairs={{0,1},{1,0},{2,3},{3,2},{4,5},{5,4},{6,7},{7,6},{8,9},{9,8},{10,11... | collective-permute-start | bytes 393224 | tf_op jit(solution)/shard_map/ppermute | solution.py:531
  105.4 19.3 %collective-permute-start.36 = (f32[512,256]{1,0:T(8,128)S(1)}, f32[512,256]{1,0:T(8,128)S(1)}, u32[]{:S(2)}, u32[]{:S(2)}) collective-permute-start(f32[512,256]{1,0:T(8,128)S(1)} %last_step.5.mine_ref.held_ref), channel_id=1, source_target_pairs={{0,8},{8,0},{16,24},{24,16},{1,9},{9,1},{17,25},{25,17},{2,10},{10... | collective-permute-start | bytes 1572872 | tf_op jit(solution)/shard_map/ppermute | solution.py:531
  107.7 18.6 %collective-permute-start.35 = (f32[512,256]{1,0:T(8,128)S(1)}, f32[512,256]{1,0:T(8,128)S(1)}, u32[]{:S(2)}, u32[]{:S(2)}) collective-permute-start(f32[512,256]{1,0:T(8,128)S(1)} %last_step.4.after_ref.mine_ref), channel_id=1, source_target_pairs={{0,8},{8,0},{16,24},{24,16},{1,9},{9,1},{17,25},{25,17},{2,10},{10... | collective-permute-start | bytes 1572872 | tf_op jit(solution)/shard_map/ppermute | solution.py:531
  108.5 19.5 %collective-permute-start.33 = (f32[512,256]{1,0:T(8,128)S(1)}, f32[512,256]{1,0:T(8,128)S(1)}, u32[]{:S(2)}, u32[]{:S(2)}) collective-permute-start(f32[512,256]{1,0:T(8,128)S(1)} %mass_products.9.refs_10_.near_ref), channel_id=1, source_target_pairs={{0,16},{8,24},{16,0},{24,8},{1,17},{9,25},{17,1},{25,9},{2,18},{10... | collective-permute-start | bytes 1572872 | tf_op jit(solution)/shard_map/ppermute | solution.py:531
  109.8 4.8 %collective-permute-start.27 = (f32[128,256]{1,0:T(8,128)S(1)}, f32[128,256]{1,0:T(8,128)S(1)}, u32[]{:S(2)}, u32[]{:S(2)}) collective-permute-start(f32[128,256]{1,0:T(8,128)S(1)} %add.46.refs_1_), channel_id=1, source_target_pairs={{0,2},{1,3},{2,0},{3,1},{4,6},{5,7},{6,4},{7,5},{8,10},{9,11},{10,... | collective-permute-start | bytes 393224 | tf_op jit(solution)/shard_map/ppermute | solution.py:531
  114.6 8.4 %collective-permute-start.30 = (f32[136,256]{1,0:T(8,128)S(1)}, f32[136,256]{1,0:T(8,128)S(1)}, u32[]{:S(2)}, u32[]{:S(2)}) collective-permute-start(f32[136,256]{1,0:T(8,128)S(1)} %add.48.refs_0_), channel_id=1, source_target_pairs={{0,4},{1,5},{2,6},{3,7},{4,0},{5,1},{6,2},{7,3},{8,12},{9,13},{10,... | collective-permute-start | bytes 417800 | tf_op jit(solution)/shard_map/ppermute | solution.py:531
  123.0 5.2 %collective-permute-start.28 = (f32[128,256]{1,0:T(8,128)S(1)}, f32[128,256]{1,0:T(8,128)S(1)}, u32[]{:S(2)}, u32[]{:S(2)}) collective-permute-start(f32[128,256]{1,0:T(8,128)S(1)} %add.47.refs_0_.refs_1_.gram_c_ref), channel_id=1, source_target_pairs={{0,8},{8,0},{16,24},{24,16},{1,9},{9,1},{17,25},{25,17},{2,10},{10... | collective-permute-start | bytes 393224 | tf_op jit(solution)/shard_map/ppermute | solution.py:531
  124.6 3.6 %collective-permute-start.31 = (f32[128,256]{1,0:T(8,128)S(1)}, f32[128,256]{1,0:T(8,128)S(1)}, u32[]{:S(2)}, u32[]{:S(2)}) collective-permute-start(f32[128,256]{1,0:T(8,128)S(1)} %slice.52.refs_3_.drive_ref), channel_id=1, source_target_pairs={{0,8},{8,0},{16,24},{24,16},{1,9},{9,1},{17,25},{25,17},{2,10},{10... | collective-permute-start | bytes 393224 | tf_op jit(solution)/shard_map/ppermute | solution.py:531
  124.7 3.5 %collective-permute-start.32 = (f32[8,256]{1,0:T(8,128)S(1)}, f32[8,256]{1,0:T(8,128)S(1)}, u32[]{:S(2)}, u32[]{:S(2)}) collective-permute-start(f32[8,256]{1,0:T(8,128)S(1)} %slice.53.refs_5_.drive_b_ref), channel_id=1, source_target_pairs={{0,16},{8,24},{16,0},{24,8},{1,17},{9,25},{17,1},{25,9},{2,18},{10... | collective-permute-start | bytes 24584 | tf_op jit(solution)/shard_map/ppermute | solution.py:531
  126.3 5.1 %collective-permute-start.39 = (f32[512,256]{1,0:T(8,128)S(1)}, f32[512,256]{1,0:T(8,128)S(1)}, u32[]{:S(2)}, u32[]{:S(2)}) collective-permute-start(f32[512,256]{1,0:T(8,128)S(1)} %last_step.6.after_ref.mine_ref), channel_id=1, source_target_pairs={{0,8},{8,0},{16,24},{24,16},{1,9},{9,1},{17,25},{25,17},{2,10},{10... | collective-permute-start | bytes 1572872 | tf_op jit(solution)/shard_map/ppermute | solution.py:531
  128.5 4.0 %collective-permute-start.38 = (f32[512,256]{1,0:T(8,128)S(1)}, f32[512,256]{1,0:T(8,128)S(1)}, u32[]{:S(2)}, u32[]{:S(2)}) collective-permute-start(f32[512,256]{1,0:T(8,128)S(1)} %last_step.7.after_ref.mine_ref), channel_id=1, source_target_pairs={{0,8},{8,0},{16,24},{24,16},{1,9},{9,1},{17,25},{25,17},{2,10},{10... | collective-permute-start | bytes 1572872 | tf_op jit(solution)/shard_map/ppermute | solution.py:531
  131.4 1.0 copy-start.3
